TPU v7x, 128 devices: a whole 4x4x4 slice. The times are simulated.
128 devices in a mesh: seq: 64 (over z, x, y_lo, core), batch: 2 (over y_hi).
Axes of the slice: x: 4, y: 4 (y_hi: 2, y_lo: 2; y = y_hi * 2 + y_lo), z: 4, core: 2. Of those that a mesh axis runs over, the one named last changes fastest.
Arguments:
- tokens: bfloat16 [2, 8192, 768], P('batch', 'seq'), may hold values from -16 to 16
- seg_lengths: int32 [2, 16], P('batch'), may hold values from 256 to 512, as said below
- ln1_gain: bfloat16 [768], P('seq'), may hold values from 0.5 to 1.5
- ln1_bias: bfloat16 [768], P('seq'), may hold values from -3 to 3
- w_query: bfloat16 [768, 768], P('seq'), may hold values from -0.21875 to 0.21875
- q_bias: bfloat16 [768], P('seq'), may hold values from -3 to 3
- w_key: bfloat16 [768, 768], P('seq'), may hold values from -0.21875 to 0.21875
- w_value: bfloat16 [768, 768], P('seq'), may hold values from -0.21875 to 0.21875
- v_bias: bfloat16 [768], P('seq'), may hold values from -3 to 3
- w_out: bfloat16 [768, 768], P('seq'), may hold values from -0.875 to 0.875
- o_bias: bfloat16 [768], P('seq'), may hold values from -3 to 3
- ln2_gain: bfloat16 [768], P('seq'), may hold values from 0.5 to 1.5
- ln2_bias: bfloat16 [768], P('seq'), may hold values from -3 to 3
- w_up: bfloat16 [768, 3072], P('seq'), may hold values from -0.21875 to 0.21875
- up_bias: bfloat16 [3072], P('seq'), may hold values from -3 to 3
- w_down: bfloat16 [768, 3072], P('seq'), may hold values from -0.109375 to 0.109375
- down_bias: bfloat16 [768], P('seq'), may hold values from -3 to 3
- d_out: bfloat16 [2, 8192, 768], P('batch', 'seq'), may hold values from -6 to 6
Outputs:
- output: bfloat16 [2, 8192, 768], P('batch', 'seq')
- g_tokens: float32 [2, 8192, 768], P('batch', 'seq')
- g_ln1_gain: float32 [768], P('seq')
- g_ln1_bias: float32 [768], P('seq')
- g_w_query: float32 [768, 768], P('seq')
- g_q_bias: float32 [768], P('seq')
- g_w_key: float32 [768, 768], P('seq')
- g_w_value: float32 [768, 768], P('seq')
- g_v_bias: float32 [768], P('seq')
- g_w_out: float32 [768, 768], P('seq')
- g_o_bias: float32 [768], P('seq')
- g_ln2_gain: float32 [768], P('seq')
- g_ln2_bias: float32 [768], P('seq')
- g_w_up: float32 [768, 3072], P('seq')
- g_up_bias: float32 [3072], P('seq')
- g_w_down: float32 [768, 3072], P('seq')
- g_down_bias: float32 [768], P('seq')
Inputs may be any that keep to these rules, and one draw needn't show every extreme that they name: `seg_lengths`: in every item one segment slot holds exactly 512 real tokens and another exactly half of 512.
All inputs are finite; a program needn't handle non-finite values.
Results may differ from a plain program's by a relative error of at most 0.024.
Values may be sent and summed in bfloat16 or wider, within the bound.
A program may use at most 128 MiB of HBM per device.

v0:
```python
import jax
import jax.numpy as jnp
from jax import lax
from jax.sharding import PartitionSpec as P

HEAD = 64
SEG_DEVS = 4
SUMMARY = 50


EPSILON = 1e-05
MASKED = -1e30
HIGHEST = lax.Precision.HIGHEST


def shifted(block, axis, distance):
    devices = range(lax.axis_size(axis))
    route = [(i - distance, i) for i in devices if i - distance in devices]
    return lax.ppermute(block, axis, route)


def from_behind(x, axis, by):
    size = lax.axis_size(axis)
    return lax.ppermute(x, axis, [(i, (i + by) % size) for i in range(size)])


def norm_rows(values, scale_gain, scale_shift):
    center = values - jnp.mean(values, axis=-1, keepdims=True)
    spread = jnp.mean(center * center, axis=-1, keepdims=True)
    return center * lax.rsqrt(spread + EPSILON) * scale_gain + scale_shift


def contract_last(left_rows, right_rows):
    return lax.dot_general(
        left_rows, right_rows, (((1,), (1,)), ((), ())), preferred_element_type=jnp.float32
    )


def contract_first(left_rows, right_rows):
    return lax.dot_general(
        left_rows, right_rows, (((0,), (0,)), ((), ())), preferred_element_type=jnp.float32
    )


def block_layout(first_pos, tok_rows, lengths_row, seg_cap):
    position = first_pos + jnp.arange(tok_rows, dtype=jnp.int32)
    segment = position // seg_cap
    offset = position - segment * seg_cap
    picked = segment[:, None] == jnp.arange(lengths_row.shape[0], dtype=jnp.int32)[None, :]
    seg_len = jnp.sum(jnp.where(picked, lengths_row[None, :], 0), axis=1)
    present = offset < seg_len
    summary = present & (offset >= seg_len - SUMMARY)
    return (position, segment, present, summary)


def allowed_keys(my_layout, theirs):
    own_seg = (theirs[1][None, :] == my_layout[1][:, None]) & (
        theirs[0][None, :] <= my_layout[0][:, None]
    )
    own_seg = own_seg & (theirs[2][None, :] | (theirs[0][None, :] == my_layout[0][:, None]))
    return own_seg


def fold_block(softmax_state, queries, key_rows, value_rows, allowed):
    row_peak, row_total, partial_sum = softmax_state
    scores = jnp.einsum("qhd,khd->hqk", queries, key_rows, preferred_element_type=jnp.float32)
    scores = jnp.where(allowed[None], scores, MASKED)
    new_peak = jnp.maximum(row_peak, jnp.max(scores, axis=-1, keepdims=True))
    powers = jnp.where(allowed[None], jnp.exp(scores - new_peak), 0.0)
    factor = jnp.exp(row_peak - new_peak)
    row_total = row_total * factor + jnp.sum(powers, axis=-1, keepdims=True)
    partial_sum = partial_sum * factor + jnp.einsum(
        "hqk,khd->hqd", powers.astype(jnp.bfloat16), value_rows, preferred_element_type=jnp.float32
    )
    return (new_peak, row_total, partial_sum)


def grad_block(queries, key_rows, value_rows, allowed, log_total, grad_mixed, row_delta):
    scores = jnp.einsum("qhd,khd->hqk", queries, key_rows, preferred_element_type=jnp.float32)
    weights = jnp.where(allowed[None], jnp.exp(scores - log_total), 0.0)
    grad_weights = jnp.einsum(
        "qhd,khd->hqk", grad_mixed, value_rows, preferred_element_type=jnp.float32
    )
    grad_scores = (weights * (grad_weights - row_delta)).astype(jnp.bfloat16)
    delta_queries = jnp.einsum(
        "hqk,khd->qhd", grad_scores, key_rows, preferred_element_type=jnp.float32
    )
    delta_keys = jnp.einsum(
        "hqk,qhd->khd", grad_scores, queries, preferred_element_type=jnp.float32
    )
    delta_values = jnp.einsum(
        "hqk,qhd->khd", weights.astype(jnp.bfloat16), grad_mixed, preferred_element_type=jnp.float32
    )
    return (delta_queries, delta_keys, delta_values)


def body(
    tokens,
    seg_lengths,
    ln1_gain,
    ln1_bias,
    w_query,
    q_bias,
    w_key,
    w_value,
    v_bias,
    w_out,
    o_bias,
    ln2_gain,
    ln2_bias,
    w_up,
    up_bias,
    w_down,
    down_bias,
    d_out,
):
    tok_rows = tokens.shape[1]
    features = tokens.shape[2]
    heads = features // HEAD
    devices = lax.axis_size("seq")
    my_index = lax.axis_index("seq")
    seg_cap = tok_rows * SEG_DEVS
    lengths_row = seg_lengths[0]
    seg_count = lengths_row.shape[0]
    my_layout = block_layout(my_index * tok_rows, tok_rows, lengths_row, seg_cap)
    pass_turns = SEG_DEVS - 1
    wq_all, wk_all, wv_all, wo_all, gain_one, shift_one, bias_query, bias_value, bias_out = (
        lax.all_gather(w_query, "seq", axis=0, tiled=True),
        lax.all_gather(w_key, "seq", axis=0, tiled=True),
        lax.all_gather(w_value, "seq", axis=0, tiled=True),
        lax.all_gather(w_out, "seq", axis=0, tiled=True),
        lax.all_gather(ln1_gain, "seq", axis=0, tiled=True),
        lax.all_gather(ln1_bias, "seq", axis=0, tiled=True),
        lax.all_gather(q_bias, "seq", axis=0, tiled=True),
        lax.all_gather(v_bias, "seq", axis=0, tiled=True),
        lax.all_gather(o_bias, "seq", axis=0, tiled=True),
    )
    gain_one = gain_one.astype(jnp.float32)
    shift_one = shift_one.astype(jnp.float32)
    input_rows = tokens[0].astype(jnp.float32)
    normed_in = norm_rows(input_rows, gain_one, shift_one).astype(jnp.bfloat16)
    head_shape = (tok_rows, heads, HEAD)
    queries = (
        ((jnp.dot(normed_in, wq_all, preferred_element_type=jnp.float32) + bias_query) * 0.125)
        .astype(jnp.bfloat16)
        .reshape(head_shape)
    )
    key_flat = jnp.dot(normed_in, wk_all, preferred_element_type=jnp.float32).astype(jnp.bfloat16)
    value_flat = (
        jnp.dot(normed_in, wv_all, preferred_element_type=jnp.float32) + bias_value
    ).astype(jnp.bfloat16)
    kv_local = jnp.stack([key_flat, value_flat])
    softmax_state = (
        jnp.full((heads, tok_rows, 1), MASKED, jnp.float32),
        jnp.zeros((heads, tok_rows, 1), jnp.float32),
        jnp.zeros((heads, tok_rows, HEAD), jnp.float32),
    )
    softmax_state = fold_block(
        softmax_state,
        queries,
        key_flat.reshape(head_shape),
        value_flat.reshape(head_shape),
        allowed_keys(my_layout, my_layout),
    )

    def forward_turn(turn_index, loop_carry):
        current_state, blocks = loop_carry
        blocks = shifted(blocks, "seq", 1)
        source = (my_index - turn_index - 1) % devices
        theirs = block_layout(source * tok_rows, tok_rows, lengths_row, seg_cap)
        allowed = allowed_keys(my_layout, theirs)
        current_state = lax.cond(
            jnp.any(allowed),
            lambda current: fold_block(
                current,
                queries,
                blocks[0].reshape(head_shape),
                blocks[1].reshape(head_shape),
                allowed,
            ),
            lambda current: current,
            current_state,
        )
        return (current_state, blocks)

    softmax_state, unused_kv = lax.fori_loop(0, pass_turns, forward_turn, (softmax_state, kv_local))
    slot_ids = jnp.arange(seg_count * SUMMARY, dtype=jnp.int32)
    slot_seg = slot_ids // SUMMARY
    slot_pick = slot_seg[:, None] == jnp.arange(seg_count, dtype=jnp.int32)[None, :]
    slot_len = jnp.sum(jnp.where(slot_pick, lengths_row[None, :], 0), axis=1)
    slot_pos = slot_seg * seg_cap + slot_len - SUMMARY + (slot_ids - slot_seg * SUMMARY)
    selector = (my_layout[0][None, :] == slot_pos[:, None]).astype(jnp.bfloat16)
    my_segment = my_index * tok_rows // seg_cap
    my_seg_len = jnp.sum(
        jnp.where(jnp.arange(seg_count, dtype=jnp.int32) == my_segment, lengths_row, 0)
    )
    window_pos = my_segment * seg_cap + my_seg_len - SUMMARY + jnp.arange(SUMMARY, dtype=jnp.int32)
    window_pick = (my_layout[0][None, :] == window_pos[:, None]).astype(jnp.bfloat16)
    window_rows = jnp.dot(
        window_pick,
        jnp.concatenate([key_flat, value_flat], axis=1),
        preferred_element_type=jnp.float32,
    ).astype(jnp.bfloat16)
    gathered = lax.all_gather(window_rows, "seq", axis=0, tiled=True)
    summary_kv = (
        jnp.sum(
            gathered.reshape(seg_count, SEG_DEVS, SUMMARY, 2 * features).astype(jnp.float32), axis=1
        )
        .reshape(seg_count * SUMMARY, 2 * features)
        .astype(jnp.bfloat16)
    )
    summary_keys = summary_kv[:, :features].reshape(seg_count * SUMMARY, heads, HEAD)
    summary_values = summary_kv[:, features:].reshape(seg_count * SUMMARY, heads, HEAD)
    summary_allowed = slot_seg[None, :] < my_layout[1][:, None]
    softmax_state = fold_block(
        softmax_state, queries, summary_keys, summary_values, summary_allowed
    )
    row_peak, row_total, partial_sum = softmax_state
    attended = partial_sum / row_total
    log_total = row_peak + jnp.log(row_total)
    mixed_rows = attended.transpose(1, 0, 2).reshape(tok_rows, features).astype(jnp.bfloat16)
    hidden = input_rows + jnp.dot(mixed_rows, wo_all, preferred_element_type=jnp.float32) + bias_out
    w_up_all, w_down_all, gain_two, shift_two, bias_up, bias_down = (
        lax.all_gather(w_up, "seq", axis=0, tiled=True),
        lax.all_gather(w_down, "seq", axis=0, tiled=True),
        lax.all_gather(ln2_gain, "seq", axis=0, tiled=True),
        lax.all_gather(ln2_bias, "seq", axis=0, tiled=True),
        lax.all_gather(up_bias, "seq", axis=0, tiled=True),
        lax.all_gather(down_bias, "seq", axis=0, tiled=True),
    )
    gain_two = gain_two.astype(jnp.float32)
    shift_two = shift_two.astype(jnp.float32)
    normed_mid = norm_rows(hidden, gain_two, shift_two).astype(jnp.bfloat16)
    pre_act = jnp.dot(normed_mid, w_up_all, preferred_element_type=jnp.float32) + bias_up
    active = jax.nn.gelu(pre_act, approximate=True).astype(jnp.bfloat16)
    result = hidden + contract_last(active, w_down_all) + bias_down
    grad_out = d_out[0]
    w_up_all, w_down_all, gain_two, shift_two, bias_up, bias_down = (
        lax.all_gather(w_up, "seq", axis=0, tiled=True),
        lax.all_gather(w_down, "seq", axis=0, tiled=True),
        lax.all_gather(ln2_gain, "seq", axis=0, tiled=True),
        lax.all_gather(ln2_bias, "seq", axis=0, tiled=True),
        lax.all_gather(up_bias, "seq", axis=0, tiled=True),
        lax.all_gather(down_bias, "seq", axis=0, tiled=True),
    )
    gain_two = gain_two.astype(jnp.float32)
    shift_two = shift_two.astype(jnp.float32)
    grad_active = jnp.dot(grad_out, w_down_all, preferred_element_type=jnp.float32)
    unused_value, gelu_back = jax.vjp(lambda inner: jax.nn.gelu(inner, approximate=True), pre_act)
    grad_pre = gelu_back(grad_active)[0].astype(jnp.bfloat16)
    grad_mid = contract_last(grad_pre, w_up_all)
    unused_norm, second_back = jax.vjp(norm_rows, hidden, gain_two, shift_two)
    grad_hidden, grad_gain_two, grad_shift_two = second_back(grad_mid)
    grad_hidden = grad_hidden + grad_out.astype(jnp.float32)
    grad_branch = grad_hidden.astype(jnp.bfloat16)
    wq_all, wk_all, wv_all, wo_all, gain_one, shift_one, bias_query, bias_value, bias_out = (
        lax.all_gather(w_query, "seq", axis=0, tiled=True),
        lax.all_gather(w_key, "seq", axis=0, tiled=True),
        lax.all_gather(w_value, "seq", axis=0, tiled=True),
        lax.all_gather(w_out, "seq", axis=0, tiled=True),
        lax.all_gather(ln1_gain, "seq", axis=0, tiled=True),
        lax.all_gather(ln1_bias, "seq", axis=0, tiled=True),
        lax.all_gather(q_bias, "seq", axis=0, tiled=True),
        lax.all_gather(v_bias, "seq", axis=0, tiled=True),
        lax.all_gather(o_bias, "seq", axis=0, tiled=True),
    )
    gain_one = gain_one.astype(jnp.float32)
    shift_one = shift_one.astype(jnp.float32)
    grad_mixed = contract_last(grad_branch, wo_all).astype(jnp.bfloat16).reshape(head_shape)
    row_delta = jnp.sum(
        grad_mixed.astype(jnp.float32).transpose(1, 0, 2) * attended, axis=-1, keepdims=True
    )
    first_q, first_k, first_v = grad_block(
        queries,
        key_flat.reshape(head_shape),
        value_flat.reshape(head_shape),
        allowed_keys(my_layout, my_layout),
        log_total,
        grad_mixed,
        row_delta,
    )
    pending = jnp.stack([first_k.reshape(tok_rows, features), first_v.reshape(tok_rows, features)])

    def backward_turn(turn_index, loop_carry):
        grad_queries, blocks, waiting = loop_carry
        blocks = shifted(blocks, "seq", 1)
        waiting = from_behind(waiting.astype(jnp.bfloat16), "seq", 1).astype(waiting.dtype)
        source = (my_index - turn_index - 1) % devices
        theirs = block_layout(source * tok_rows, tok_rows, lengths_row, seg_cap)
        allowed = allowed_keys(my_layout, theirs)

        def add_block(current):
            sum_queries, sum_waiting = current
            delta_queries, delta_keys, delta_values = grad_block(
                queries,
                blocks[0].reshape(head_shape),
                blocks[1].reshape(head_shape),
                allowed,
                log_total,
                grad_mixed,
                row_delta,
            )
            return (
                sum_queries + delta_queries,
                sum_waiting
                + jnp.stack(
                    [
                        delta_keys.reshape(tok_rows, features),
                        delta_values.reshape(tok_rows, features),
                    ]
                ),
            )

        grad_queries, waiting = lax.cond(
            jnp.any(allowed), add_block, lambda current: current, (grad_queries, waiting)
        )
        return (grad_queries, blocks, waiting)

    grad_queries, unused_blocks, pending = lax.fori_loop(
        0, pass_turns, backward_turn, (first_q, kv_local, pending)
    )
    pending = from_behind(pending.astype(jnp.bfloat16), "seq", -pass_turns).astype(pending.dtype)
    sum_dq, sum_dk, sum_dv = grad_block(
        queries, summary_keys, summary_values, summary_allowed, log_total, grad_mixed, row_delta
    )
    grad_queries = grad_queries + sum_dq
    summary_part = jnp.concatenate(
        [
            sum_dk.reshape(seg_count * SUMMARY, features),
            sum_dv.reshape(seg_count * SUMMARY, features),
        ],
        axis=1,
    )
    summary_total = lax.psum(summary_part, "seq")
    returned = jnp.dot(selector.astype(jnp.float32).T, summary_total, precision=HIGHEST)
    pending = pending + jnp.stack([returned[:, :features], returned[:, features:]])
    grad_keys = pending[0].astype(jnp.bfloat16)
    grad_values = pending[1].astype(jnp.bfloat16)
    grad_query_rows = grad_queries.reshape(tok_rows, features).astype(jnp.bfloat16) * jnp.bfloat16(
        0.125
    )
    grad_normed = (
        contract_last(grad_query_rows, wq_all)
        + contract_last(grad_keys, wk_all)
        + contract_last(grad_values, wv_all)
    )
    unused_first, first_back = jax.vjp(norm_rows, input_rows, gain_one, shift_one)
    grad_input, grad_gain_one, grad_shift_one = first_back(grad_normed)
    grad_input = grad_input + grad_hidden
    matrix_grads = lax.psum_scatter(
        jnp.concatenate(
            [
                contract_first(normed_in, grad_query_rows),
                contract_first(normed_in, grad_keys),
                contract_first(normed_in, grad_values),
                contract_first(mixed_rows, grad_branch),
                contract_first(normed_mid, grad_pre),
                contract_first(grad_out, active),
            ],
            axis=1,
        ),
        "seq",
        scatter_dimension=0,
        tiled=True,
    )
    vector_shares = (
        lax.psum_scatter(grad_gain_one, "seq", scatter_dimension=0, tiled=True),
        lax.psum_scatter(grad_shift_one, "seq", scatter_dimension=0, tiled=True),
        lax.psum_scatter(
            jnp.sum(grad_query_rows.astype(jnp.float32), axis=0),
            "seq",
            scatter_dimension=0,
            tiled=True,
        ),
        lax.psum_scatter(
            jnp.sum(grad_values.astype(jnp.float32), axis=0), "seq", scatter_dimension=0, tiled=True
        ),
        lax.psum_scatter(
            jnp.sum(grad_branch.astype(jnp.float32), axis=0), "seq", scatter_dimension=0, tiled=True
        ),
        lax.psum_scatter(grad_gain_two, "seq", scatter_dimension=0, tiled=True),
        lax.psum_scatter(grad_shift_two, "seq", scatter_dimension=0, tiled=True),
        lax.psum_scatter(
            jnp.sum(grad_pre.astype(jnp.float32), axis=0), "seq", scatter_dimension=0, tiled=True
        ),
        lax.psum_scatter(
            jnp.sum(grad_out.astype(jnp.float32), axis=0), "seq", scatter_dimension=0, tiled=True
        ),
    )
    totals = (
        lax.psum(matrix_grads.astype(jnp.bfloat16), "batch").astype(jnp.float32),
        lax.psum(vector_shares[0].astype(jnp.bfloat16), "batch").astype(jnp.float32),
        lax.psum(vector_shares[1].astype(jnp.bfloat16), "batch").astype(jnp.float32),
        lax.psum(vector_shares[2].astype(jnp.bfloat16), "batch").astype(jnp.float32),
        lax.psum(vector_shares[3].astype(jnp.bfloat16), "batch").astype(jnp.float32),
        lax.psum(vector_shares[4].astype(jnp.bfloat16), "batch").astype(jnp.float32),
        lax.psum(vector_shares[5].astype(jnp.bfloat16), "batch").astype(jnp.float32),
        lax.psum(vector_shares[6].astype(jnp.bfloat16), "batch").astype(jnp.float32),
        lax.psum(vector_shares[7].astype(jnp.bfloat16), "batch").astype(jnp.float32),
        lax.psum(vector_shares[8].astype(jnp.bfloat16), "batch").astype(jnp.float32),
    )
    matrices = totals[0]
    ff_width = w_up.shape[1]
    g_query = matrices[:, 0:features]
    g_key = matrices[:, features : 2 * features]
    g_value = matrices[:, 2 * features : 3 * features]
    g_out = matrices[:, 3 * features : 4 * features]
    g_up = matrices[:, 4 * features : 4 * features + ff_width]
    g_down = matrices[:, 4 * features + ff_width :]
    return (
        result.astype(jnp.bfloat16)[None],
        grad_input[None],
        totals[1],
        totals[2],
        g_query,
        totals[3],
        g_key,
        g_value,
        totals[4],
        g_out,
        totals[5],
        totals[6],
        totals[7],
        g_up,
        totals[8],
        g_down,
        totals[9],
    )


def solution(mesh):
    placed = (
        P("batch", "seq", None),
        P("batch", None),
        P("seq"),
        P("seq"),
        P("seq", None),
        P("seq"),
        P("seq", None),
        P("seq", None),
        P("seq"),
        P("seq", None),
        P("seq"),
        P("seq"),
        P("seq"),
        P("seq", None),
        P("seq"),
        P("seq", None),
        P("seq"),
        P("batch", "seq", None),
    )
    return jax.shard_map(
        body,
        mesh=mesh,
        in_specs=placed,
        out_specs=(
            P("batch", "seq", None),
            P("batch", "seq", None),
            P("seq"),
            P("seq"),
            P("seq", None),
            P("seq"),
            P("seq", None),
            P("seq", None),
            P("seq"),
            P("seq", None),
            P("seq"),
            P("seq"),
            P("seq"),
            P("seq", None),
            P("seq"),
            P("seq", None),
            P("seq"),
        ),
        check_vma=False,
    )
```

profile of v0, /device:TPU:1, one launch (start us, length us, event | category | flops | bytes accessed | tf_op | source)
XLA Modules:
  0.0 2324.9 jit_solution(15165452266670400036)
XLA Ops:
  21.4 276.8 %all-reduce.21 = (bf16[768]{0:T(1024)(128)(2,1)S(1)}, bf16[768]{0:T(1024)(128)(2,1)S(1)}, bf16[768]{0:T(1024)(128)(2,1)S(1)}, bf16[768]{0:T(1024)(128)(2,1)S(1)}...) all-reduce(bf16[768]{0:T(1024)(128)(2,1)S(1)} %dynamic-update-slice, ...), channel_id=1, replica_groups=mesh['seq'=64,'batch'=2] {'seq'}, use_global_device_ids=true, to_apply=%add.3 | all-reduce | flops 9216 | bytes 36864
  302.5 2.3 reshape.624
  304.8 2.7 reshape.626
  310.7 12.6 all-gather.15.cloned.1.call-done
  323.3 2.2 reshape.622
  328.2 98.5 %all-gather.23.cloned.1.call-done = bf16[64,12,768]{2,1,0:T(8,128)(2,1)} async-done(((bf16[1,12,768]{2,1,0:T(8,128)(2,1)}), bf16[64,12,768]{2,1,0:T(8,128)(2,1)}) %all-gather.23.cloned.1.call-update) | async-done | bytes 1179664 | tf_op jit(solution)/shard_map/all_gather | solution.py:131
  426.7 3.1 reshape.630
  430.7 105.4 %all-gather.27.cloned.1.call-done = bf16[64,12,3072]{2,1,0:T(8,128)(2,1)} async-done(((bf16[1,12,3072]{2,1,0:T(8,128)(2,1)}), bf16[64,12,3072]{2,1,0:T(8,128)(2,1)}) %all-gather.27.cloned.1.call-update) | async-done | bytes 4718608 | tf_op jit(solution)/shard_map/all_gather | solution.py:225
  536.1 7.5 reshape.634
  543.6 101.8 %all-gather.25.cloned.1.call-done = bf16[64,12,3072]{2,1,0:T(8,128)(2,1)} async-done(((bf16[1,12,3072]{2,1,0:T(8,128)(2,1)}), bf16[64,12,3072]{2,1,0:T(8,128)(2,1)}) %all-gather.25.cloned.1.call-update) | async-done | bytes 4718608 | tf_op jit(solution)/shard_map/all_gather | solution.py:224
  645.4 7.5 reshape.632
  652.9 109.9 %all-gather.21.cloned.1.call-done = bf16[64,50,1536]{2,1,0:T(8,128)(2,1)} async-done(((bf16[1,50,1536]{2,1,0:T(8,128)(2,1)}), bf16[64,50,1536]{2,1,0:T(8,128)(2,1)}) %all-gather.21.cloned.1.call-update) | async-done | bytes 9830416 | tf_op jit(solution)/shard_map/all_gather | solution.py:204
  762.8 8.4 bitcast_reduce_fusion
  771.3 4.3 convert_element_type.292
  775.5 3.2 fusion.145
  780.6 2.9 copy.107
  783.5 3.2 select_reduce_fusion.2
  786.8 30.4 %while.46 = (s32[]{:T(128)}, f32[12,128,1]{1,0,2:T(8,128)S(1)}, f32[12,128,1]{1,0,2:T(8,128)S(1)}, f32[12,128,64]{1,2,0:T(8,128)S(1)}, bf16[2,128,768]{1,2,0:T(8...) while((s32[]{:T(128)}, f32[12,128,1]{1,0,2:T(8,128)S(1)}, ...), condition=%wide.region_12.13_spmd.clone.clone, body=%wide.region_5.12_spmd.clone.clone.sunk | while | flops 52232976 | bytes 7051520 | solution.py:186
  786.8 2.6 collective-permute-start
  791.0 3.4 collective-permute-done
  796.0 4.3 collective-permute-start
  801.9 3.4 collective-permute-done
  806.0 5.1 collective-permute-start
  812.8 3.4 collective-permute-done
  817.2 3.6 fusion.25
  821.0 2.8 fusion.150
  825.7 2.5 convert_reduce_fusion
  828.2 2.3 multiply_reduce_fusion
  833.7 3.5 fusion.27
  837.3 4.1 multiply_convert_fusion
  842.9 2.7 pad_maximum_fusion
  850.8 44.7 %while.47 = (s32[]{:T(128)}, f32[128,12,64]{0,2,1:T(8,128)S(1)}, bf16[2,128,768]{1,2,0:T(8,128)(2,1)}, f32[2,128,768]{1,2,0:T(8,128)S(1)}, s32[]{:T(128)}, /*ind...) while((s32[]{:T(128)}, f32[128,12,64]{0,2,1:T(8,128)S(1)}, ...), condition=%wide.region_27.28_spmd.clone.clone, body=%wide.region_22.27_spmd.clone.clone.sunk | while | flops 128020752 | bytes 15976760 | solution.py:319
  850.9 2.4 collective-permute-start.1
  853.4 2.0 collective-permute-start.2
  858.1 5.2 collective-permute-done.2
  866.1 2.4 collective-permute-start.1
  872.1 2.1 collective-permute-done.1
  874.2 5.2 collective-permute-done.2
  880.3 4.4 collective-permute-start.1
  889.6 5.2 collective-permute-done.2
  895.8 4.7 collective-permute-start.3
  900.5 2.8 convert_reduce_fusion.5
  904.0 2.2 convolution_dynamic-update-slice_fusion.4
  906.1 509.9 %all-reduce.26.cloned.1.call-done = f32[800,1536]{0,1:T(8,128)} async-done(((f32[800,1536]{0,1:T(8,128)}), f32[800,1536]{0,1:T(8,128)}) %all-reduce.26.cloned.1.call-update) | async-done | bytes 4915216 | tf_op jit(solution)/shard_map/psum | solution.py:334
  1416.0 5.9 fusion.95
  1422.0 2.1 convolution_dynamic-update-slice_fusion.3
  1424.1 2.1 convolution_dynamic-update-slice_fusion.2
  1428.2 5.1 convolution_dynamic-update-slice_fusion
  1433.3 5.0 bitcast_dynamic-update-slice_fusion
  1438.3 400.8 %fusion.8 = f32[16,9216]{1,0:T(8,128)S(1)} fusion(f32[768,9216]{1,0:T(8,128)} %bitcast_dynamic-update-slice_fusion), kind=kCustom, calls=%all-reduce-scatter | all-reduce-scatter fusion | flops 9437185 | bytes 28901888
  1845.8 4.5 collective-permute-start.16
  1850.3 5.9 collective-permute-start.15
  1860.1 19.4 collective-permute-start.13
  1879.6 8.4 collective-permute-start.12
  1888.0 3.8 collective-permute-start.11
  1891.8 2.9 collective-permute-start.10
  1897.2 269.5 %all-reduce.20 = (bf16[768]{0:T(1024)(128)(2,1)S(1)}, bf16[768]{0:T(1024)(128)(2,1)S(1)}, bf16[768]{0:T(1024)(128)(2,1)S(1)}, bf16[768]{0:T(1024)(128)(2,1)S(1)}...) all-reduce(f32[768]{0:T(1024)S(1)} %get-tuple-element.910, ...), channel_id=2, replica_groups=mesh['seq'=64,'batch'=2] {'seq'}, use_global_device_ids=true, to_apply=%region_33.34.clone | all-reduce | flops 9216 | bytes 55296
  2167.4 2.3 collective-permute-start.8
  2173.8 2.0 collective-permute-start.5
  2175.8 3.5 collective-permute-start.4
  2179.3 4.8 fusion.57
  2184.1 5.5 all-reduce.22
  2194.3 80.4 %concatenate.12 = bf16[268,9216]{1,0:T(8,128)(2,1)} concatenate(bf16[12,9216]{1,0:T(8,128)(2,1)S(1)} %copy-done.31, bf16[16,9216]{1,0:T(8,128)(2,1)} %copy-done.32, bf16[16,9216]{1,0:T(8,128)(2,1)} %copy-done.33, bf16[16,9216]{1,0:T(8,128)(2,1)} %copy-done.34, bf16[16,9216]{1,0:T(8,128)(2,1)} %copy-done.35, bf16[16,9216]{1,0:T(8,128)(2,1)} %copy-done.36, ...), dimensions={0} | concatenate | bytes 10174464
  2277.5 37.5 %all-reduce.28.cloned.1.call-done = bf16[12,9216]{1,0:T(8,128)(2,1)} async-done(((bf16[12,9216]{1,0:T(8,128)(2,1)}), bf16[12,9216]{1,0:T(8,128)(2,1)}) %all-reduce.28.cloned.1.call-update) | async-done | bytes 221200 | tf_op jit(solution)/shard_map/psum | solution.py:391
  (360 shorter events, 87.2 us)
Async XLA Ops:
  7.2 295.3 %all-gather.17.cloned.1.call-start = ((), (), s32[]{:S(2)}) async-start(), calls=%async_computation.3 | async-start | bytes 1597440 | tf_op jit(solution)/shard_map/all_gather | solution.py:129
  7.9 296.9 %all-gather.19.cloned.1.call-start = ((), (), s32[]{:S(2)}) async-start(), calls=%async_computation.4 | async-start | bytes 1597440 | tf_op jit(solution)/shard_map/all_gather | solution.py:130
  8.7 314.6 %all-gather.15.cloned.1.call-start = ((), (), s32[]{:S(2)}) async-start(), calls=%async_computation.2 | async-start | bytes 1597440 | tf_op jit(solution)/shard_map/all_gather | solution.py:128
  9.4 417.2 %all-gather.23.cloned.1.call-start = ((), (), s32[]{:S(2)}) async-start(), calls=%async_computation.6 | async-start | bytes 1597440 | tf_op jit(solution)/shard_map/all_gather | solution.py:131
  10.0 526.1 %all-gather.27.cloned.1.call-start = ((), (), s32[]{:S(2)}) async-start(), calls=%async_computation.8 | async-start | bytes 6389760 | tf_op jit(solution)/shard_map/all_gather | solution.py:225
  10.6 634.8 %all-gather.25.cloned.1.call-start = ((), (), s32[]{:S(2)}) async-start(), calls=%async_computation.7 | async-start | bytes 6389760 | tf_op jit(solution)/shard_map/all_gather | solution.py:224
  11.1 751.7 %all-gather.21.cloned.1.call-start = ((), (), s32[]{:S(2)}) async-start(), calls=%async_computation.5 | async-start | bytes 11182080 | tf_op jit(solution)/shard_map/all_gather | solution.py:204
  300.3 9.7 copy-start.50
  302.5 1121.6 %copy-start.44 = (f32[128]{0:T(128)}, f32[128]{0:T(128)S(1)}, u32[]{:S(2)}) copy-start(f32[128]{0:T(128)S(1)} %fusion.118) | copy-start | bytes 1540
  309.6 1106.5 %all-reduce.26.cloned.1.call-start = ((), (), s32[]{:S(2)}) async-start(), calls=%async_computation | async-start | bytes 11010048 | tf_op jit(solution)/shard_map/psum | solution.py:334
  310.5 119.3 %copy-start.19 = (bf16[128,768]{0,1:T(8,128)(2,1)}, bf16[128,768]{0,1:T(8,128)(2,1)S(1)}, u32[]{:S(2)}) copy-start(bf16[128,768]{0,1:T(8,128)(2,1)S(1)} %copy.102) | copy-start | bytes 589828
  310.6 119.7 %copy-start.26 = (bf16[128,768]{0,1:T(8,128)(2,1)}, bf16[128,768]{0,1:T(8,128)(2,1)S(1)}, u32[]{:S(2)}) copy-start(bf16[128,768]{0,1:T(8,128)(2,1)S(1)} %copy.103) | copy-start | bytes 589828
  327.4 102.4 %copy-start.25 = (bf16[2,128,768]{1,2,0:T(8,128)(2,1)}, bf16[2,128,768]{1,2,0:T(8,128)(2,1)S(1)}, u32[]{:S(2)}) copy-start(bf16[2,128,768]{1,2,0:T(8,128)(2,1)S(1)} %copy.105) | copy-start | bytes 1179652
  786.8 7.6 collective-permute-start
  796.0 9.3 collective-permute-start
  806.0 10.2 collective-permute-start
  817.2 8.3 slice-start.2
  845.6 1469.4 %all-reduce.28.cloned.1.call-start = ((), (), s32[]{:S(2)}) async-start(), calls=%async_computation.1 | async-start | bytes 589824 | tf_op jit(solution)/shard_map/psum | solution.py:391
  850.9 7.2 collective-permute-start.1
  853.4 10.0 collective-permute-start.2
  866.1 8.0 collective-permute-start.1
  868.6 10.9 collective-permute-start.2
  880.3 9.2 collective-permute-start.1
  884.7 10.1 collective-permute-start.2
  895.8 526.2 %collective-permute-start.3 = (bf16[2,128,768]{2,1,0:T(8,128)(2,1)S(1)}, bf16[2,128,768]{2,1,0:T(8,128)(2,1)S(1)}, u32[]{:S(2)}, u32[]{:S(2)}) collective-permute-start(bf16[2,128,768]{2,1,0:T(8,128)(2,1)S(1)} %copy.114), channel_id=1, source_target_pairs={{0,122},{2,124},{4,126},{6,0},{8,2},{10,4},{12,6},{14,8},{16,10},{... | collective-permute-start | bytes 1179656 | tf_op jit(solution)/shard_map/ppermute | solution.py:24
  903.3 512.7 %copy-start.51 = (s32[128]{0:T(128)S(1)}, s32[128]{0:T(128)}, u32[]{:S(2)}) copy-start(s32[128]{0:T(128)} %copy-done.50) | copy-start | bytes 1540
  1839.1 18.5 copy-start.11
  1839.1 17.1 collective-permute-start.19
  1842.4 15.8 copy-start.9
  1843.1 17.0 collective-permute-start.18
  1844.4 35.1 %collective-permute-start.17 = (bf16[16,9216]{1,0:T(8,128)(2,1)}, bf16[16,9216]{1,0:T(8,128)(2,1)S(1)}, u32[]{:S(2)}, u32[]{:S(2)}) collective-permute-start(bf16[16,9216]{1,0:T(8,128)(2,1)} %convert.57), channel_id=1, source_target_pairs={{0,28},{2,30},{4,32},{6,34},{8,36},{10,38},{12,40},{14,42},{16,44}... | collective-permute-start | bytes 884744
  1845.8 42.2 %collective-permute-start.16 = (bf16[16,9216]{1,0:T(8,128)(2,1)}, bf16[16,9216]{1,0:T(8,128)(2,1)S(1)}, u32[]{:S(2)}, u32[]{:S(2)}) collective-permute-start(bf16[16,9216]{1,0:T(8,128)(2,1)} %convert.57), channel_id=1, source_target_pairs={{0,26},{2,28},{4,30},{6,32},{8,34},{10,36},{12,38},{14,40},{16,42}... | collective-permute-start | bytes 884744
  1850.3 41.5 %collective-permute-start.15 = (bf16[16,9216]{1,0:T(8,128)(2,1)}, bf16[16,9216]{1,0:T(8,128)(2,1)S(1)}, u32[]{:S(2)}, u32[]{:S(2)}) collective-permute-start(bf16[16,9216]{1,0:T(8,128)(2,1)} %convert.57), channel_id=1, source_target_pairs={{0,24},{2,26},{4,28},{6,30},{8,32},{10,34},{12,36},{14,38},{16,40}... | collective-permute-start | bytes 884744
  1856.3 38.5 %collective-permute-start.14 = (bf16[16,9216]{1,0:T(8,128)(2,1)}, bf16[16,9216]{1,0:T(8,128)(2,1)S(1)}, u32[]{:S(2)}, u32[]{:S(2)}) collective-permute-start(bf16[16,9216]{1,0:T(8,128)(2,1)} %convert.57), channel_id=1, source_target_pairs={{0,22},{2,24},{4,26},{6,28},{8,30},{10,32},{12,34},{14,36},{16,38}... | collective-permute-start | bytes 884744
  1858.2 38.6 %copy-start.59 = (f32[128]{0:T(128)S(1)}, f32[128]{0:T(128)}, u32[]{:S(2)}) copy-start(f32[128]{0:T(128)} %copy-done.58) | copy-start | bytes 1540
  1858.2 38.6 %copy-start.45 = (f32[128]{0:T(128)S(1)}, f32[128]{0:T(128)}, u32[]{:S(2)}) copy-start(f32[128]{0:T(128)} %copy-done.44) | copy-start | bytes 1540
  1858.2 38.9 %copy-start.39 = (f32[768]{0:T(1024)S(1)}, f32[768]{0:T(1024)}, u32[]{:S(2)}) copy-start(f32[768]{0:T(1024)} %get-tuple-element.908) | copy-start | bytes 9220
  1858.2 38.9 %copy-start.40 = (f32[768]{0:T(1024)S(1)}, f32[768]{0:T(1024)}, u32[]{:S(2)}) copy-start(f32[768]{0:T(1024)} %get-tuple-element.912) | copy-start | bytes 9220
  1858.2 38.9 %copy-start.41 = (f32[768]{0:T(1024)S(1)}, f32[768]{0:T(1024)}, u32[]{:S(2)}) copy-start(f32[768]{0:T(1024)} %get-tuple-element.988) | copy-start | bytes 9220
  1858.2 38.9 %copy-start.42 = (f32[768]{0:T(1024)S(1)}, f32[768]{0:T(1024)}, u32[]{:S(2)}) copy-start(f32[768]{0:T(1024)} %get-tuple-element.1031) | copy-start | bytes 9220
  1858.2 38.9 %copy-start.43 = (f32[768]{0:T(1024)S(1)}, f32[768]{0:T(1024)}, u32[]{:S(2)}) copy-start(f32[768]{0:T(1024)} %reduce_sum.330) | copy-start | bytes 9220
  1858.2 38.9 %copy-start.49 = (f32[3072]{0:T(1024)S(1)}, f32[3072]{0:T(1024)}, u32[]{:S(2)}) copy-start(f32[3072]{0:T(1024)} %get-tuple-element.1053) | copy-start | bytes 36868
  1858.2 321.0 %copy-start.52 = (f32[768]{0:T(1024)S(1)}, f32[768]{0:T(1024)}, u32[]{:S(2)}) copy-start(f32[768]{0:T(1024)} %convert_element_type.303) | copy-start | bytes 9220
  1858.9 38.2 %copy-start.15 = (f32[128,768]{1,0:T(8,128)}, f32[128,768]{1,0:T(8,128)S(1)}, u32[]{:S(2)}) copy-start(f32[128,768]{1,0:T(8,128)S(1)} %get-tuple-element.1050) | copy-start | bytes 1179652
  1860.1 36.9 %copy-start.32 = (bf16[16,9216]{1,0:T(8,128)(2,1)}, bf16[16,9216]{1,0:T(8,128)(2,1)S(1)}, u32[]{:S(2)}) copy-start(bf16[16,9216]{1,0:T(8,128)(2,1)S(1)} %collective-permute-done.18) | copy-start | bytes 884740
  1860.1 307.3 %collective-permute-start.13 = (bf16[16,9216]{1,0:T(8,128)(2,1)}, bf16[16,9216]{1,0:T(8,128)(2,1)}, u32[]{:S(2)}, u32[]{:S(2)}) collective-permute-start(bf16[16,9216]{1,0:T(8,128)(2,1)} %convert.57), channel_id=1, source_target_pairs={{0,20},{2,22},{4,24},{6,26},{8,28},{10,30},{12,32},{14,34},{16,36}... | collective-permute-start | bytes 884744
  1879.6 17.5 copy-start.33
  1879.6 290.2 %collective-permute-start.12 = (bf16[16,9216]{1,0:T(8,128)(2,1)}, bf16[16,9216]{1,0:T(8,128)(2,1)}, u32[]{:S(2)}, u32[]{:S(2)}) collective-permute-start(bf16[16,9216]{1,0:T(8,128)(2,1)} %convert.57), channel_id=1, source_target_pairs={{0,18},{2,20},{4,22},{6,24},{8,26},{10,28},{12,30},{14,32},{16,34}... | collective-permute-start | bytes 884744
  1888.0 9.1 copy-start.34
  1888.0 283.8 %collective-permute-start.11 = (bf16[16,9216]{1,0:T(8,128)(2,1)}, bf16[16,9216]{1,0:T(8,128)(2,1)}, u32[]{:S(2)}, u32[]{:S(2)}) collective-permute-start(bf16[16,9216]{1,0:T(8,128)(2,1)} %convert.57), channel_id=1, source_target_pairs={{0,16},{2,18},{4,20},{6,22},{8,24},{10,26},{12,28},{14,30},{16,32}... | collective-permute-start | bytes 884744
  1891.8 282.0 %collective-permute-start.10 = (bf16[16,9216]{1,0:T(8,128)(2,1)}, bf16[16,9216]{1,0:T(8,128)(2,1)}, u32[]{:S(2)}, u32[]{:S(2)}) collective-permute-start(bf16[16,9216]{1,0:T(8,128)(2,1)} %convert.57), channel_id=1, source_target_pairs={{0,14},{2,16},{4,18},{6,20},{8,22},{10,24},{12,26},{14,28},{16,30}... | collective-permute-start | bytes 884744
  1894.7 281.1 %collective-permute-start.9 = (bf16[16,9216]{1,0:T(8,128)(2,1)}, bf16[16,9216]{1,0:T(8,128)(2,1)}, u32[]{:S(2)}, u32[]{:S(2)}) collective-permute-start(bf16[16,9216]{1,0:T(8,128)(2,1)} %convert.57), channel_id=1, source_target_pairs={{0,12},{2,14},{4,16},{6,18},{8,20},{10,22},{12,24},{14,26},{16,28}... | collective-permute-start | bytes 884744
  1896.8 287.3 %copy-start.53 = (f32[128]{0:T(128)}, f32[128]{0:T(128)S(1)}, u32[]{:S(2)}) copy-start(f32[128]{0:T(128)S(1)} %multiply_multiply_fusion.2) | copy-start | bytes 1540
  2167.4 26.9 %copy-start.31 = (bf16[12,9216]{1,0:T(8,128)(2,1)S(1)}, bf16[12,9216]{1,0:T(8,128)(2,1)}, u32[]{:S(2)}) copy-start(bf16[12,9216]{1,0:T(8,128)(2,1)} %copy-done.30) | copy-start | bytes 663556
  2167.4 26.8 %collective-permute-start.8 = (bf16[16,9216]{1,0:T(8,128)(2,1)}, bf16[16,9216]{1,0:T(8,128)(2,1)}, u32[]{:S(2)}, u32[]{:S(2)}) collective-permute-start(bf16[16,9216]{1,0:T(8,128)(2,1)} %convert.57), channel_id=1, source_target_pairs={{0,10},{2,12},{4,14},{6,16},{8,18},{10,20},{12,22},{14,24},{16,26}... | collective-permute-start | bytes 884744
  2169.7 24.5 %collective-permute-start.7 = (bf16[16,9216]{1,0:T(8,128)(2,1)}, bf16[16,9216]{1,0:T(8,128)(2,1)}, u32[]{:S(2)}, u32[]{:S(2)}) collective-permute-start(bf16[16,9216]{1,0:T(8,128)(2,1)} %convert.57), channel_id=1, source_target_pairs={{0,8},{2,10},{4,12},{6,14},{8,16},{10,18},{12,20},{14,22},{16,24},... | collective-permute-start | bytes 884744
  2171.7 22.5 collective-permute-start.6
  2173.8 20.5 collective-permute-start.5
  2175.8 18.4 collective-permute-start.4
  2194.2 82.3 %copy-start.14 = (f32[128,768]{1,0:T(8,128)S(1)}, f32[128,768]{1,0:T(8,128)}, u32[]{:S(2)}) copy-start(f32[128,768]{1,0:T(8,128)} %copy-done.13) | copy-start | bytes 1179652
  2194.2 82.3 %copy-start.16 = (f32[128,768]{1,0:T(8,128)S(1)}, f32[128,768]{1,0:T(8,128)}, u32[]{:S(2)}) copy-start(f32[128,768]{1,0:T(8,128)} %copy-done.15) | copy-start | bytes 1179652
  2194.2 82.3 %copy-start.46 = (f32[128]{0:T(128)S(1)}, f32[128]{0:T(128)}, u32[]{:S(2)}) copy-start(f32[128]{0:T(128)} %copy-done.44) | copy-start | bytes 1540
  2194.2 82.3 %copy-start.54 = (f32[128]{0:T(128)S(1)}, f32[128]{0:T(128)}, u32[]{:S(2)}) copy-start(f32[128]{0:T(128)} %copy-done.53) | copy-start | bytes 1540
  2194.2 82.3 %copy-start.57 = (f32[128]{0:T(128)S(1)}, f32[128]{0:T(128)}, u32[]{:S(2)}) copy-start(f32[128]{0:T(128)} %copy-done.56) | copy-start | bytes 1540
  (38 other events, 109.4 us)
Sparse Core Ops, SparseCore 0:
  9.7 106.5 all-gather.16
  118.0 101.6 all-gather.18
  221.4 101.7 all-gather.14
  324.8 101.7 all-gather.22
  428.2 107.8 all-gather.26
  537.6 107.7 all-gather.24
  647.7 115.1 all-gather.20
  845.7 570.2 all-reduce.25
  2276.6 38.3 all-reduce.27
where the time goes:
time: 2340 us; the launch traced here: 2320 us
  waiting for transfers between devices  1010 us (43%)
  blocking collectives  953 us (41%)
  local copies, waits for them, and re-layouts  145 us (6%)
  starting transfers between devices  96.6 us (4%)
  matrix products  62.5 us (3%)
  other arithmetic  33.4 us (1%)
    unnamed x3, blocking collectives  947 us
    psum x1, waiting for transfers between devices, body(): summary_total = lax.psum(summary_part, 'seq')  510 us
    unnamed x172, local copies, waits for them, and re-layouts  121 us
    all_gather x1, waiting for transfers between devices, body(): gathered = lax.all_gather(window_rows, 'seq', axis=0, tiled=True)  110 us
    all_gather x1, waiting for transfers between devices, body(): lax.all_gather(w_down, 'seq', axis=0, tiled=True)  105 us
    all_gather x1, waiting for transfers between devices, body(): lax.all_gather(w_up, 'seq', axis=0, tiled=True)  102 us
    all_gather x1, waiting for transfers between devices, body(): lax.all_gather(w_out, 'seq', axis=0, tiled=True)  98.5 us
    unnamed x16, starting transfers between devices  64.3 us
  transfers between devices with their start and end apart: 35, of which 17 were waited for; matrix products, arithmetic and copies ran while one was open for 3% of the time, Pallas kernels for 0%

commit v1 on v0

v1 whole, which is shorter than its diff:
```python
import functools
import types

import jax
import jax.numpy as jnp
from jax import lax
from jax.experimental import pallas as pl
from jax.experimental.pallas import tpu as pltpu
from jax.sharding import PartitionSpec as P

BF = jnp.bfloat16
F32 = jnp.float32
MESH = pl.DeviceIdType.MESH
EPSILON = 1e-05
MASKED = -1e30
HIGHEST = lax.Precision.HIGHEST

ROWS = 128
SEG = 512
D = 768
HW = 192
HEADS = 3
SUMMARY = 50
SLOT = 64
SLOTS = 16
KEYS = SEG + SLOTS * SLOT
SUMS = SLOTS * SLOT


def dot(a, b, **kw):
    return jnp.dot(a, b, preferred_element_type=F32, **kw)


def dot_nt(a, b):
    return lax.dot_general(a, b, (((1,), (1,)), ((), ())), preferred_element_type=F32)


def dot_tn(a, b):
    return lax.dot_general(a, b, (((0,), (0,)), ((), ())), preferred_element_type=F32)


def iota(shape, dim):
    return lax.broadcasted_iota(jnp.int32, shape, dim)


def norm_stats(values):
    center = values - jnp.mean(values, axis=-1, keepdims=True)
    spread = jnp.mean(center * center, axis=-1, keepdims=True)
    return center, lax.rsqrt(spread + EPSILON)


SCRATCH = dict(
    pk1=((4, 16, D), BF),
    pk2=((4, 16, 2 * D), BF),
    p01=((4, 16, D), BF),
    p02=((4, 16, 2 * D), BF),
    w1=((4, 4, 48, D), BF),
    w2=((4, 4, 48, 2 * D), BF),
    wosl=((4, D, HW), BF),
    wof=((D, D), BF),
    vb=((16, D), BF),
    vg=((3, 16, D), BF),
    vs1=((16, D), BF),
    vx=((3, 16, D), BF),
    vs2=((16, D), BF),
    vz=((3, 16, D), BF),
    vecs=((16, D), F32),
    toka=((SEG, D), BF),
    doa=((SEG, D), BF),
    nrm=((SEG, D), BF),
    nrmt=((D, SEG), BF),
    dot_=((D, SEG), BF),
    bias=((SEG, SEG), F32),
    q=((SEG, HW), BF),
    kv=((2, KEYS, HW), BF),
    ssrc=((2, SLOT, HW), BF),
    sloc=((HEADS, SEG, SEG), F32),
    ssum=((SEG, SUMS), F32),
    prob=((HEADS, SEG, KEYS), BF),
    att=((SEG, HW), F32),
    atta=((4, SEG, HW), BF),
    attt=((D, SEG), BF),
    hid=((SEG, D), F32),
    nm=((SEG, D), BF),
    nmt=((D, SEG), BF),
    pre=((SEG, D), F32),
    ga=((SEG, D), F32),
    act=((SEG, D), BF),
    gp=((SEG, D), BF),
    rm_s=((SEG, D), BF),
    rm_1=((2, ROWS, D), BF),
    rm_x=((ROWS, D), BF),
    rm_2=((ROWS, D), BF),
    ro_s=((SEG, D), BF),
    ro_1=((2, ROWS, D), BF),
    ro_x=((ROWS, D), BF),
    ro_2=((ROWS, D), BF),
    rn_s=((SEG, D), BF),
    rn_1=((2, ROWS, D), BF),
    rn_x=((ROWS, D), BF),
    rn_2=((ROWS, D), BF),
    gm=((ROWS, D), F32),
    gh=((ROWS, D), F32),
    gbr=((ROWS, D), BF),
    sa=((4, ROWS, HW), BF),
    sb=((4, ROWS, HW), BF),
    do=((4, ROWS, HW), BF),
    gba=((4, ROWS, HW), BF),
    ds=((SEG, SUMS), BF),
    dq=((SEG, HW), F32),
    dkt=((HW, SEG), F32),
    dvt=((HW, SEG), F32),
    dkst=((HW, SUMS), F32),
    dvst=((HW, SUMS), F32),
    dkvs=((2, SUMS, HW), BF),
    sumg=((SLOTS, 2, SLOT, HW), BF),
    dqkv=((SEG, 3 * HW), BF),
    g1=((4, 4, 48, D), BF),
    g2=((4, 4, 48, 2 * D), BF),
    rza1=((3, 4, 48, D // 2), BF),
    rxa1=((3, 48, D // 2), BF),
    rxb1=((3, 4, 48, D // 2), BF),
    rzb1=((3, 48, D // 2), BF),
    ha1=((4, 48, D // 2), BF),
    hb1=((4, 48, D // 2), BF),
    rza2=((3, 4, 48, D), BF),
    rxa2=((3, 48, D), BF),
    rxb2=((3, 4, 48, D), BF),
    rzb2=((3, 48, D), BF),
    ha2=((4, 48, D), BF),
    hb2=((4, 48, D), BF),
    fx1=((4, 16, D), BF),
    fx2=((4, 16, 2 * D), BF),
    fin1=((8, 16, D), BF),
    fin2=((8, 16, 2 * D), BF),
    vgr=((16, D), F32),
    vgx=((3, 16, D), F32),
    vgs=((16, D), F32),
    vgz=((3, 16, D), F32),
    vgt=((16, D), F32),
    vfin=((8, 16, D), F32),
)
COPIES = 224


def layer_kernel(
    seg_ref, tok, dout, wq, wk, wv, wo, wu, wd, vec,
    out_o, gtok_o, gq_o, gk_o, gv_o, go_o, gu_o, gd_o, gvec_o,
    *scratch,
):
    m = types.SimpleNamespace(**dict(zip(SCRATCH, scratch[:-2])))
    ss, rs = scratch[-2:]
    batch = lax.axis_index("batch")
    place = lax.axis_index("seq")
    s = place // 4
    t = place % 4
    z = s // 4
    x = s % 4
    sib = t + 1 - 2 * (t % 2)
    over = (t + 2) % 4
    diag = 3 - t

    def dev(seg, tt, bb):
        return (4 * seg + tt, bb)

    used = [0]
    sent = []

    def take(n=1):
        first = used[0]
        used[0] += n
        return first

    def send(src, dst, device):
        k = take()
        copy = pltpu.make_async_remote_copy(
            src_ref=src, dst_ref=dst, send_sem=ss.at[k], recv_sem=rs.at[k],
            device_id=device, device_id_type=MESH,
        )
        copy.start()
        sent.append(copy)
        return copy

    def rows_of(ref, k):
        return ref.at[pl.ds(pl.multiple_of(k * ROWS, ROWS), ROWS)]

    def get_rows(ref, k):
        return ref[pl.ds(pl.multiple_of(k * ROWS, ROWS), ROWS), :]

    def put_rows(ref, k, value):
        ref[pl.ds(pl.multiple_of(k * ROWS, ROWS), ROWS), :] = value

    group = (over, diag, sib)

    def blocks(count, size, fn, unroll=1):
        def step(j, carry):
            fn(pl.ds(pl.multiple_of(j * size, size), size), j * size)
            return carry

        lax.fori_loop(0, count, step, 0, unroll=unroll)

    m.kv[:, SEG:, :] = jnp.zeros((2, SUMS, HW), BF)
    m.sumg[...] = jnp.zeros((SLOTS, 2, SLOT, HW), BF)
    barrier = pltpu.get_barrier_semaphore()
    partners = [dev(s, u, batch) for u in group]
    partners += [dev((s + k) % 16, t, batch) for k in range(1, 16)]
    partners += [dev(s, u, 1 - batch) for u in (t, sib, over, diag)]
    for partner in partners:
        pl.semaphore_signal(barrier, inc=1, device_id=partner, device_id_type=MESH)
    m.pk1[...] = jnp.zeros((4, 16, D), BF)
    m.pk2[...] = jnp.zeros((4, 16, 2 * D), BF)
    for u in range(4):
        cols = slice(HW * u, HW * u + HW)
        m.pk1[u, 0:12, :] = jnp.concatenate(
            [wq[:, cols], wk[:, cols], wv[:, cols], wo[:, cols]], axis=1
        )
        wide = slice(D * u, D * u + D)
        m.pk2[u, 0:12, 0:D] = wu[:, wide]
        m.pk2[u, 0:12, D:] = wd[:, wide]
    shift = iota((128, D), 1) - iota((128, D), 0)
    put_12 = (shift == 12 * place).astype(BF)
    put_48 = (shift == 48 * (place % 16)).astype(BF)
    narrow = dot(vec[...], put_12)
    wider = dot(vec[...], put_48)
    vec_row = iota((16, D), 0)
    m.vb[...] = jnp.where(
        vec_row < 8, narrow, jnp.where(vec_row == 8 + z, wider[8:9, :], 0.0)
    ).astype(BF)
    pl.semaphore_wait(barrier, len(partners))

    first1 = [send(m.pk1.at[u], m.p01.at[t], dev(s, u, batch)) for u in group]
    firstv = [
        send(m.vb, m.vg.at[k], dev(s, u, batch)) for k, u in enumerate((sib, over, diag))
    ]

    def gather_start(src, ref):
        return [
            send(src, rows_of(ref, t), dev(s, over, batch)),
            send(src, rows_of(ref, t), dev(s, sib, batch)),
        ]

    def gather_pass(copies, ref):
        copies[0].wait_recv()
        copies.append(send(rows_of(ref, over), rows_of(ref, over), dev(s, sib, batch)))

    def gather_end(copies):
        copies[1].wait_recv()
        copies[2].wait_recv()

    ag_tok = gather_start(tok, m.toka)
    first2 = [send(m.pk2.at[u], m.p02.at[t], dev(s, u, batch)) for u in group]
    ag_do = gather_start(dout, m.doa)
    m.p01[t] = m.pk1[t]
    m.p02[t] = m.pk2[t]
    put_rows(m.toka, t, tok[...])
    put_rows(m.doa, t, dout[...])

    row48 = iota((48, 64), 0)
    owner48 = (
        (row48 >= 12).astype(jnp.int32)
        + (row48 >= 24).astype(jnp.int32)
        + (row48 >= 36).astype(jnp.int32)
    )
    squeeze = (iota((48, 64), 1) == row48 + 4 * owner48).astype(BF)

    def spread_start(w, p0, copies, half):
        for copy in copies:
            copy.wait_recv()
        w[z, x] = dot(squeeze, p0[...].reshape(64, 2 * half)).astype(BF)
        a_cols, b_cols = pl.ds(0, half), pl.ds(half, half)
        a = [
            send(w.at[z, x, :, a_cols], w.at[z, x, :, a_cols], dev(4 * z + (x + k) % 4, t, batch))
            for k in (1, 3, 2)
        ]
        b = [
            send(w.at[z, x, :, b_cols], w.at[z, x, :, b_cols], dev(4 * ((z + k) % 4) + x, t, batch))
            for k in (1, 3, 2)
        ]
        return a, b

    def spread_pass(w, phase, half):
        a, b = phase
        a_cols, b_cols = pl.ds(0, half), pl.ds(half, half)
        for copy in a:
            copy.wait_recv()
        a2 = [
            send(w.at[z, :, :, a_cols], w.at[z, :, :, a_cols], dev(4 * ((z + k) % 4) + x, t, batch))
            for k in (1, 3, 2)
        ]
        for copy in b:
            copy.wait_recv()
        b2 = [
            send(w.at[:, x, :, b_cols], w.at[:, x, :, b_cols], dev(4 * z + (x + k) % 4, t, batch))
            for k in (1, 3, 2)
        ]
        return a2 + b2

    def finish(copies):
        for copy in copies:
            copy.wait_recv()

    phase1 = spread_start(m.w1, m.p01, first1, D // 2)
    finish(firstv)
    m.vs1[...] = (
        m.vb[...].astype(F32) + m.vg[0].astype(F32) + m.vg[1].astype(F32) + m.vg[2].astype(F32)
    ).astype(BF)
    vx = [
        send(m.vs1, m.vx.at[k - 1], dev(4 * z + (x + k) % 4, t, batch)) for k in (1, 2, 3)
    ]
    phase2 = spread_start(m.w2, m.p02, first2, D)
    gather_pass(ag_tok, m.toka)
    ends1 = spread_pass(m.w1, phase1, D // 2)
    finish(vx)
    m.vs2[...] = (
        m.vs1[...].astype(F32) + m.vx[0].astype(F32) + m.vx[1].astype(F32) + m.vx[2].astype(F32)
    ).astype(BF)
    vz = [
        send(m.vs2, m.vz.at[k - 1], dev(4 * ((z + k) % 4) + x, t, batch)) for k in (1, 2, 3)
    ]
    gather_pass(ag_do, m.doa)

    seg_len = seg_ref[0, s]
    q_pos = iota((ROWS, SEG), 0)
    k_pos = iota((ROWS, SEG), 1)
    for k in range(4):
        mine = q_pos + ROWS * k
        ok = ((k_pos <= mine) & (k_pos < seg_len)) | (k_pos == mine)
        m.bias[k * ROWS:(k + 1) * ROWS, :] = jnp.where(ok, 0.0, MASKED)
    s_col = iota((8, SUMS), 1)
    sum_bias = jnp.where((s_col < SLOT * s) & (s_col % SLOT < SUMMARY), 0.0, MASKED)[0:1, :]
    pick = (
        (iota((SLOT, SEG), 1) == seg_len - SUMMARY + iota((SLOT, SEG), 0))
        & (iota((SLOT, SEG), 0) < SUMMARY)
    ).astype(BF)
    lane_head = iota((1, HW), 1) // 64

    def of_head(value, h):
        return jnp.where(lane_head == h, value, jnp.zeros_like(value))

    ends2 = spread_pass(m.w2, phase2, D)
    gather_end(ag_tok)
    finish(vz)
    m.vecs[...] = (
        m.vs2[...].astype(F32) + m.vz[0].astype(F32) + m.vz[1].astype(F32) + m.vz[2].astype(F32)
    )
    gain1, shift1 = m.vecs[0:1, :], m.vecs[1:2, :]
    gain2, shift2 = m.vecs[5:6, :], m.vecs[6:7, :]
    o_bias, down_bias = m.vecs[4:5, :], m.vecs[7:8, :]

    def my_cols(row):
        whole = m.vecs[row:row + 1, :]
        value = whole[:, 0:HW]
        for u in range(1, 4):
            value = jnp.where(t == u, whole[:, HW * u:HW * u + HW], value)
        return value

    q_bias, v_bias = my_cols(2), my_cols(3)
    up_bias = m.vecs[8:9, :]
    for u in range(1, 4):
        up_bias = jnp.where(t == u, m.vecs[8 + u:9 + u, :], up_bias)

    def norm1(rows, _):
        center, scale = norm_stats(m.toka[rows, :].astype(F32))
        m.nrm[rows, :] = (center * scale * gain1 + shift1).astype(BF)

    blocks(8, 64, norm1)
    m.nrmt[...] = m.nrm[...].T
    gather_end(ag_do)
    m.dot_[...] = m.doa[...].T

    finish(ends1)
    w1 = m.w1[...].reshape(D, D)
    m.wosl[t] = w1[:, 3 * HW:]
    ag_wo = [
        send(m.wosl.at[t], m.wosl.at[t], dev(s, over, batch)),
        send(m.wosl.at[t], m.wosl.at[t], dev(s, sib, batch)),
    ]
    qkv = dot(m.nrm[...], w1)
    m.q[...] = ((qkv[:, 0:HW] + q_bias) * 0.125).astype(BF)
    m.kv[0, 0:SEG, :] = qkv[:, HW:2 * HW].astype(BF)
    m.kv[1, 0:SEG, :] = (qkv[:, 2 * HW:3 * HW] + v_bias).astype(BF)

    m.ssrc[0] = dot(pick, m.kv[0, 0:SEG, :]).astype(BF)
    m.ssrc[1] = dot(pick, m.kv[1, 0:SEG, :]).astype(BF)
    sum_at = take(16)

    def sum_copy(j):
        return pltpu.make_async_remote_copy(
            src_ref=m.ssrc,
            dst_ref=m.kv.at[:, pl.ds(pl.multiple_of(SEG + SLOT * s, SLOT), SLOT), :],
            send_sem=ss.at[sum_at + j], recv_sem=rs.at[sum_at + s],
            device_id=dev(j, t, batch), device_id_type=MESH,
        )

    for j in range(1, 16):
        @pl.when(j > s)
        def _(j=j):
            sum_copy(j).start()

    for h in range(HEADS):
        m.sloc[h] = dot_nt(of_head(m.q[...], h), m.kv[0, 0:SEG, :]) + m.bias[...]
    ag_wo[0].wait_recv()
    ag_wo.append(send(m.wosl.at[over], m.wosl.at[over], dev(s, sib, batch)))

    def sum_arrived(j):
        pltpu.make_async_remote_copy(
            src_ref=m.ssrc,
            dst_ref=m.kv.at[:, pl.ds(SEG + SLOT * j, SLOT), :],
            send_sem=ss.at[sum_at + j], recv_sem=rs.at[sum_at + j],
            device_id=dev(j, t, batch), device_id_type=MESH,
        ).wait_recv()

    for j in range(15):
        @pl.when(j < s)
        def _(j=j):
            sum_arrived(j)

    for h in range(HEADS):
        m.ssum[...] = dot_nt(of_head(m.q[...], h), m.kv[0, SEG:, :]) + sum_bias

        def soften(rows, _, h=h):
            local = m.sloc[h, rows, :]
            other = m.ssum[rows, :]
            peak = jnp.maximum(
                jnp.max(local, axis=-1, keepdims=True), jnp.max(other, axis=-1, keepdims=True)
            )
            local = jnp.exp(local - peak)
            other = jnp.exp(other - peak)
            total = jnp.sum(local, axis=-1, keepdims=True) + jnp.sum(other, axis=-1, keepdims=True)
            share = 1.0 / total
            m.prob[h, rows, 0:SEG] = (local * share).astype(BF)
            m.prob[h, rows, SEG:] = (other * share).astype(BF)

        blocks(16, 32, soften, unroll=2)
        part = dot(m.prob[h], of_head(m.kv[1], h))
        m.att[...] = part if h == 0 else m.att[...] + part
    m.atta[t] = m.att[...].astype(BF)
    ag_att = [
        send(m.atta.at[t], m.atta.at[t], dev(s, over, batch)),
        send(m.atta.at[t], m.atta.at[t], dev(s, sib, batch)),
    ]
    ag_wo[1].wait_recv()
    ag_wo[2].wait_recv()
    m.wof[...] = jnp.concatenate([m.wosl[0], m.wosl[1], m.wosl[2], m.wosl[3]], axis=1)
    finish(ends2)
    m.ga[...] = dot(m.doa[...], m.w2[:, :, :, D:].reshape(D, D))
    ag_att[0].wait_recv()
    ag_att.append(send(m.atta.at[over], m.atta.at[over], dev(s, sib, batch)))
    ag_att[1].wait_recv()
    ag_att[2].wait_recv()

    branch = dot(m.atta[0], m.wof[0:HW, :])
    for u in range(1, 4):
        branch = branch + dot(m.atta[u], m.wof[HW * u:HW * u + HW, :])
    m.hid[...] = m.toka[...].astype(F32) + branch + o_bias

    def norm2(rows, _):
        center, scale = norm_stats(m.hid[rows, :])
        m.nm[rows, :] = (center * scale * gain2 + shift2).astype(BF)

    blocks(8, 64, norm2)

    w_up = m.w2[:, :, :, 0:D].reshape(D, D)
    m.pre[...] = dot(m.nm[...], w_up) + up_bias

    def gelu(rows, _):
        a = m.pre[rows, :]
        square = a * a
        bend = jnp.tanh(0.7978845608028654 * (a + 0.044715 * (square * a)))
        half = 0.5 * (1.0 + bend)
        m.act[rows, :] = (a * half).astype(BF)
        slope = half + (0.5 * a) * (1.0 - bend * bend) * (
            0.7978845608028654 * (1.0 + 0.134145 * square)
        )
        m.gp[rows, :] = (m.ga[rows, :] * slope).astype(BF)

    blocks(16, 32, gelu)

    def scatter_start(name):
        src, r1 = getattr(m, name + "_s"), getattr(m, name + "_1")
        return [
            send(rows_of(src, diag), r1.at[1], dev(s, sib, batch)),
            send(rows_of(src, sib), r1.at[0], dev(s, sib, batch)),
        ]

    def scatter_pass(name, copies):
        src, r1 = getattr(m, name + "_s"), getattr(m, name + "_1")
        cross, r2 = getattr(m, name + "_x"), getattr(m, name + "_2")
        copies[0].wait_recv()
        cross[...] = (get_rows(src, over).astype(F32) + r1[1].astype(F32)).astype(BF)
        copies.append(send(cross, r2, dev(s, over, batch)))

    def scatter_end(name, copies):
        src, r1 = getattr(m, name + "_s"), getattr(m, name + "_1")
        r2 = getattr(m, name + "_2")
        copies[1].wait_recv()
        copies[2].wait_recv()
        return get_rows(src, t).astype(F32) + r1[0].astype(F32) + r2[...].astype(F32)

    m.rm_s[...] = dot_nt(m.gp[...], m.w2[:, :, :, 0:D].reshape(D, D)).astype(BF)
    rm = scatter_start("rm")
    m.nmt[...] = m.nm[...].T
    scatter_pass("rm", rm)
    m.g2[:, :, :, 0:D] = dot(m.nmt[...], m.gp[...]).astype(BF).reshape(4, 4, 48, D)
    m.g2[:, :, :, D:] = dot(m.dot_[...], m.act[...]).astype(BF).reshape(4, 4, 48, D)

    def reduce_start(g, tag, half):
        rza, rxb = getattr(m, "rza" + tag), getattr(m, "rxb" + tag)
        a_cols, b_cols = pl.ds(0, half), pl.ds(half, half)
        a = [
            send(g.at[(z + k) % 4, :, :, a_cols], rza.at[k - 1],
                 dev(4 * ((z + k) % 4) + x, t, batch))
            for k in (1, 3, 2)
        ]
        b = [
            send(g.at[:, (x + k) % 4, :, b_cols], rxb.at[k - 1],
                 dev(4 * z + (x + k) % 4, t, batch))
            for k in (1, 3, 2)
        ]
        return a, b

    def add4(own, got):
        return (
            own.astype(F32) + got[0].astype(F32) + got[1].astype(F32) + got[2].astype(F32)
        )

    def reduce_pass(g, tag, half, phase):
        a, b = phase
        rza, rxb = getattr(m, "rza" + tag), getattr(m, "rxb" + tag)
        rxa, rzb = getattr(m, "rxa" + tag), getattr(m, "rzb" + tag)
        ha, hb = getattr(m, "ha" + tag), getattr(m, "hb" + tag)
        finish(a)
        for k in range(4):
            ha[k] = add4(g[z, k, :, 0:half], [rza[j, k] for j in range(3)]).astype(BF)
        a2 = [
            send(ha.at[(x + k) % 4], rxa.at[k - 1], dev(4 * z + (x + k) % 4, t, batch))
            for k in (1, 3, 2)
        ]
        finish(b)
        for k in range(4):
            hb[k] = add4(g[k, x, :, half:], [rxb[j, k] for j in range(3)]).astype(BF)
        b2 = [
            send(hb.at[(z + k) % 4], rzb.at[k - 1], dev(4 * ((z + k) % 4) + x, t, batch))
            for k in (1, 3, 2)
        ]
        return a2 + b2

    row64 = iota((64, 48), 0)
    expand = (
        (iota((64, 48), 1) == row64 - 4 * (row64 // 16)) & (row64 % 16 < 12)
    ).astype(BF)

    def reduce_last(tag, half, phase):
        rxa, rzb = getattr(m, "rxa" + tag), getattr(m, "rzb" + tag)
        ha, hb = getattr(m, "ha" + tag), getattr(m, "hb" + tag)
        fx, fin = getattr(m, "fx" + tag), getattr(m, "fin" + tag)
        finish(phase)
        a = add4(ha[x], [rxa[j] for j in range(3)]).astype(BF)
        b = add4(hb[z], [rzb[j] for j in range(3)]).astype(BF)
        fx[:, :, 0:half] = dot(expand, a).astype(BF).reshape(4, 16, half)
        fx[:, :, half:] = dot(expand, b).astype(BF).reshape(4, 16, half)
        mine = 4 * batch + t
        copies = [
            send(fx.at[u], fin.at[mine], dev(s, u, 1 - batch)) for u in (over, diag, sib, t)
        ]
        copies += [send(fx.at[u], fin.at[mine], dev(s, u, batch)) for u in group]
        fin[mine] = fx[t]
        return copies

    rg2 = reduce_start(m.g2, "2", D)
    m.ro_s[...] = dot_nt(m.act[...], m.w2[:, :, :, D:].reshape(D, D)).astype(BF)

    m.gm[...] = scatter_end("rm", rm)
    own = t * ROWS
    zero_row = jnp.zeros((1, D), F32)

    def norm_back(values, grads, gain):
        center, scale = norm_stats(values)
        unit = center * scale
        inner = grads * gain
        return (
            scale * (
                inner
                - jnp.mean(inner, axis=-1, keepdims=True)
                - unit * jnp.mean(inner * unit, axis=-1, keepdims=True)
            ),
            jnp.sum(grads * unit, axis=0, keepdims=True),
            jnp.sum(grads, axis=0, keepdims=True),
        )

    g_gain2, g_shift2, g_obias, g_dbias = zero_row, zero_row, zero_row, zero_row
    for k in range(2):
        at = pl.ds(pl.multiple_of(own + 64 * k, 64), 64)
        here = slice(64 * k, 64 * k + 64)
        into, d_gain, d_shift = norm_back(m.hid[at, :], m.gm[here, :], gain2)
        cot = dout[here, :].astype(F32)
        into = into + cot
        m.gh[here, :] = into
        low = into.astype(BF)
        m.gbr[here, :] = low
        g_gain2 += d_gain
        g_shift2 += d_shift
        g_obias += jnp.sum(low.astype(F32), axis=0, keepdims=True)
        g_dbias += jnp.sum(cot, axis=0, keepdims=True)
    for u in range(4):
        m.sa[u] = dot_nt(m.gbr[...], m.wof[HW * u:HW * u + HW, :]).astype(BF)
    aa = [send(m.sa.at[u], m.do.at[t], dev(s, u, batch)) for u in group]
    m.do[t] = m.sa[t]
    for u in range(4):
        m.sb[u] = m.gbr[:, HW * u:HW * u + HW]
    ab = [send(m.sb.at[u], m.gba.at[t], dev(s, u, batch)) for u in group]
    m.gba[t] = m.sb[t]
    ro = scatter_start("ro")
    for u in range(4):
        m.attt[HW * u:HW * u + HW, :] = m.atta[u].T
    qt = m.q[...].T
    scatter_pass("ro", ro)
    ends_g2 = reduce_pass(m.g2, "2", D, rg2)
    finish(aa)

    do_all = m.do[...].reshape(SEG, HW)
    dot_t = do_all.T
    weighed = do_all.astype(F32) * m.att[...]
    delta = [jnp.sum(of_head(weighed, h), axis=-1, keepdims=True) for h in range(HEADS)]
    m.dq[...] = jnp.zeros((SEG, HW), F32)
    delta_of = jnp.concatenate(delta, axis=1)
    m.att[:, 0:HEADS] = delta_of

    for h in range(HEADS):
        d_head = of_head(do_all, h)
        m.ssum[...] = dot_nt(d_head, m.kv[1, SEG:, :])

        def back_sum(rows, _, h=h):
            w = m.prob[h, rows, SEG:].astype(F32)
            m.ds[rows, :] = (w * (m.ssum[rows, :] - m.att[rows, h:h + 1])).astype(BF)

        blocks(16, 32, back_sum, unroll=2)
        m.dq[...] += dot(m.ds[...], of_head(m.kv[0, SEG:, :], h))
        feat = slice(64 * h, 64 * h + 64)
        m.dkst[feat, :] = dot(qt[feat, :], m.ds[...])
        m.dvst[feat, :] = dot(dot_t[feat, :], m.prob[h, :, SEG:])
    m.dkvs[0] = m.dkst[...].T.astype(BF)
    m.dkvs[1] = m.dvst[...].T.astype(BF)
    grad_at = take(16)

    def grad_copy(j):
        return pltpu.make_async_remote_copy(
            src_ref=m.dkvs.at[:, pl.ds(SLOT * j, SLOT), :],
            dst_ref=m.sumg.at[s],
            send_sem=ss.at[grad_at + j], recv_sem=rs.at[grad_at + s],
            device_id=dev(j, t, batch), device_id_type=MESH,
        )

    for j in range(15):
        @pl.when(j < s)
        def _(j=j):
            grad_copy(j).start()

    for h in range(HEADS):
        m.sloc[h] = dot_nt(of_head(do_all, h), m.kv[1, 0:SEG, :])
    for h in range(HEADS):
        def back_own(rows, _, h=h):
            w = m.prob[h, rows, 0:SEG].astype(F32)
            m.ds[rows, 0:SEG] = (w * (m.sloc[h, rows, :] - m.att[rows, h:h + 1])).astype(BF)

        blocks(8, 64, back_own, unroll=2)
        score_grads = m.ds[:, 0:SEG]
        m.dq[...] += dot(score_grads, of_head(m.kv[0, 0:SEG, :], h))
        feat = slice(64 * h, 64 * h + 64)
        m.dkt[feat, :] = dot(qt[feat, :], score_grads)
        m.dvt[feat, :] = dot(dot_t[feat, :], m.prob[h, :, 0:SEG])
    fin_g2 = reduce_last("2", D, ends_g2)
    finish(ab)
    grad_out_cols = m.gba[...].reshape(SEG, HW)
    g_o = dot(m.attt[...], grad_out_cols)

    for j in range(1, 16):
        @pl.when(j > s)
        def _(j=j):
            pltpu.make_async_remote_copy(
                src_ref=m.dkvs.at[:, pl.ds(0, SLOT), :],
                dst_ref=m.sumg.at[j],
                send_sem=ss.at[grad_at + j], recv_sem=rs.at[grad_at + j],
                device_id=dev(j, t, batch), device_id_type=MESH,
            ).wait_recv()

    def returned(which):
        total = m.sumg[0, which].astype(F32)
        for j in range(1, SLOTS):
            total = total + m.sumg[j, which].astype(F32)
        high = total.astype(BF)
        rest = (total - high.astype(F32)).astype(BF)
        return dot_tn(high, pick) + dot_tn(rest, pick)

    dk = (m.dkt[...] + returned(0)).T.astype(BF)
    dv = (m.dvt[...] + returned(1)).T.astype(BF)
    dq = m.dq[...].astype(BF) * jnp.asarray(0.125, BF)
    m.dqkv[...] = jnp.concatenate([dq, dk, dv], axis=1)

    m.rn_s[...] = dot_nt(m.dqkv[...], m.w1[...].reshape(D, D)[:, 0:3 * HW]).astype(BF)
    rn = scatter_start("rn")
    g_qkv = dot(m.nrmt[...], m.dqkv[...])
    m.g1[...] = jnp.concatenate([g_qkv, g_o], axis=1).astype(BF).reshape(4, 4, 48, D)
    rg1 = reduce_start(m.g1, "1", D // 2)
    scatter_pass("rn", rn)
    out_o[...] = (
        scatter_end("ro", ro) + get_rows(m.hid, t) + down_bias
    ).astype(BF)
    g_qb = jnp.sum(dq.astype(F32), axis=0, keepdims=True)
    g_vb = jnp.sum(dv.astype(F32), axis=0, keepdims=True)
    g_ub = zero_row
    for k in range(4):
        g_ub += jnp.sum(m.gp[ROWS * k:ROWS * k + ROWS, :].astype(F32), axis=0, keepdims=True)

    def in_place(row):
        none = jnp.zeros((1, HW), F32)
        return jnp.concatenate([jnp.where(t == u, row, none) for u in range(4)], axis=1)

    g_qb, g_vb = in_place(g_qb), in_place(g_vb)
    m.gm[...] = scatter_end("rn", rn)
    g_gain1, g_shift1 = zero_row, zero_row
    for k in range(2):
        here = slice(64 * k, 64 * k + 64)
        into, d_gain, d_shift = norm_back(tok[here, :].astype(F32), m.gm[here, :], gain1)
        gtok_o[here, :] = into + m.gh[here, :]
        g_gain1 += d_gain
        g_shift1 += d_shift
    rows8 = (g_gain1, g_shift1, g_qb, g_vb, g_obias, g_gain2, g_shift2, g_dbias)
    m.vgr[...] = jnp.zeros((16, D), F32)
    for k, row in enumerate(rows8):
        m.vgr[k:k + 1, :] = row
    for u in range(4):
        m.vgr[8 + u:9 + u, :] = jnp.where(t == u, g_ub, zero_row)
    vgx = [
        send(m.vgr, m.vgx.at[k - 1], dev(4 * z + (x + k) % 4, t, batch)) for k in (1, 2, 3)
    ]
    ends_g1 = reduce_pass(m.g1, "1", D // 2, rg1)
    finish(vgx)
    m.vgs[...] = add4(m.vgr[...], [m.vgx[j] for j in range(3)])
    vgz = [
        send(m.vgs, m.vgz.at[k - 1], dev(4 * ((z + k) % 4) + x, t, batch)) for k in (1, 2, 3)
    ]
    fin_g1 = reduce_last("1", D // 2, ends_g1)
    finish(vgz)
    m.vgt[...] = add4(m.vgs[...], [m.vgz[j] for j in range(3)])
    mine = 4 * batch + t
    fin_v = [send(m.vgt, m.vfin.at[mine], dev(s, u, 1 - batch)) for u in (over, diag, sib, t)]
    fin_v += [send(m.vgt, m.vfin.at[mine], dev(s, u, batch)) for u in group]
    m.vfin[mine] = m.vgt[...]

    def both(fin, u, cols):
        return fin[u, 0:12, cols].astype(F32) + fin[4 + u, 0:12, cols].astype(F32)

    finish(fin_g2)
    for u in range(4):
        wide = slice(D * u, D * u + D)
        gu_o[:, wide] = both(m.fin2, u, slice(0, D))
        gd_o[:, wide] = both(m.fin2, u, slice(D, 2 * D))
    finish(fin_g1)
    parts = [both(m.fin1, u, slice(0, D)) for u in range(4)]
    for k, ref in enumerate((gq_o, gk_o, gv_o, go_o)):
        ref[...] = jnp.concatenate([p[:, HW * k:HW * k + HW] for p in parts], axis=1)
    finish(fin_v)
    total = m.vfin[0]
    for k in range(1, 8):
        total = total + m.vfin[k]
    back = iota((D, 128), 0) - iota((D, 128), 1)
    lane = iota((D, 128), 1)
    get_12 = ((back == 12 * place) & (lane < 12)).astype(F32)
    get_48 = ((back == 48 * (place % 16)) & (lane < 48)).astype(F32)
    small = dot(total, get_12, precision=HIGHEST)
    large = dot(total, get_48, precision=HIGHEST)
    row16 = iota((16, 128), 0)
    chosen = jnp.sum(jnp.where(row16 == 8 + z, large, 0.0), axis=0, keepdims=True)
    gvec_o[...] = jnp.where(row16 < 8, small, jnp.where(row16 == 8, chosen, 0.0))

    for copy in sent:
        copy.wait_send()
    for j in range(1, 16):
        @pl.when(j > s)
        def _(j=j):
            sum_copy(j).wait_send()
    for j in range(15):
        @pl.when(j < s)
        def _(j=j):
            grad_copy(j).wait_send()
    assert used[0] <= COPIES, used[0]


def body(
    tokens, seg_lengths, ln1_gain, ln1_bias, w_query, q_bias, w_key, w_value, v_bias,
    w_out, o_bias, ln2_gain, ln2_bias, w_up, up_bias, w_down, down_bias, d_out,
):
    narrow = jnp.stack(
        [ln1_gain, ln1_bias, q_bias, v_bias, o_bias, ln2_gain, ln2_bias, down_bias]
    )
    vec = jnp.zeros((16, 128), BF)
    vec = vec.at[0:8, 0:12].set(narrow).at[8, 0:48].set(up_bias)
    shape = jax.ShapeDtypeStruct
    vmem = pl.BlockSpec(memory_space=pltpu.VMEM)
    outs = pl.pallas_call(
        layer_kernel,
        out_shape=[
            shape((ROWS, D), BF),
            shape((ROWS, D), F32),
            shape((12, D), F32),
            shape((12, D), F32),
            shape((12, D), F32),
            shape((12, D), F32),
            shape((12, 4 * D), F32),
            shape((12, 4 * D), F32),
            shape((16, 128), F32),
        ],
        in_specs=[pl.BlockSpec(memory_space=pltpu.SMEM)] + [vmem] * 9,
        out_specs=[vmem] * 9,
        scratch_shapes=[pltpu.VMEM(dims, kind) for dims, kind in SCRATCH.values()]
        + [pltpu.SemaphoreType.DMA((COPIES,)), pltpu.SemaphoreType.DMA((COPIES,))],
        compiler_params=pltpu.CompilerParams(
            collective_id=0, has_side_effects=True, vmem_limit_bytes=62 * 2**20
        ),
        name="layer",
    )(
        seg_lengths, tokens[0], d_out[0], w_query, w_key, w_value, w_out, w_up, w_down, vec
    )
    out, g_tok, g_q, g_k, g_v, g_o, g_up, g_down, g_vec = outs
    return (
        out[None],
        g_tok[None],
        g_vec[0, 0:12],
        g_vec[1, 0:12],
        g_q,
        g_vec[2, 0:12],
        g_k,
        g_v,
        g_vec[3, 0:12],
        g_o,
        g_vec[4, 0:12],
        g_vec[5, 0:12],
        g_vec[6, 0:12],
        g_up,
        g_vec[8, 0:48],
        g_down,
        g_vec[7, 0:12],
    )


def solution(mesh):
    rows, cols = P("batch", "seq", None), P("seq", None)
    one = P("seq")
    placed = (
        rows, P("batch", None), one, one, cols, one, cols, cols, one,
        cols, one, one, one, cols, one, cols, one, rows,
    )
    return jax.shard_map(
        body,
        mesh=mesh,
        in_specs=placed,
        out_specs=(
            rows, rows, one, one, cols, one, cols, cols, one,
            cols, one, one, one, cols, one, cols, one,
        ),
        check_vma=False,
    )
```

time: 2340 us -> 163 us (0.07)
  waiting for transfers between devices: 1010 us -> 0 us
  blocking collectives: 953 us -> 0 us
  Pallas kernels: 0 us -> 150 us
  local copies, waits for them, and re-layouts: 145 us -> 11.5 us
  starting transfers between devices: 96.6 us -> 0 us
  matrix products: 62.5 us -> 0 us
  other arithmetic: 33.4 us -> 0 us
    unnamed x3 -> x0, blocking collectives: 947 us -> none
    psum x2 -> x0, waiting for transfers between devices: 547 us -> none  [the longest x1 510 us: body(): summary_total = lax.psum(summary_part, 'seq')]
    all_gather x7 -> x0, waiting for transfers between devices: 428 us -> none  [the longest x1 110 us: body(): gathered = lax.all_gather(window_rows, 'seq', axis=0, tiled=True)]
    pallas_call x0 -> x1, Pallas kernels: none -> 150 us  [body(): pl.pallas_call(layer_kernel, out_shape=[shape((ROWS, D), BF), shape((ROWS...]
    unnamed x172 -> x42, local copies, waits for them, and re-layouts: 121 us -> 8.71 us
    unnamed x16 -> x0, starting transfers between devices: 64.3 us -> none
    dot_general x39 -> x0, matrix products: 62.5 us -> none  [the longest x6 18.4 us: contract_first(): lax.dot_general(left_rows, right_rows, (((0,), (0,)), ((), ())), preferre...]
    ppermute x10 -> x0, starting transfers between devices: 31.9 us -> none  [the longest x6 17.9 us: shifted(): return lax.ppermute(block, axis, route)]
  transfers between devices with their start and end apart: 35 -> 0, of which waited for: 17 -> 0; matrix products, arithmetic and copies ran while one was open for 3% -> 0% of each run, Pallas kernels for 0% -> 0%
where the time goes in v1:
time: 163 us
  Pallas kernels  150 us (92%)
  local copies, waits for them, and re-layouts  11.5 us (7%)
    pallas_call x1, Pallas kernels, body(): pl.pallas_call(layer_kernel, out_shape=[shape((ROWS, D), BF), shape((ROWS...  150 us
    unnamed x42, local copies, waits for them, and re-layouts  8.71 us

profile of v1, /device:TPU:1, one launch (start us, length us, event | category | flops | bytes accessed | tf_op | source)
XLA Modules:
  0.0 162.7 jit_solution(9002765103023768828)
XLA Ops:
  0.7 0.0 copy-start.15
  0.7 0.0 copy-start.11
  0.7 0.0 copy-start.12
  0.7 0.0 copy-start.13
  0.7 0.0 copy-start.14
  0.7 0.0 copy-start.8
  0.7 0.0 copy-start.9
  0.7 0.0 copy-start.10
  0.7 0.6 copy-done.15
  1.3 0.0 copy-done.11
  1.3 0.0 copy-done.12
  1.3 0.0 copy-done.13
  1.4 0.0 copy-done.14
  1.4 0.0 copy-done.8
  1.4 0.0 copy-done.9
  1.4 0.0 copy-done.10
  1.5 0.0 copy-start.16
  1.5 0.6 copy-done.16
  2.1 0.1 scatter.9.vec
  2.2 0.0 copy-start.7
  2.2 0.6 copy-done.7
  2.8 150.4 %layer.1 = (bf16[128,768]{1,0:T(8,128)(2,1)}, f32[128,768]{1,0:T(8,128)}, f32[12,768]{1,0:T(8,128)}, f32[12,768]{1,0:T(8,128)}, f32[12,768]{1,0:T(8,128)}, /*ind...) custom-call(s32[1,16]{1,0:T(1,128)} %seg_ref.1, bf16[128,768]{1,0:T(8,128)(2,1)} %bitcast.33, ...), custom_call_target="tpu_custom_call" | custom-call | tf_op jit(solution)/shard_map/layer/pallas_call | solution.py:801
  153.2 0.0 copy-start
  153.2 1.5 slice_bitcast_fusion
  154.7 1.2 slice_bitcast_fusion.1
  155.9 1.6 copy.44
  157.5 0.0 copy-done
  157.5 0.0 copy-start.6
  157.5 0.0 copy-start.5
  157.5 0.0 copy-start.4
  157.5 0.7 copy.45
  158.2 0.0 copy-done.6
  158.3 0.0 copy-start.2
  158.3 0.6 copy.46
  158.9 0.0 copy-done.5
  158.9 0.6 copy.47
  159.5 0.0 copy-done.4
  159.5 0.0 copy-start.3
  159.5 0.6 copy.48
  160.2 0.2 copy-done.3
  160.4 0.6 copy.49
  161.0 0.0 copy-done.2
  161.0 0.0 copy-start.1
  161.0 0.7 copy.50
  161.7 0.3 copy-done.1
  162.0 0.7 copy.51
  (2 shorter events, 0.0 us)
Async XLA Ops:
  0.7 0.7 copy-start.15
  0.7 0.7 copy-start.11
  0.7 0.7 copy-start.12
  0.7 0.7 copy-start.13
  0.7 0.7 copy-start.14
  0.7 0.7 copy-start.8
  0.7 0.7 copy-start.9
  0.7 0.7 copy-start.10
  1.5 0.7 copy-start.16
  2.2 0.6 copy-start.7
  153.2 4.3 %copy-start = (f32[128,768]{1,0:T(8,128)S(1)}, f32[128,768]{1,0:T(8,128)}, u32[]{:S(2)}) copy-start(f32[128,768]{1,0:T(8,128)} %get-tuple-element.51) | copy-start | bytes 1179652
  157.5 0.8 copy-start.6
  157.5 1.4 copy-start.5
  157.5 2.0 %copy-start.4 = (f32[12,768]{1,0:T(8,128)S(1)}, f32[12,768]{1,0:T(8,128)}, u32[]{:S(2)}) copy-start(f32[12,768]{1,0:T(8,128)} %get-tuple-element.91) | copy-start | bytes 110596
  158.3 2.7 %copy-start.2 = (f32[12,3072]{1,0:T(8,128)S(1)}, f32[12,3072]{1,0:T(8,128)}, u32[]{:S(2)}) copy-start(f32[12,3072]{1,0:T(8,128)} %get-tuple-element.97) | copy-start | bytes 442372
  159.5 0.8 copy-start.3
  161.0 1.0 copy-start.1

commit v2 on v1

v2 whole, which is shorter than its diff:
```python
import functools
import types

import jax
import jax.numpy as jnp
from jax import lax
from jax.experimental import pallas as pl
from jax.experimental.pallas import tpu as pltpu
from jax.sharding import PartitionSpec as P

BF = jnp.bfloat16
F32 = jnp.float32
MESH = pl.DeviceIdType.MESH
EPSILON = 1e-05
MASKED = -1e30
HIGHEST = lax.Precision.HIGHEST

ROWS = 128
SEG = 512
D = 768
HW = 192
HEADS = 3
HALF = 64
CHUNK = 256
SUMMARY = 50
SLOT = 64
SLOTS = 16
SUMS = SLOTS * SLOT


def dot(a, b, **kw):
    return jnp.dot(a, b, preferred_element_type=F32, **kw)


def dot_nt(a, b):
    return lax.dot_general(a, b, (((1,), (1,)), ((), ())), preferred_element_type=F32)


def dot_tn(a, b):
    return lax.dot_general(a, b, (((0,), (0,)), ((), ())), preferred_element_type=F32)


def iota(shape, dim):
    return lax.broadcasted_iota(jnp.int32, shape, dim)


def norm_stats(values):
    center = values - jnp.mean(values, axis=-1, keepdims=True)
    spread = jnp.mean(center * center, axis=-1, keepdims=True)
    return center, lax.rsqrt(spread + EPSILON)


SCRATCH = dict(
    pk1=((4, 16, D), BF),
    pk2=((4, 16, 2 * D), BF),
    p01=((4, 16, D), BF),
    p02=((4, 16, 2 * D), BF),
    w1=((4, 4, 48, D), BF),
    w2=((4, 4, 48, 2 * D), BF),
    wosl=((4, D, HW), BF),
    wof=((D, D), BF),
    vin=((16, 128), F32),
    vb=((16, D), BF),
    vg=((3, 16, D), BF),
    vs1=((16, D), BF),
    vx=((3, 16, D), BF),
    vs2=((16, D), BF),
    vz=((3, 16, D), BF),
    vecs=((16, D), F32),
    toka=((SEG, D), BF),
    doa=((SEG, D), BF),
    nrm=((SEG, D), BF),
    nrmt=((D, SEG), BF),
    dot_=((D, SEG), BF),
    stat=((SEG, 128), F32),
    bias=((SEG, SEG), F32),
    q=((SEG, HW), BF),
    kv=((2, SEG, HW), BF),
    kvs=((2, SUMS, HW), BF),
    ssrc=((2, SLOT, HW), BF),
    sloc=((HEADS, SEG, SEG), F32),
    ssum=((SEG, SUMS), F32),
    prob1=((HEADS, SEG, SEG), BF),
    prob2=((HEADS, SEG, SUMS), BF),
    m1=((SEG, 128), F32),
    l1=((SEG, 128), F32),
    m2=((SEG, 128), F32),
    l2=((SEG, 128), F32),
    a1=((SEG, 128), F32),
    a2=((SEG, 128), F32),
    delta=((SEG, 128), F32),
    a1x=((SEG, HW), F32),
    a2x=((SEG, HW), F32),
    o1=((SEG, HW), F32),
    att=((SEG, HW), F32),
    atta=((4, SEG, HW), BF),
    attt=((D, SEG), BF),
    hid=((SEG, D), F32),
    nm=((SEG, D), BF),
    nmt=((D, SEG), BF),
    pre=((SEG, D), F32),
    ga=((SEG, D), F32),
    act=((SEG, D), BF),
    gp=((SEG, D), BF),
    rm_s=((SEG, D), BF),
    rm_1=((2, 2, HALF, D), BF),
    rm_x=((2, HALF, D), BF),
    rm_2=((2, HALF, D), BF),
    ro_s=((SEG, D), BF),
    ro_1=((2, 2, HALF, D), BF),
    ro_x=((2, HALF, D), BF),
    ro_2=((2, HALF, D), BF),
    rn_s=((SEG, D), BF),
    rn_1=((2, 2, HALF, D), BF),
    rn_x=((2, HALF, D), BF),
    rn_2=((2, HALF, D), BF),
    gh=((ROWS, D), F32),
    gbr=((ROWS, D), BF),
    sa=((2, 4, HALF, HW), BF),
    sb=((2, 4, HALF, HW), BF),
    do=((2, 4, HALF, HW), BF),
    gba=((2, 4, HALF, HW), BF),
    ds=((SEG, SUMS), BF),
    dq=((SEG, HW), F32),
    dkt=((HW, SEG), F32),
    dvt=((HW, SEG), F32),
    dkst=((HW, SUMS), F32),
    dvst=((HW, SUMS), F32),
    dkvs=((2, SUMS, HW), BF),
    sumg=((SLOTS, 2, SLOT, HW), BF),
    dqkv=((SEG, 3 * HW), BF),
    g1=((4, 4, 48, D), BF),
    g2=((4, 4, 48, 2 * D), BF),
    rza1=((3, 4, 48, D // 2), BF),
    rxa1=((3, 48, D // 2), BF),
    rxb1=((3, 4, 48, D // 2), BF),
    rzb1=((3, 48, D // 2), BF),
    ha1=((4, 48, D // 2), BF),
    hb1=((4, 48, D // 2), BF),
    rza2=((3, 4, 48, D), BF),
    rxa2=((3, 48, D), BF),
    rxb2=((3, 4, 48, D), BF),
    rzb2=((3, 48, D), BF),
    ha2=((4, 48, D), BF),
    hb2=((4, 48, D), BF),
    fx1=((4, 16, D), BF),
    fx2=((4, 16, 2 * D), BF),
    fin1=((8, 16, D), BF),
    fin2=((8, 16, 2 * D), BF),
    vgr=((16, D), F32),
    vgx=((3, 16, D), F32),
    vgs=((16, D), F32),
    vgz=((3, 16, D), F32),
    vgt=((16, D), F32),
    vfin=((8, 16, D), F32),
)
SENDS = 24
RECVS = 100


class Flight:
    def __init__(self, waiter):
        self.waiter = waiter
        self.arrived = False
        self.left = False

    def wait_recv(self):
        if not self.arrived:
            self.waiter.wait_recv()
        self.arrived = True

    def wait_send(self):
        if not self.left:
            self.waiter.wait_send()
        self.left = True


def layer_kernel(
    seg_ref, tok, dout, wq, wk, wv, wo, wu, wd, *refs,
):
    vectors, refs = refs[:9], refs[9:]
    out_o, gtok_o, gq_o, gk_o, gv_o, go_o, gu_o, gd_o, gvec_o = refs[:9]
    scratch = refs[9:]
    m = types.SimpleNamespace(**dict(zip(SCRATCH, scratch[:-3])))
    ss, rs, sum_ss = scratch[-3:]
    batch = lax.axis_index("batch")
    place = lax.axis_index("seq")
    s = place // 4
    t = place % 4
    z = s // 4
    x = s % 4
    sib = t + 1 - 2 * (t % 2)
    over = (t + 2) % 4
    diag = 3 - t
    group = (over, diag, sib)

    def dev(seg, tt, bb):
        return (4 * seg + tt, bb)

    def here(tt):
        return dev(s, tt, batch)

    def along_x(k):
        return dev(4 * z + (x + k) % 4, t, batch)

    def along_z(k):
        return dev(4 * ((z + k) % 4) + x, t, batch)

    used = [0]
    sent = []

    def take(n=1):
        first = used[0]
        used[0] += n
        return first

    def fly(copies, total=None):
        k = len(sent)
        if k >= SENDS:
            sent[k - SENDS].wait_send()
        send_sem, recv_sem = ss.at[k % SENDS], rs.at[take()]
        for src, dst, device in copies:
            copy = pltpu.make_async_remote_copy(
                src_ref=src, dst_ref=dst, send_sem=send_sem, recv_sem=recv_sem,
                device_id=device, device_id_type=MESH,
            )
            copy.start()
        if total is not None:
            copy = pltpu.make_async_remote_copy(
                src_ref=total, dst_ref=total, send_sem=send_sem, recv_sem=recv_sem,
                device_id=device, device_id_type=MESH,
            )
        flight = Flight(copy)
        sent.append(flight)
        return flight

    def block(c, k):
        return pl.ds(pl.multiple_of(CHUNK * c + HALF * k, HALF), HALF)

    def loop(first, count, size, fn, unroll=1):
        def step(j, carry):
            fn(pl.ds(pl.multiple_of(first + j * size, size), size))
            return carry

        lax.fori_loop(0, count, step, 0, unroll=unroll)

    m.kvs[...] = jnp.zeros((2, SUMS, HW), BF)
    m.sumg[...] = jnp.zeros((SLOTS, 2, SLOT, HW), BF)
    barrier = pltpu.get_barrier_semaphore()
    partners = [here(u) for u in group]
    partners += [dev((s + k) % 16, t, batch) for k in range(1, 16)]
    partners += [dev(s, u, 1 - batch) for u in (t, sib, over, diag)]
    for partner in partners:
        pl.semaphore_signal(barrier, inc=1, device_id=partner, device_id_type=MESH)
    m.pk1[...] = jnp.zeros((4, 16, D), BF)
    for u in range(4):
        cols = slice(HW * u, HW * u + HW)
        m.pk1[u, 0:12, :] = jnp.concatenate(
            [wq[:, cols], wk[:, cols], wv[:, cols], wo[:, cols]], axis=1
        )
    m.vin[...] = jnp.zeros((16, 128), F32)
    for k, ref in enumerate(vectors[:8]):
        m.vin[k:k + 1, 0:12] = ref[...].astype(F32)
    m.vin[8:9, 0:48] = vectors[8][...].astype(F32)
    shift = iota((128, D), 1) - iota((128, D), 0)
    narrow = dot(m.vin[...].astype(BF), (shift == 12 * place).astype(BF))
    wider = dot(m.vin[...].astype(BF), (shift == 48 * (place % 16)).astype(BF))
    vec_row = iota((16, D), 0)
    m.vb[...] = jnp.where(
        vec_row < 8, narrow, jnp.where(vec_row == 8 + z, wider[8:9, :], 0.0)
    ).astype(BF)
    pl.semaphore_wait(barrier, len(partners))

    first1 = fly([(m.pk1.at[u], m.p01.at[t], here(u)) for u in group], m.p01.at[0:3])
    firstv = fly(
        [(m.vb, m.vg.at[k], here(u)) for k, u in enumerate((sib, over, diag))], m.vg
    )
    m.p01[t] = m.pk1[t]
    m.pk2[...] = jnp.zeros((4, 16, 2 * D), BF)
    for u in range(4):
        wide = slice(D * u, D * u + D)
        m.pk2[u, 0:12, 0:D] = wu[:, wide]
        m.pk2[u, 0:12, D:] = wd[:, wide]
    m.p02[t] = m.pk2[t]
    for c in range(2):
        m.toka[block(c, t), :] = tok[HALF * c:HALF * c + HALF, :]
        m.doa[block(c, t), :] = dout[HALF * c:HALF * c + HALF, :]

    def gather_start(ref):
        moves = [
            fly([(ref.at[block(c, t)], ref.at[block(c, t)], here(u)) for c in (0, 1)],
                ref.at[0:ROWS])
            for u in (over, sib)
        ]
        return moves

    def gather_pass(moves, ref):
        moves[0].wait_recv()
        moves.append(
            fly([(ref.at[block(c, over)], ref.at[block(c, over)], here(sib)) for c in (0, 1)],
                ref.at[0:ROWS])
        )

    def finish(moves):
        for move in moves:
            move.wait_recv()

    row48 = iota((48, 64), 0)
    owner48 = (
        (row48 >= 12).astype(jnp.int32)
        + (row48 >= 24).astype(jnp.int32)
        + (row48 >= 36).astype(jnp.int32)
    )
    squeeze = (iota((48, 64), 1) == row48 + 4 * owner48).astype(BF)

    def spread_start(w, half):
        a, b = pl.ds(0, half), pl.ds(half, half)
        mine_a, mine_b = w.at[z, x, :, a], w.at[z, x, :, b]
        return (
            fly([(mine_a, mine_a, along_x(k)) for k in (1, 3, 2)], w.at[0, 0:3, :, a]),
            fly([(mine_b, mine_b, along_z(k)) for k in (1, 3, 2)], w.at[0, 0:3, :, b]),
        )

    def spread_pass(w, half, moves):
        a, b = pl.ds(0, half), pl.ds(half, half)
        plane_a, plane_b = w.at[z, :, :, a], w.at[:, x, :, b]
        moves[0].wait_recv()
        a2 = fly([(plane_a, plane_a, along_z(k)) for k in (1, 3, 2)], w.at[0:3, :, :, a])
        moves[1].wait_recv()
        b2 = fly([(plane_b, plane_b, along_x(k)) for k in (1, 3, 2)], w.at[0:3, :, :, b])
        return a2, b2

    first1.wait_recv()
    m.w1[z, x] = dot(squeeze, m.p01[...].reshape(64, D)).astype(BF)
    phase1 = spread_start(m.w1, D // 2)
    first2 = fly([(m.pk2.at[u], m.p02.at[t], here(u)) for u in group], m.p02.at[0:3])
    ag_tok = gather_start(m.toka)

    seg_len = seg_ref[0, s]

    def token_of(rows):
        return rows + 64 * ((rows % CHUNK) // HALF) - 192 * (rows // CHUNK)

    k_pos = token_of(iota((1, SEG), 1))

    def mask(rows):
        mine = token_of(rows.start + iota((ROWS, 1), 0))
        ok = ((k_pos <= mine) & (k_pos < seg_len)) | (k_pos == mine)
        m.bias[rows, :] = jnp.where(ok, 0.0, MASKED)

    loop(0, 4, ROWS, mask)
    s_col = iota((8, SUMS), 1)
    sum_bias = jnp.where((s_col < SLOT * s) & (s_col % SLOT < SUMMARY), 0.0, MASKED)[0:1, :]
    pick_row = iota((SLOT, SEG), 0)
    pick = ((k_pos == seg_len - SUMMARY + pick_row) & (pick_row < SUMMARY)).astype(BF)
    lane_head = iota((1, HW), 1) // 64

    def of_head(value, h):
        return jnp.where(lane_head == h, value, jnp.zeros_like(value))

    def by_head(cols):
        return jnp.where(
            lane_head == 0, cols[:, 0:1], jnp.where(lane_head == 1, cols[:, 1:2], cols[:, 2:3])
        )

    def add4(own, got):
        return own.astype(F32) + got[0].astype(F32) + got[1].astype(F32) + got[2].astype(F32)

    firstv.wait_recv()
    m.vs1[...] = add4(m.vb[...], m.vg).astype(BF)
    vx = fly([(m.vs1, m.vx.at[k - 1], along_x(k)) for k in (1, 2, 3)], m.vx)
    ends1 = spread_pass(m.w1, D // 2, phase1)
    vx.wait_recv()
    m.vs2[...] = add4(m.vs1[...], m.vx).astype(BF)
    vz = fly([(m.vs2, m.vz.at[k - 1], along_z(k)) for k in (1, 2, 3)], m.vz)
    first2.wait_recv()
    m.w2[z, x] = dot(squeeze, m.p02[...].reshape(64, 2 * D)).astype(BF)
    gather_pass(ag_tok, m.toka)
    vz.wait_recv()
    m.vecs[...] = add4(m.vs2[...], m.vz)
    gain1, shift1 = m.vecs[0:1, :], m.vecs[1:2, :]
    gain2, shift2 = m.vecs[5:6, :], m.vecs[6:7, :]
    o_bias, down_bias = m.vecs[4:5, :], m.vecs[7:8, :]

    def my_cols(row):
        whole = m.vecs[row:row + 1, :]
        value = whole[:, 0:HW]
        for u in range(1, 4):
            value = jnp.where(t == u, whole[:, HW * u:HW * u + HW], value)
        return value

    q_bias, v_bias = my_cols(2), my_cols(3)
    up_bias = m.vecs[8:9, :]
    for u in range(1, 4):
        up_bias = jnp.where(t == u, m.vecs[8 + u:9 + u, :], up_bias)

    finish(ag_tok)

    def norm1(rows):
        values = m.toka[rows, :].astype(F32)
        mean = jnp.mean(values, axis=-1, keepdims=True)
        center = values - mean
        scale = lax.rsqrt(jnp.mean(center * center, axis=-1, keepdims=True) + EPSILON)
        m.nrm[rows, :] = (center * scale * gain1 + shift1).astype(BF)
        m.stat[rows, 0:1] = mean
        m.stat[rows, 1:2] = scale

    loop(0, 4, ROWS, norm1)
    m.nrmt[...] = m.nrm[...].T

    finish(ends1)
    phase2 = spread_start(m.w2, D)
    w1 = m.w1[...].reshape(D, D)
    qkv = dot(m.nrm[...], w1)
    m.q[...] = ((qkv[:, 0:HW] + q_bias) * 0.125).astype(BF)
    m.kv[0] = qkv[:, HW:2 * HW].astype(BF)
    m.kv[1] = (qkv[:, 2 * HW:3 * HW] + v_bias).astype(BF)

    m.ssrc[0] = dot(pick, m.kv[0]).astype(BF)
    m.ssrc[1] = dot(pick, m.kv[1]).astype(BF)
    sum_at = take(16)

    def sum_copy(j):
        return pltpu.make_async_remote_copy(
            src_ref=m.ssrc,
            dst_ref=m.kvs.at[:, pl.ds(pl.multiple_of(SLOT * s, SLOT), SLOT), :],
            send_sem=sum_ss.at[j], recv_sem=rs.at[sum_at + s],
            device_id=dev(j, t, batch), device_id_type=MESH,
        )

    def sum_arrived(j):
        pltpu.make_async_remote_copy(
            src_ref=m.ssrc,
            dst_ref=m.kvs.at[:, pl.ds(SLOT * j, SLOT), :],
            send_sem=sum_ss.at[j], recv_sem=rs.at[sum_at + j],
            device_id=dev(j, t, batch), device_id_type=MESH,
        ).wait_recv()

    for j in range(1, 16):
        @pl.when(j > s)
        def _(j=j):
            sum_copy(j).start()
    m.wosl[t] = m.w1[...].reshape(D, D)[:, 3 * HW:]
    ag_wo = [fly([(m.wosl.at[t], m.wosl.at[t], here(u))]) for u in (over, sib)]

    for h in range(HEADS):
        m.sloc[h] = dot_nt(of_head(m.q[...], h), m.kv[0]) + m.bias[...]
    for h in range(HEADS):
        def soften1(rows, h=h):
            score = m.sloc[h, rows, :]
            peak = jnp.max(score, axis=-1, keepdims=True)
            power = jnp.exp(score - peak)
            m.prob1[h, rows, :] = power.astype(BF)
            m.m1[rows, h:h + 1] = peak
            m.l1[rows, h:h + 1] = jnp.sum(power, axis=-1, keepdims=True)

        loop(0, 4, ROWS, soften1)
        part = dot(m.prob1[h], of_head(m.kv[1], h))
        m.o1[...] = part if h == 0 else m.o1[...] + part
    ag_wo[0].wait_recv()
    ag_wo.append(fly([(m.wosl.at[over], m.wosl.at[over], here(sib))]))
    ag_do = gather_start(m.doa)

    for j in range(15):
        @pl.when(j < s)
        def _(j=j):
            sum_arrived(j)
    ends2 = spread_pass(m.w2, D, phase2)

    ag_att = []
    for c in range(2):
        rows_c = slice(CHUNK * c, CHUNK * c + CHUNK)
        part = None
        for h in range(HEADS):
            m.ssum[rows_c, :] = dot_nt(of_head(m.q[rows_c, :], h), m.kvs[0]) + sum_bias

            def soften2(rows, h=h):
                score = m.ssum[rows, :]
                peak = jnp.max(score, axis=-1, keepdims=True)
                power = jnp.exp(score - peak)
                m.prob2[h, rows, :] = power.astype(BF)
                m.m2[rows, h:h + 1] = peak
                m.l2[rows, h:h + 1] = jnp.sum(power, axis=-1, keepdims=True)

            loop(CHUNK * c, 2, ROWS, soften2)
            more = dot(m.prob2[h, rows_c, :], of_head(m.kvs[1], h))
            part = more if h == 0 else part + more
        m1, m2 = m.m1[rows_c, 0:HEADS], m.m2[rows_c, 0:HEADS]
        peak = jnp.maximum(m1, m2)
        e1, e2 = jnp.exp(m1 - peak), jnp.exp(m2 - peak)
        share = 1.0 / (m.l1[rows_c, 0:HEADS] * e1 + m.l2[rows_c, 0:HEADS] * e2)
        a1, a2 = e1 * share, e2 * share
        m.a1[rows_c, 0:HEADS] = a1
        m.a2[rows_c, 0:HEADS] = a2
        a1x, a2x = by_head(a1), by_head(a2)
        m.a1x[rows_c, :] = a1x
        m.a2x[rows_c, :] = a2x
        attended = m.o1[rows_c, :] * a1x + part * a2x
        m.att[rows_c, :] = attended
        m.atta[t, rows_c, :] = attended.astype(BF)
        mine_c = m.atta.at[t, rows_c]
        ag_att.append([fly([(mine_c, mine_c, here(u))]) for u in (over, sib)])
        if c == 0:
            finish(ag_wo)
            m.wof[...] = jnp.concatenate([m.wosl[u] for u in range(4)], axis=1)

    def att_pass(c):
        rows_c = slice(CHUNK * c, CHUNK * c + CHUNK)
        ag_att[c][0].wait_recv()
        theirs = m.atta.at[over, rows_c]
        ag_att[c].append(fly([(theirs, theirs, here(sib))]))

    def scatter_start(name, cs):
        src, r1 = getattr(m, name + "_s"), getattr(m, name + "_1")
        return [
            fly([(src.at[block(c, k)], r1.at[c, i], here(sib)) for c in cs],
                r1.at[0:len(cs), i])
            for i, k in ((1, diag), (0, sib))
        ]

    def scatter_pass(name, cs, moves):
        src, r1 = getattr(m, name + "_s"), getattr(m, name + "_1")
        cross, r2 = getattr(m, name + "_x"), getattr(m, name + "_2")
        moves[0].wait_recv()
        for c in cs:
            cross[c] = (src[block(c, over), :].astype(F32) + r1[c, 1].astype(F32)).astype(BF)
        moves.append(
            fly([(cross.at[c], r2.at[c], here(over)) for c in cs], r2.at[0:len(cs)])
        )

    def scatter_end(name, c, moves):
        src, r1 = getattr(m, name + "_s"), getattr(m, name + "_1")
        r2 = getattr(m, name + "_2")
        moves[1].wait_recv()
        moves[2].wait_recv()
        return src[block(c, t), :].astype(F32) + r1[c, 0].astype(F32) + r2[c].astype(F32)

    def gelu(rows):
        a = m.pre[rows, :]
        square = a * a
        bend = jnp.tanh(0.7978845608028654 * (a + 0.044715 * (square * a)))
        half = 0.5 * (1.0 + bend)
        m.act[rows, :] = (a * half).astype(BF)
        slope = half + (0.5 * a) * (1.0 - bend * bend) * (
            0.7978845608028654 * (1.0 + 0.134145 * square)
        )
        m.gp[rows, :] = (m.ga[rows, :] * slope).astype(BF)

    def norm2(rows):
        center, scale = norm_stats(m.hid[rows, :])
        m.nm[rows, :] = (center * scale * gain2 + shift2).astype(BF)

    def project(c):
        rows_c = slice(CHUNK * c, CHUNK * c + CHUNK)
        finish(ag_att[c])
        branch = dot(m.atta[0, rows_c, :], m.wof[0:HW, :])
        for u in range(1, 4):
            branch = branch + dot(m.atta[u, rows_c, :], m.wof[HW * u:HW * u + HW, :])
        m.hid[rows_c, :] = m.toka[rows_c, :].astype(F32) + branch + o_bias
        loop(CHUNK * c, 2, ROWS, norm2)

    def feed(c):
        rows_c = slice(CHUNK * c, CHUNK * c + CHUNK)
        m.pre[rows_c, :] = dot(m.nm[rows_c, :], m.w2[:, :, :, 0:D].reshape(D, D)) + up_bias
        m.ga[rows_c, :] = dot(m.doa[rows_c, :], m.w2[:, :, :, D:].reshape(D, D))
        loop(CHUNK * c, 4, 64, gelu)
        m.rm_s[rows_c, :] = dot_nt(m.gp[rows_c, :], m.w2[:, :, :, 0:D].reshape(D, D)).astype(BF)
        return scatter_start("rm", (c,))

    gather_pass(ag_do, m.doa)
    att_pass(0)
    project(0)
    att_pass(1)
    finish(ag_do)
    finish(ends2)
    rm0 = feed(0)
    project(1)
    scatter_pass("rm", (0,), rm0)
    rm1 = feed(1)

    m.dot_[...] = m.doa[...].T
    m.nmt[...] = m.nm[...].T
    scatter_pass("rm", (1,), rm1)
    m.g2[:, :, :, 0:D] = dot(m.nmt[...], m.gp[...]).astype(BF).reshape(4, 4, 48, D)
    m.g2[:, :, :, D:] = dot(m.dot_[...], m.act[...]).astype(BF).reshape(4, 4, 48, D)

    def reduce_start(g, tag, half):
        rza, rxb = getattr(m, "rza" + tag), getattr(m, "rxb" + tag)
        a, b = pl.ds(0, half), pl.ds(half, half)
        return (
            fly([(g.at[(z + k) % 4, :, :, a], rza.at[k - 1], along_z(k)) for k in (1, 3, 2)], rza),
            fly([(g.at[:, (x + k) % 4, :, b], rxb.at[k - 1], along_x(k)) for k in (1, 3, 2)], rxb),
        )

    def reduce_pass(g, tag, half, moves):
        rza, rxb = getattr(m, "rza" + tag), getattr(m, "rxb" + tag)
        rxa, rzb = getattr(m, "rxa" + tag), getattr(m, "rzb" + tag)
        ha, hb = getattr(m, "ha" + tag), getattr(m, "hb" + tag)
        moves[0].wait_recv()
        for k in range(4):
            ha[k] = add4(g[z, k, :, 0:half], [rza[j, k] for j in range(3)]).astype(BF)
        a2 = fly([(ha.at[(x + k) % 4], rxa.at[k - 1], along_x(k)) for k in (1, 3, 2)], rxa)
        moves[1].wait_recv()
        for k in range(4):
            hb[k] = add4(g[k, x, :, half:], [rxb[j, k] for j in range(3)]).astype(BF)
        b2 = fly([(hb.at[(z + k) % 4], rzb.at[k - 1], along_z(k)) for k in (1, 3, 2)], rzb)
        return a2, b2

    row64 = iota((64, 48), 0)
    expand = (
        (iota((64, 48), 1) == row64 - 4 * (row64 // 16)) & (row64 % 16 < 12)
    ).astype(BF)
    mine = 4 * batch + t
    everyone = [(u, dev(s, u, 1 - batch)) for u in (over, diag, sib, t)]
    everyone += [(u, here(u)) for u in group]

    def reduce_last(tag, half, moves):
        rxa, rzb = getattr(m, "rxa" + tag), getattr(m, "rzb" + tag)
        ha, hb = getattr(m, "ha" + tag), getattr(m, "hb" + tag)
        fx, fin = getattr(m, "fx" + tag), getattr(m, "fin" + tag)
        finish(moves)
        a = add4(ha[x], [rxa[j] for j in range(3)]).astype(BF)
        b = add4(hb[z], [rzb[j] for j in range(3)]).astype(BF)
        fx[:, :, 0:half] = dot(expand, a).astype(BF).reshape(4, 16, half)
        fx[:, :, half:] = dot(expand, b).astype(BF).reshape(4, 16, half)
        moves = fly([(fx.at[u], fin.at[mine], device) for u, device in everyone], fin.at[0:7])
        fin[mine] = fx[t]
        return moves

    rg2 = reduce_start(m.g2, "2", D)

    zero_row = jnp.zeros((1, D), F32)
    ones = jnp.ones((8, SEG), BF)

    def col_sums(value):
        return dot(ones[:, 0:value.shape[0]], value)[0:1, :]

    def norm_back(values, grads, gain):
        center, scale = norm_stats(values)
        unit = center * scale
        inner = grads * gain
        return unit, scale * (
            inner
            - jnp.mean(inner, axis=-1, keepdims=True)
            - unit * jnp.mean(inner * unit, axis=-1, keepdims=True)
        )

    g_gain2, g_shift2 = zero_row, zero_row
    aa = []
    for c in range(2):
        at = slice(HALF * c, HALF * c + HALF)
        grads = scatter_end("rm", c, rm0 if c == 0 else rm1)
        unit, into = norm_back(m.hid[block(c, t), :], grads, gain2)
        into = into + dout[at, :].astype(F32)
        m.gh[at, :] = into
        low = into.astype(BF)
        m.gbr[at, :] = low
        for u in range(4):
            m.sa[c, u] = dot_nt(low, m.wof[HW * u:HW * u + HW, :]).astype(BF)
        aa.append(
            fly([(m.sa.at[c, u], m.do.at[c, t], here(u)) for u in group], m.do.at[c, 0:3])
        )
        m.do[c, t] = m.sa[c, t]
        g_gain2 += jnp.sum(grads * unit, axis=0, keepdims=True)
        g_shift2 += jnp.sum(grads, axis=0, keepdims=True)
    m.ro_s[...] = dot_nt(m.act[...], m.w2[:, :, :, D:].reshape(D, D)).astype(BF)
    for u in range(4):
        cols = m.gbr[:, HW * u:HW * u + HW]
        m.sb[0, u] = cols[0:HALF, :]
        m.sb[1, u] = cols[HALF:, :]
    qt = m.q[...].T
    m.dq[...] = jnp.zeros((SEG, HW), F32)

    finish(aa)
    do_all = m.do[...].reshape(SEG, HW)
    do_wide = do_all.astype(F32)
    weighed = do_wide * m.att[...]
    for h in range(HEADS):
        m.delta[:, h:h + 1] = jnp.sum(of_head(weighed, h), axis=-1, keepdims=True)
    dot1 = (do_wide * m.a1x[...]).astype(BF).T
    dot2 = (do_wide * m.a2x[...]).astype(BF).T
    ab = fly(
        [(m.sb.at[c, u], m.gba.at[c, t], here(u)) for u in group for c in (0, 1)],
        m.gba.at[:, 0:3],
    )
    m.gba[0, t] = m.sb[0, t]
    m.gba[1, t] = m.sb[1, t]
    ro = scatter_start("ro", (0, 1))
    for h in range(HEADS):
        m.ssum[...] = dot_nt(of_head(do_all, h), m.kvs[1])

        def back_sum(rows, h=h):
            weight = m.prob2[h, rows, :].astype(F32)
            slope = (m.ssum[rows, :] - m.delta[rows, h:h + 1]) * m.a2[rows, h:h + 1]
            m.ds[rows, :] = (weight * slope).astype(BF)

        loop(0, 4, ROWS, back_sum)
        m.dq[...] += dot(m.ds[...], of_head(m.kvs[0], h))
        feat = slice(64 * h, 64 * h + 64)
        m.dkst[feat, :] = dot(qt[feat, :], m.ds[...])
        m.dvst[feat, :] = dot(dot2[feat, :], m.prob2[h])
    m.dkvs[0] = m.dkst[...].T.astype(BF)
    m.dkvs[1] = m.dvst[...].T.astype(BF)
    for j in range(1, 16):
        @pl.when(j > s)
        def _(j=j):
            sum_copy(j).wait_send()
    grad_at = take(16)

    def grad_copy(j):
        return pltpu.make_async_remote_copy(
            src_ref=m.dkvs.at[:, pl.ds(SLOT * j, SLOT), :],
            dst_ref=m.sumg.at[s],
            send_sem=sum_ss.at[j], recv_sem=rs.at[grad_at + s],
            device_id=dev(j, t, batch), device_id_type=MESH,
        )

    def grad_arrived(j):
        pltpu.make_async_remote_copy(
            src_ref=m.dkvs.at[:, pl.ds(0, SLOT), :],
            dst_ref=m.sumg.at[j],
            send_sem=sum_ss.at[j], recv_sem=rs.at[grad_at + j],
            device_id=dev(j, t, batch), device_id_type=MESH,
        ).wait_recv()

    for j in range(15):
        @pl.when(j < s)
        def _(j=j):
            grad_copy(j).start()
    scatter_pass("ro", (0, 1), ro)

    for h in range(HEADS):
        m.sloc[h] = dot_nt(of_head(do_all, h), m.kv[1])
    for h in range(HEADS):
        def back_own(rows, h=h):
            weight = m.prob1[h, rows, :].astype(F32)
            slope = (m.sloc[h, rows, :] - m.delta[rows, h:h + 1]) * m.a1[rows, h:h + 1]
            m.ds[rows, 0:SEG] = (weight * slope).astype(BF)

        loop(0, 4, ROWS, back_own)
        score_grads = m.ds[:, 0:SEG]
        m.dq[...] += dot(score_grads, of_head(m.kv[0], h))
        feat = slice(64 * h, 64 * h + 64)
        m.dkt[feat, :] = dot(qt[feat, :], score_grads)
        m.dvt[feat, :] = dot(dot1[feat, :], m.prob1[h])
    for u in range(4):
        m.attt[HW * u:HW * u + HW, :] = m.atta[u].T
    ab.wait_recv()
    g_o = dot(m.attt[...], m.gba[...].reshape(SEG, HW))
    ends_g2 = reduce_pass(m.g2, "2", D, rg2)

    for j in range(1, 16):
        @pl.when(j > s)
        def _(j=j):
            grad_arrived(j)

    def returned(which):
        total = m.sumg[0, which].astype(F32)
        for j in range(1, SLOTS):
            total = total + m.sumg[j, which].astype(F32)
        high = total.astype(BF)
        rest = (total - high.astype(F32)).astype(BF)
        return dot_tn(high, pick) + dot_tn(rest, pick)

    dk = (m.dkt[...] + returned(0)).T.astype(BF)
    dv = (m.dvt[...] + returned(1)).T.astype(BF)
    dq = m.dq[...].astype(BF) * jnp.asarray(0.125, BF)
    m.dqkv[...] = jnp.concatenate([dq, dk, dv], axis=1)

    g_qkv = dot(m.nrmt[...], m.dqkv[...])
    m.g1[...] = jnp.concatenate([g_qkv, g_o], axis=1).astype(BF).reshape(4, 4, 48, D)
    rg1 = reduce_start(m.g1, "1", D // 2)
    m.rn_s[...] = dot_nt(m.dqkv[...], m.w1[...].reshape(D, D)[:, 0:3 * HW]).astype(BF)
    rn = [scatter_start("rn", (c,)) for c in range(2)]

    def gain_grads(j, carry):
        rows = pl.ds(pl.multiple_of(j * 64, 64), 64)
        grads = m.rn_s[rows, :].astype(F32)
        unit = (m.toka[rows, :].astype(F32) - m.stat[rows, 0:1]) * m.stat[rows, 1:2]
        return (
            carry[0] + jnp.sum((grads * unit).reshape(8, 8, D), axis=0),
            carry[1] + jnp.sum(grads.reshape(8, 8, D), axis=0),
        )

    zero8 = jnp.zeros((8, D), F32)
    g_gain1, g_shift1 = lax.fori_loop(0, 8, gain_grads, (zero8, zero8))
    scatter_pass("rn", (0,), rn[0])
    scatter_pass("rn", (1,), rn[1])
    g_qkvb = col_sums(m.dqkv[...])

    def in_place(row):
        none = jnp.zeros((1, HW), F32)
        return jnp.concatenate([jnp.where(t == u, row, none) for u in range(4)], axis=1)

    rows8 = (
        jnp.sum(g_gain1, axis=0, keepdims=True),
        jnp.sum(g_shift1, axis=0, keepdims=True),
        in_place(g_qkvb[:, 0:HW]),
        in_place(g_qkvb[:, 2 * HW:]),
        col_sums(m.gbr[...]),
        g_gain2,
        g_shift2,
        col_sums(dout[...]),
    )
    m.vgr[...] = jnp.zeros((16, D), F32)
    for k, row in enumerate(rows8):
        m.vgr[k:k + 1, :] = row
    g_ub = col_sums(m.gp[...])
    for u in range(4):
        m.vgr[8 + u:9 + u, :] = jnp.where(t == u, g_ub, zero_row)
    vgx = fly([(m.vgr, m.vgx.at[k - 1], along_x(k)) for k in (1, 2, 3)], m.vgx)
    fin_g2 = reduce_last("2", D, ends_g2)
    for c in range(2):
        out_o[HALF * c:HALF * c + HALF, :] = (
            scatter_end("ro", c, ro) + m.hid[block(c, t), :] + down_bias
        ).astype(BF)
    ends_g1 = reduce_pass(m.g1, "1", D // 2, rg1)
    vgx.wait_recv()
    m.vgs[...] = add4(m.vgr[...], m.vgx)
    vgz = fly([(m.vgs, m.vgz.at[k - 1], along_z(k)) for k in (1, 2, 3)], m.vgz)

    for c in range(2):
        at = slice(HALF * c, HALF * c + HALF)
        grads = scatter_end("rn", c, rn[c])
        _, into = norm_back(tok[at, :].astype(F32), grads, gain1)
        gtok_o[at, :] = into + m.gh[at, :]
    vgz.wait_recv()
    m.vgt[...] = add4(m.vgs[...], m.vgz)
    fin_v = fly([(m.vgt, m.vfin.at[mine], device) for _, device in everyone], m.vfin.at[0:7])
    m.vfin[mine] = m.vgt[...]
    fin_g1 = reduce_last("1", D // 2, ends_g1)

    def both(fin, u, cols):
        return fin[u, 0:12, cols].astype(F32) + fin[4 + u, 0:12, cols].astype(F32)

    fin_g2.wait_recv()
    for u in range(4):
        wide = slice(D * u, D * u + D)
        gu_o[:, wide] = both(m.fin2, u, slice(0, D))
        gd_o[:, wide] = both(m.fin2, u, slice(D, 2 * D))
    fin_v.wait_recv()
    total = m.vfin[0]
    for k in range(1, 8):
        total = total + m.vfin[k]
    back = iota((D, 128), 0) - iota((D, 128), 1)
    lane = iota((D, 128), 1)
    get_12 = ((back == 12 * place) & (lane < 12)).astype(F32)
    get_48 = ((back == 48 * (place % 16)) & (lane < 48)).astype(F32)
    small = dot(total, get_12, precision=HIGHEST)
    large = dot(total, get_48, precision=HIGHEST)
    row16 = iota((16, 128), 0)
    chosen = jnp.sum(jnp.where(row16 == 8 + z, large, 0.0), axis=0, keepdims=True)
    gvec_o[...] = jnp.where(row16 < 8, small, jnp.where(row16 == 8, chosen, 0.0))
    fin_g1.wait_recv()
    parts = [both(m.fin1, u, slice(0, D)) for u in range(4)]
    for k, ref in enumerate((gq_o, gk_o, gv_o, go_o)):
        ref[...] = jnp.concatenate([p[:, HW * k:HW * k + HW] for p in parts], axis=1)

    for flight in sent:
        flight.wait_send()
    for j in range(15):
        @pl.when(j < s)
        def _(j=j):
            grad_copy(j).wait_send()
    assert used[0] <= RECVS, used[0]


def hand_out(*refs):
    whole, vec, outs = refs[:8], refs[8], refs[9:]
    for src, dst in zip(whole, outs[:8]):
        dst[...] = src[...]
    for k, dst in enumerate(outs[8:16]):
        dst[...] = vec[k:k + 1, 0:12]
    outs[16][...] = vec[8:9, 0:48]


def body(
    tokens, seg_lengths, ln1_gain, ln1_bias, w_query, q_bias, w_key, w_value, v_bias,
    w_out, o_bias, ln2_gain, ln2_bias, w_up, up_bias, w_down, down_bias, d_out,
):
    vectors = [ln1_gain, ln1_bias, q_bias, v_bias, o_bias, ln2_gain, ln2_bias, down_bias, up_bias]
    shape = jax.ShapeDtypeStruct
    vmem = pl.BlockSpec(memory_space=pltpu.VMEM)
    shapes = [
        shape((ROWS, D), BF),
        shape((ROWS, D), F32),
        shape((12, D), F32),
        shape((12, D), F32),
        shape((12, D), F32),
        shape((12, D), F32),
        shape((12, 4 * D), F32),
        shape((12, 4 * D), F32),
    ]
    outs = pl.pallas_call(
        layer_kernel,
        out_shape=shapes + [shape((16, 128), F32)],
        in_specs=[pl.BlockSpec(memory_space=pltpu.SMEM)] + [vmem] * 17,
        out_specs=[vmem] * 9,
        scratch_shapes=[pltpu.VMEM(dims, kind) for dims, kind in SCRATCH.values()]
        + [pltpu.SemaphoreType.DMA((n,)) for n in (SENDS, RECVS, SLOTS)],
        compiler_params=pltpu.CompilerParams(
            collective_id=0, has_side_effects=True, vmem_limit_bytes=62 * 2**20
        ),
        name="layer",
    )(
        seg_lengths, tokens[0], d_out[0], w_query, w_key, w_value, w_out, w_up, w_down,
        *[v.reshape(1, -1) for v in vectors],
    )
    outs = pl.pallas_call(
        hand_out,
        out_shape=shapes + [shape((1, 12), F32)] * 8 + [shape((1, 48), F32)],
        in_specs=[vmem] * 9,
        out_specs=[vmem] * 17,
        compiler_params=pltpu.CompilerParams(vmem_limit_bytes=62 * 2**20),
        name="hand_out",
    )(*outs)
    out, g_tok, g_q, g_k, g_v, g_o, g_up, g_down = outs[:8]
    l1g, l1b, qb, vb, ob, l2g, l2b, db, ub = [v.reshape(-1) for v in outs[8:]]
    return (
        out[None], g_tok[None], l1g, l1b, g_q, qb, g_k, g_v, vb,
        g_o, ob, l2g, l2b, g_up, ub, g_down, db,
    )


def solution(mesh):
    rows, cols = P("batch", "seq", None), P("seq", None)
    one = P("seq")
    placed = (
        rows, P("batch", None), one, one, cols, one, cols, cols, one,
        cols, one, one, one, cols, one, cols, one, rows,
    )
    return jax.shard_map(
        body,
        mesh=mesh,
        in_specs=placed,
        out_specs=(
            rows, rows, one, one, cols, one, cols, cols, one,
            cols, one, one, one, cols, one, cols, one,
        ),
        check_vma=False,
    )
```

time: 163 us -> 128 us (0.79)
  Pallas kernels: 150 us -> 127 us
  local copies, waits for them, and re-layouts: 11.5 us -> 0 us
    pallas_call x1 -> x2, Pallas kernels: 150 us -> 127 us  [the longest x1 124 us: body(): pl.pallas_call(layer_kernel, out_shape=shapes + [shape((16, 128), F32)],...]
    unnamed x42 -> x0, local copies, waits for them, and re-layouts: 8.71 us -> none
    squeeze x2 -> x0, local copies, waits for them, and re-layouts: 2.7 us -> none  [the longest x1 1.51 us: body(): g_vec[7, 0:12]]
where the time goes in v2:
time: 128 us
  Pallas kernels  127 us (99%)
    pallas_call x1, Pallas kernels, body(): pl.pallas_call(layer_kernel, out_shape=shapes + [shape((16, 128), F32)],...  124 us

profile of v2, /device:TPU:1, one launch (start us, length us, event | category | flops | bytes accessed | tf_op | source)
XLA Modules:
  0.0 127.6 jit_solution(1367359781618905038)
XLA Ops:
  0.7 124.4 %layer.1 = (bf16[128,768]{1,0:T(8,128)(2,1)}, f32[128,768]{1,0:T(8,128)}, f32[12,768]{1,0:T(8,128)}, f32[12,768]{1,0:T(8,128)}, f32[12,768]{1,0:T(8,128)}, /*ind...) custom-call(s32[1,16]{1,0:T(1,128)} %seg_ref.1, bf16[128,768]{1,0:T(8,128)(2,1)} %bitcast.22, ...), custom_call_target="tpu_custom_call" | custom-call | tf_op jit(solution)/shard_map/layer/pallas_call | solution.py:894
  125.0 2.4 %hand_out.1 = (bf16[128,768]{1,0:T(8,128)(2,1)}, f32[128,768]{1,0:T(8,128)}, f32[12,768]{1,0:T(8,128)}, f32[12,768]{1,0:T(8,128)}, f32[12,768]{1,0:T(8,128)}, /*...) custom-call(bf16[128,768]{1,0:T(8,128)(2,1)} %get-tuple-element.43.r, ...), custom_call_target="tpu_custom_call" | custom-call | tf_op jit(solution)/shard_map/hand_out/pallas_call | solution.py:909

commit v3 on v2

--- a/solution.py
+++ b/solution.py
@@ -57,7 +57,7 @@
     p02=((4, 16, 2 * D), BF),
     w1=((4, 4, 48, D), BF),
     w2=((4, 4, 48, 2 * D), BF),
-    wosl=((4, D, HW), BF),
+    wosl=((4, D // 2, 2 * HW), BF),
     wof=((D, D), BF),
     vin=((16, 128), F32),
     vb=((16, D), BF),
@@ -76,10 +76,13 @@
     bias=((SEG, SEG), F32),
     q=((SEG, HW), BF),
     kv=((2, SEG, HW), BF),
-    kvs=((2, SUMS, HW), BF),
-    ssrc=((2, SLOT, HW), BF),
-    sloc=((HEADS, SEG, SEG), F32),
-    ssum=((SEG, SUMS), F32),
+    kvl=((SEG, 2 * HW), BF),
+    kvs=((SUMS, 2 * HW), BF),
+    ks=((SUMS, HW), BF),
+    vs=((SUMS, HW), BF),
+    ssrc=((SLOT, 2 * HW), BF),
+    big=((SEG, HEADS * SEG), F32),
+    ssum=((HEADS, SEG, SUMS), F32),
     prob1=((HEADS, SEG, SEG), BF),
     prob2=((HEADS, SEG, SUMS), BF),
     m1=((SEG, 128), F32),
@@ -93,13 +96,12 @@
     a2x=((SEG, HW), F32),
     o1=((SEG, HW), F32),
     att=((SEG, HW), F32),
+    attp=((4, 2, ROWS, 2 * HW), BF),
     atta=((4, SEG, HW), BF),
     attt=((D, SEG), BF),
     hid=((SEG, D), F32),
     nm=((SEG, D), BF),
     nmt=((D, SEG), BF),
-    pre=((SEG, D), F32),
-    ga=((SEG, D), F32),
     act=((SEG, D), BF),
     gp=((SEG, D), BF),
     rm_s=((SEG, D), BF),
@@ -120,14 +122,12 @@
     sb=((2, 4, HALF, HW), BF),
     do=((2, 4, HALF, HW), BF),
     gba=((2, 4, HALF, HW), BF),
-    ds=((SEG, SUMS), BF),
+    ds=((HEADS, SEG, SUMS), BF),
     dq=((SEG, HW), F32),
-    dkt=((HW, SEG), F32),
-    dvt=((HW, SEG), F32),
-    dkst=((HW, SUMS), F32),
-    dvst=((HW, SUMS), F32),
-    dkvs=((2, SUMS, HW), BF),
-    sumg=((SLOTS, 2, SLOT, HW), BF),
+    dkvt=((2 * HW, SEG), F32),
+    dkvst=((2 * HW, SUMS), F32),
+    dkvs=((SUMS, 2 * HW), BF),
+    sumg=((SLOTS, SLOT, 2 * HW), BF),
     dqkv=((SEG, 3 * HW), BF),
     g1=((4, 4, 48, D), BF),
     g2=((4, 4, 48, 2 * D), BF),
@@ -151,8 +151,9 @@
     vgx=((3, 16, D), F32),
     vgs=((16, D), F32),
     vgz=((3, 16, D), F32),
-    vgt=((16, D), F32),
-    vfin=((8, 16, D), F32),
+    sel=((D, 384), BF),
+    vgt=((16, 256), F32),
+    vfin=((8, 16, 256), F32),
 )
 SENDS = 24
 RECVS = 100
@@ -237,15 +238,15 @@
     def block(c, k):
         return pl.ds(pl.multiple_of(CHUNK * c + HALF * k, HALF), HALF)
 
-    def loop(first, count, size, fn, unroll=1):
+    def loop(first, count, size, fn, unroll=4):
         def step(j, carry):
             fn(pl.ds(pl.multiple_of(first + j * size, size), size))
             return carry
 
         lax.fori_loop(0, count, step, 0, unroll=unroll)
 
-    m.kvs[...] = jnp.zeros((2, SUMS, HW), BF)
-    m.sumg[...] = jnp.zeros((SLOTS, 2, SLOT, HW), BF)
+    m.kvs[...] = jnp.zeros((SUMS, 2 * HW), BF)
+    m.sumg[...] = jnp.zeros((SLOTS, SLOT, 2 * HW), BF)
     barrier = pltpu.get_barrier_semaphore()
     partners = [here(u) for u in group]
     partners += [dev((s + k) % 16, t, batch) for k in range(1, 16)]
@@ -366,6 +367,19 @@
     def add4(own, got):
         return own.astype(F32) + got[0].astype(F32) + got[1].astype(F32) + got[2].astype(F32)
 
+    def moved_by(rows, one_hot):
+        high = rows.astype(BF)
+        rest = rows - high.astype(F32)
+        mid = rest.astype(BF)
+        low = (rest - mid.astype(F32)).astype(BF)
+        pieces = dot(jnp.concatenate([high, mid, low], axis=0), one_hot)
+        return pieces[0:16, :] + pieces[16:32, :] + pieces[32:48, :]
+
+    feature, lane = iota((D, 128), 0), iota((D, 128), 1)
+    m.sel[:, 0:128] = ((feature - lane == 48 * s) & (lane < 48)).astype(BF)
+    feature, lane = iota((D, 256), 0), iota((D, 256), 1)
+    m.sel[:, 128:384] = ((feature - lane == 192 * x) & (lane < 192)).astype(BF)
+
     firstv.wait_recv()
     m.vs1[...] = add4(m.vb[...], m.vg).astype(BF)
     vx = fly([(m.vs1, m.vx.at[k - 1], along_x(k)) for k in (1, 2, 3)], m.vx)
@@ -375,7 +389,9 @@
     vz = fly([(m.vs2, m.vz.at[k - 1], along_z(k)) for k in (1, 2, 3)], m.vz)
     first2.wait_recv()
     m.w2[z, x] = dot(squeeze, m.p02[...].reshape(64, 2 * D)).astype(BF)
+    phase2 = spread_start(m.w2, D)
     gather_pass(ag_tok, m.toka)
+    ag_do = gather_start(m.doa)
     vz.wait_recv()
     m.vecs[...] = add4(m.vs2[...], m.vz)
     gain1, shift1 = m.vecs[0:1, :], m.vecs[1:2, :]
@@ -409,45 +425,38 @@
     m.nrmt[...] = m.nrm[...].T
 
     finish(ends1)
-    phase2 = spread_start(m.w2, D)
     w1 = m.w1[...].reshape(D, D)
     qkv = dot(m.nrm[...], w1)
     m.q[...] = ((qkv[:, 0:HW] + q_bias) * 0.125).astype(BF)
-    m.kv[0] = qkv[:, HW:2 * HW].astype(BF)
-    m.kv[1] = (qkv[:, 2 * HW:3 * HW] + v_bias).astype(BF)
-
-    m.ssrc[0] = dot(pick, m.kv[0]).astype(BF)
-    m.ssrc[1] = dot(pick, m.kv[1]).astype(BF)
+    kv_bias = jnp.concatenate([jnp.zeros((1, HW), F32), v_bias], axis=1)
+    m.kvl[...] = (qkv[:, HW:3 * HW] + kv_bias).astype(BF)
+
+    m.ssrc[...] = dot(pick, m.kvl[...]).astype(BF)
     sum_at = take(16)
 
-    def sum_copy(j):
+    def sum_copy(k):
         return pltpu.make_async_remote_copy(
             src_ref=m.ssrc,
-            dst_ref=m.kvs.at[:, pl.ds(pl.multiple_of(SLOT * s, SLOT), SLOT), :],
-            send_sem=sum_ss.at[j], recv_sem=rs.at[sum_at + s],
-            device_id=dev(j, t, batch), device_id_type=MESH,
-        )
-
-    def sum_arrived(j):
-        pltpu.make_async_remote_copy(
-            src_ref=m.ssrc,
-            dst_ref=m.kvs.at[:, pl.ds(SLOT * j, SLOT), :],
-            send_sem=sum_ss.at[j], recv_sem=rs.at[sum_at + j],
-            device_id=dev(j, t, batch), device_id_type=MESH,
-        ).wait_recv()
-
-    for j in range(1, 16):
-        @pl.when(j > s)
-        def _(j=j):
-            sum_copy(j).start()
-    m.wosl[t] = m.w1[...].reshape(D, D)[:, 3 * HW:]
+            dst_ref=m.kvs.at[pl.ds(pl.multiple_of(SLOT * s, SLOT), SLOT)],
+            send_sem=sum_ss.at[k], recv_sem=rs.at[sum_at + k],
+            device_id=dev((s + k) % 16, t, batch), device_id_type=MESH,
+        )
+
+    for k in range(1, 16):
+        @pl.when(s + k < 16)
+        def _(k=k):
+            sum_copy(k).start()
+    w_o = m.w1[...].reshape(D, D)[:, 3 * HW:]
+    m.wosl[t] = jnp.concatenate([w_o[0:D // 2, :], w_o[D // 2:, :]], axis=1)
+    m.kv[0] = m.kvl[:, 0:HW]
+    m.kv[1] = m.kvl[:, HW:]
     ag_wo = [fly([(m.wosl.at[t], m.wosl.at[t], here(u))]) for u in (over, sib)]
 
     for h in range(HEADS):
-        m.sloc[h] = dot_nt(of_head(m.q[...], h), m.kv[0]) + m.bias[...]
+        m.big[:, SEG * h:SEG * h + SEG] = dot_nt(of_head(m.q[...], h), m.kv[0]) + m.bias[...]
     for h in range(HEADS):
         def soften1(rows, h=h):
-            score = m.sloc[h, rows, :]
+            score = m.big[rows, SEG * h:SEG * h + SEG]
             peak = jnp.max(score, axis=-1, keepdims=True)
             power = jnp.exp(score - peak)
             m.prob1[h, rows, :] = power.astype(BF)
@@ -457,25 +466,26 @@
         loop(0, 4, ROWS, soften1)
         part = dot(m.prob1[h], of_head(m.kv[1], h))
         m.o1[...] = part if h == 0 else m.o1[...] + part
-    ag_wo[0].wait_recv()
-    ag_wo.append(fly([(m.wosl.at[over], m.wosl.at[over], here(sib))]))
-    ag_do = gather_start(m.doa)
-
-    for j in range(15):
-        @pl.when(j < s)
-        def _(j=j):
-            sum_arrived(j)
+    gather_pass(ag_do, m.doa)
+
+    for k in range(1, 16):
+        @pl.when(s >= k)
+        def _(k=k):
+            sum_copy(k).wait_recv()
     ends2 = spread_pass(m.w2, D, phase2)
+    m.ks[...] = m.kvs[:, 0:HW]
+    m.vs[...] = m.kvs[:, HW:]
 
     ag_att = []
-    for c in range(2):
+
+    def attend(c):
         rows_c = slice(CHUNK * c, CHUNK * c + CHUNK)
         part = None
         for h in range(HEADS):
-            m.ssum[rows_c, :] = dot_nt(of_head(m.q[rows_c, :], h), m.kvs[0]) + sum_bias
+            m.ssum[h, rows_c, :] = dot_nt(of_head(m.q[rows_c, :], h), m.ks[...]) + sum_bias
 
             def soften2(rows, h=h):
-                score = m.ssum[rows, :]
+                score = m.ssum[h, rows, :]
                 peak = jnp.max(score, axis=-1, keepdims=True)
                 power = jnp.exp(score - peak)
                 m.prob2[h, rows, :] = power.astype(BF)
@@ -483,7 +493,7 @@
                 m.l2[rows, h:h + 1] = jnp.sum(power, axis=-1, keepdims=True)
 
             loop(CHUNK * c, 2, ROWS, soften2)
-            more = dot(m.prob2[h, rows_c, :], of_head(m.kvs[1], h))
+            more = dot(m.prob2[h, rows_c, :], of_head(m.vs[...], h))
             part = more if h == 0 else part + more
         m1, m2 = m.m1[rows_c, 0:HEADS], m.m2[rows_c, 0:HEADS]
         peak = jnp.maximum(m1, m2)
@@ -497,17 +507,22 @@
         m.a2x[rows_c, :] = a2x
         attended = m.o1[rows_c, :] * a1x + part * a2x
         m.att[rows_c, :] = attended
-        m.atta[t, rows_c, :] = attended.astype(BF)
-        mine_c = m.atta.at[t, rows_c]
+        low = attended.astype(BF)
+        m.attp[t, c] = jnp.concatenate([low[0:ROWS, :], low[ROWS:, :]], axis=1)
+        mine_c = m.attp.at[t, c]
         ag_att.append([fly([(mine_c, mine_c, here(u))]) for u in (over, sib)])
-        if c == 0:
-            finish(ag_wo)
-            m.wof[...] = jnp.concatenate([m.wosl[u] for u in range(4)], axis=1)
+
+    attend(0)
+    ag_wo[0].wait_recv()
+    ag_wo.append(fly([(m.wosl.at[over], m.wosl.at[over], here(sib))]))
+    attend(1)
+    finish(ag_wo)
+    m.wof[0:D // 2, :] = jnp.concatenate([m.wosl[u, :, 0:HW] for u in range(4)], axis=1)
+    m.wof[D // 2:, :] = jnp.concatenate([m.wosl[u, :, HW:] for u in range(4)], axis=1)
 
     def att_pass(c):
-        rows_c = slice(CHUNK * c, CHUNK * c + CHUNK)
         ag_att[c][0].wait_recv()
-        theirs = m.atta.at[over, rows_c]
+        theirs = m.attp.at[over, c]
         ag_att[c].append(fly([(theirs, theirs, here(sib))]))
 
     def scatter_start(name, cs):
@@ -536,7 +551,7 @@
         return src[block(c, t), :].astype(F32) + r1[c, 0].astype(F32) + r2[c].astype(F32)
 
     def gelu(rows):
-        a = m.pre[rows, :]
+        a = m.big[rows, 0:D]
         square = a * a
         bend = jnp.tanh(0.7978845608028654 * (a + 0.044715 * (square * a)))
         half = 0.5 * (1.0 + bend)
@@ -544,7 +559,7 @@
         slope = half + (0.5 * a) * (1.0 - bend * bend) * (
             0.7978845608028654 * (1.0 + 0.134145 * square)
         )
-        m.gp[rows, :] = (m.ga[rows, :] * slope).astype(BF)
+        m.gp[rows, :] = (m.big[rows, D:] * slope).astype(BF)
 
     def norm2(rows):
         center, scale = norm_stats(m.hid[rows, :])
@@ -553,6 +568,9 @@
     def project(c):
         rows_c = slice(CHUNK * c, CHUNK * c + CHUNK)
         finish(ag_att[c])
+        for u in range(4):
+            m.atta[u, CHUNK * c:CHUNK * c + ROWS, :] = m.attp[u, c, :, 0:HW]
+            m.atta[u, CHUNK * c + ROWS:CHUNK * c + CHUNK, :] = m.attp[u, c, :, HW:]
         branch = dot(m.atta[0, rows_c, :], m.wof[0:HW, :])
         for u in range(1, 4):
             branch = branch + dot(m.atta[u, rows_c, :], m.wof[HW * u:HW * u + HW, :])
@@ -561,13 +579,12 @@
 
     def feed(c):
         rows_c = slice(CHUNK * c, CHUNK * c + CHUNK)
-        m.pre[rows_c, :] = dot(m.nm[rows_c, :], m.w2[:, :, :, 0:D].reshape(D, D)) + up_bias
-        m.ga[rows_c, :] = dot(m.doa[rows_c, :], m.w2[:, :, :, D:].reshape(D, D))
+        m.big[rows_c, 0:D] = dot(m.nm[rows_c, :], m.w2[:, :, :, 0:D].reshape(D, D)) + up_bias
+        m.big[rows_c, D:] = dot(m.doa[rows_c, :], m.w2[:, :, :, D:].reshape(D, D))
         loop(CHUNK * c, 4, 64, gelu)
         m.rm_s[rows_c, :] = dot_nt(m.gp[rows_c, :], m.w2[:, :, :, 0:D].reshape(D, D)).astype(BF)
         return scatter_start("rm", (c,))
 
-    gather_pass(ag_do, m.doa)
     att_pass(0)
     project(0)
     att_pass(1)
@@ -687,85 +704,74 @@
     m.gba[1, t] = m.sb[1, t]
     ro = scatter_start("ro", (0, 1))
     for h in range(HEADS):
-        m.ssum[...] = dot_nt(of_head(do_all, h), m.kvs[1])
+        m.ssum[h] = dot_nt(of_head(do_all, h), m.vs[...])
 
         def back_sum(rows, h=h):
             weight = m.prob2[h, rows, :].astype(F32)
-            slope = (m.ssum[rows, :] - m.delta[rows, h:h + 1]) * m.a2[rows, h:h + 1]
-            m.ds[rows, :] = (weight * slope).astype(BF)
+            slope = (m.ssum[h, rows, :] - m.delta[rows, h:h + 1]) * m.a2[rows, h:h + 1]
+            m.ds[h, rows, :] = (weight * slope).astype(BF)
 
         loop(0, 4, ROWS, back_sum)
-        m.dq[...] += dot(m.ds[...], of_head(m.kvs[0], h))
-        feat = slice(64 * h, 64 * h + 64)
-        m.dkst[feat, :] = dot(qt[feat, :], m.ds[...])
-        m.dvst[feat, :] = dot(dot2[feat, :], m.prob2[h])
-    m.dkvs[0] = m.dkst[...].T.astype(BF)
-    m.dkvs[1] = m.dvst[...].T.astype(BF)
-    for j in range(1, 16):
-        @pl.when(j > s)
-        def _(j=j):
-            sum_copy(j).wait_send()
+        feat, feat_v = slice(64 * h, 64 * h + 64), slice(HW + 64 * h, HW + 64 * h + 64)
+        m.dkvst[feat, :] = dot(qt[feat, :], m.ds[h])
+        m.dkvst[feat_v, :] = dot(dot2[feat, :], m.prob2[h])
+    m.dkvs[...] = m.dkvst[...].T.astype(BF)
+    for k in range(1, 16):
+        @pl.when(s + k < 16)
+        def _(k=k):
+            sum_copy(k).wait_send()
     grad_at = take(16)
 
-    def grad_copy(j):
+    def grad_copy(k):
+        slot = (s + 16 - k) % 16
         return pltpu.make_async_remote_copy(
-            src_ref=m.dkvs.at[:, pl.ds(SLOT * j, SLOT), :],
-            dst_ref=m.sumg.at[s],
-            send_sem=sum_ss.at[j], recv_sem=rs.at[grad_at + s],
-            device_id=dev(j, t, batch), device_id_type=MESH,
-        )
-
-    def grad_arrived(j):
-        pltpu.make_async_remote_copy(
-            src_ref=m.dkvs.at[:, pl.ds(0, SLOT), :],
-            dst_ref=m.sumg.at[j],
-            send_sem=sum_ss.at[j], recv_sem=rs.at[grad_at + j],
-            device_id=dev(j, t, batch), device_id_type=MESH,
-        ).wait_recv()
-
-    for j in range(15):
-        @pl.when(j < s)
-        def _(j=j):
-            grad_copy(j).start()
+            src_ref=m.dkvs.at[pl.ds(pl.multiple_of(SLOT * slot, SLOT), SLOT)],
+            dst_ref=m.sumg.at[k],
+            send_sem=sum_ss.at[k], recv_sem=rs.at[grad_at + k],
+            device_id=dev(slot, t, batch), device_id_type=MESH,
+        )
+
+    for k in range(1, 16):
+        @pl.when(s >= k)
+        def _(k=k):
+            grad_copy(k).start()
     scatter_pass("ro", (0, 1), ro)
 
     for h in range(HEADS):
-        m.sloc[h] = dot_nt(of_head(do_all, h), m.kv[1])
+        m.dq[...] += dot(m.ds[h], of_head(m.ks[...], h))
+    for h in range(HEADS):
+        m.big[:, SEG * h:SEG * h + SEG] = dot_nt(of_head(do_all, h), m.kv[1])
     for h in range(HEADS):
         def back_own(rows, h=h):
             weight = m.prob1[h, rows, :].astype(F32)
-            slope = (m.sloc[h, rows, :] - m.delta[rows, h:h + 1]) * m.a1[rows, h:h + 1]
-            m.ds[rows, 0:SEG] = (weight * slope).astype(BF)
+            slope = (m.big[rows, SEG * h:SEG * h + SEG] - m.delta[rows, h:h + 1]) * m.a1[rows, h:h + 1]
+            m.ds[h, rows, 0:SEG] = (weight * slope).astype(BF)
 
         loop(0, 4, ROWS, back_own)
-        score_grads = m.ds[:, 0:SEG]
+        score_grads = m.ds[h, :, 0:SEG]
         m.dq[...] += dot(score_grads, of_head(m.kv[0], h))
-        feat = slice(64 * h, 64 * h + 64)
-        m.dkt[feat, :] = dot(qt[feat, :], score_grads)
-        m.dvt[feat, :] = dot(dot1[feat, :], m.prob1[h])
+        feat, feat_v = slice(64 * h, 64 * h + 64), slice(HW + 64 * h, HW + 64 * h + 64)
+        m.dkvt[feat, :] = dot(qt[feat, :], score_grads)
+        m.dkvt[feat_v, :] = dot(dot1[feat, :], m.prob1[h])
     for u in range(4):
         m.attt[HW * u:HW * u + HW, :] = m.atta[u].T
     ab.wait_recv()
     g_o = dot(m.attt[...], m.gba[...].reshape(SEG, HW))
     ends_g2 = reduce_pass(m.g2, "2", D, rg2)
 
-    for j in range(1, 16):
-        @pl.when(j > s)
-        def _(j=j):
-            grad_arrived(j)
-
-    def returned(which):
-        total = m.sumg[0, which].astype(F32)
-        for j in range(1, SLOTS):
-            total = total + m.sumg[j, which].astype(F32)
-        high = total.astype(BF)
-        rest = (total - high.astype(F32)).astype(BF)
-        return dot_tn(high, pick) + dot_tn(rest, pick)
-
-    dk = (m.dkt[...] + returned(0)).T.astype(BF)
-    dv = (m.dvt[...] + returned(1)).T.astype(BF)
+    for k in range(1, 16):
+        @pl.when(s + k < 16)
+        def _(k=k):
+            grad_copy(k).wait_recv()
+
+    total = m.sumg[0].astype(F32)
+    for k in range(1, SLOTS):
+        total = total + m.sumg[k].astype(F32)
+    high = total.astype(BF)
+    rest = (total - high.astype(F32)).astype(BF)
+    dkv = (m.dkvt[...] + dot_tn(high, pick) + dot_tn(rest, pick)).T.astype(BF)
     dq = m.dq[...].astype(BF) * jnp.asarray(0.125, BF)
-    m.dqkv[...] = jnp.concatenate([dq, dk, dv], axis=1)
+    m.dqkv[...] = jnp.concatenate([dq, dkv], axis=1)
 
     g_qkv = dot(m.nrmt[...], m.dqkv[...])
     m.g1[...] = jnp.concatenate([g_qkv, g_o], axis=1).astype(BF).reshape(4, 4, 48, D)
@@ -824,11 +830,16 @@
         grads = scatter_end("rn", c, rn[c])
         _, into = norm_back(tok[at, :].astype(F32), grads, gain1)
         gtok_o[at, :] = into + m.gh[at, :]
+    fin_g1 = reduce_last("1", D // 2, ends_g1)
     vgz.wait_recv()
-    m.vgt[...] = add4(m.vgs[...], m.vgz)
+    totals = add4(m.vgs[...], m.vgz)
+    moved = moved_by(totals, m.sel[...])
+    up_row = jnp.sum(jnp.where(iota((16, 256), 0) == 8 + z, moved[:, 128:384], 0.0), axis=0, keepdims=True)
+    m.vgt[...] = jnp.zeros((16, 256), F32)
+    m.vgt[0:8, 0:128] = moved[0:8, 0:128]
+    m.vgt[8:9, :] = up_row
     fin_v = fly([(m.vgt, m.vfin.at[mine], device) for _, device in everyone], m.vfin.at[0:7])
     m.vfin[mine] = m.vgt[...]
-    fin_g1 = reduce_last("1", D // 2, ends_g1)
 
     def both(fin, u, cols):
         return fin[u, 0:12, cols].astype(F32) + fin[4 + u, 0:12, cols].astype(F32)
@@ -839,18 +850,14 @@
         gu_o[:, wide] = both(m.fin2, u, slice(0, D))
         gd_o[:, wide] = both(m.fin2, u, slice(D, 2 * D))
     fin_v.wait_recv()
-    total = m.vfin[0]
+    totals = m.vfin[0]
     for k in range(1, 8):
-        total = total + m.vfin[k]
-    back = iota((D, 128), 0) - iota((D, 128), 1)
-    lane = iota((D, 128), 1)
-    get_12 = ((back == 12 * place) & (lane < 12)).astype(F32)
-    get_48 = ((back == 48 * (place % 16)) & (lane < 48)).astype(F32)
-    small = dot(total, get_12, precision=HIGHEST)
-    large = dot(total, get_48, precision=HIGHEST)
+        totals = totals + m.vfin[k]
+    source, target = iota((256, 128), 0), iota((256, 128), 1)
+    own_12 = ((source - target == 12 * t) & (target < 12)).astype(BF)
+    own_48 = ((source - target == 48 * t) & (target < 48)).astype(BF)
     row16 = iota((16, 128), 0)
-    chosen = jnp.sum(jnp.where(row16 == 8 + z, large, 0.0), axis=0, keepdims=True)
-    gvec_o[...] = jnp.where(row16 < 8, small, jnp.where(row16 == 8, chosen, 0.0))
+    gvec_o[...] = jnp.where(row16 < 8, moved_by(totals, own_12), moved_by(totals, own_48))
     fin_g1.wait_recv()
     parts = [both(m.fin1, u, slice(0, D)) for u in range(4)]
     for k, ref in enumerate((gq_o, gk_o, gv_o, go_o)):
@@ -858,10 +865,10 @@
 
     for flight in sent:
         flight.wait_send()
-    for j in range(15):
-        @pl.when(j < s)
-        def _(j=j):
-            grad_copy(j).wait_send()
+    for k in range(1, 16):
+        @pl.when(s >= k)
+        def _(k=k):
+            grad_copy(k).wait_send()
     assert used[0] <= RECVS, used[0]
 
 

time: 128 us -> 113 us (0.88)
  Pallas kernels: 127 us -> 112 us
    pallas_call x1, Pallas kernels: 124 us -> 110 us  [body(): pl.pallas_call(layer_kernel, out_shape=shapes + [shape((16, 128), F32)],...]
where the time goes in v3:
time: 113 us
  Pallas kernels  112 us (99%)
    pallas_call x1, Pallas kernels, body(): pl.pallas_call(layer_kernel, out_shape=shapes + [shape((16, 128), F32)],...  110 us
    pallas_call x1, Pallas kernels, body(): pl.pallas_call(hand_out, out_shape=shapes + [shape((1, 12), F32)] * 8 + [...  2.35 us

profile of v3, /device:TPU:1, one launch (start us, length us, event | category | flops | bytes accessed | tf_op | source)
XLA Modules:
  0.0 112.9 jit_solution(2829986243407667199)
XLA Ops:
  0.7 109.7 %layer.1 = (bf16[128,768]{1,0:T(8,128)(2,1)}, f32[128,768]{1,0:T(8,128)}, f32[12,768]{1,0:T(8,128)}, f32[12,768]{1,0:T(8,128)}, f32[12,768]{1,0:T(8,128)}, /*ind...) custom-call(s32[1,16]{1,0:T(1,128)} %seg_ref.1, bf16[128,768]{1,0:T(8,128)(2,1)} %bitcast.22, ...), custom_call_target="tpu_custom_call" | custom-call | tf_op jit(solution)/shard_map/layer/pallas_call | solution.py:901
  110.4 2.4 %hand_out.1 = (bf16[128,768]{1,0:T(8,128)(2,1)}, f32[128,768]{1,0:T(8,128)}, f32[12,768]{1,0:T(8,128)}, f32[12,768]{1,0:T(8,128)}, f32[12,768]{1,0:T(8,128)}, /*...) custom-call(bf16[128,768]{1,0:T(8,128)(2,1)} %get-tuple-element.43.r, ...), custom_call_target="tpu_custom_call" | custom-call | tf_op jit(solution)/shard_map/hand_out/pallas_call | solution.py:916

commit v4 on v3

--- a/solution.py
+++ b/solution.py
@@ -82,7 +82,7 @@
     vs=((SUMS, HW), BF),
     ssrc=((SLOT, 2 * HW), BF),
     big=((SEG, HEADS * SEG), F32),
-    ssum=((HEADS, SEG, SUMS), F32),
+    ssum=((HEADS, CHUNK, SUMS), F32),
     prob1=((HEADS, SEG, SEG), BF),
     prob2=((HEADS, SEG, SUMS), BF),
     m1=((SEG, 128), F32),
@@ -91,14 +91,12 @@
     l2=((SEG, 128), F32),
     a1=((SEG, 128), F32),
     a2=((SEG, 128), F32),
-    delta=((SEG, 128), F32),
     a1x=((SEG, HW), F32),
     a2x=((SEG, HW), F32),
     o1=((SEG, HW), F32),
     att=((SEG, HW), F32),
     attp=((4, 2, ROWS, 2 * HW), BF),
     atta=((4, SEG, HW), BF),
-    attt=((D, SEG), BF),
     hid=((SEG, D), F32),
     nm=((SEG, D), BF),
     nmt=((D, SEG), BF),
@@ -123,9 +121,6 @@
     do=((2, 4, HALF, HW), BF),
     gba=((2, 4, HALF, HW), BF),
     ds=((HEADS, SEG, SUMS), BF),
-    dq=((SEG, HW), F32),
-    dkvt=((2 * HW, SEG), F32),
-    dkvst=((2 * HW, SUMS), F32),
     dkvs=((SUMS, 2 * HW), BF),
     sumg=((SLOTS, SLOT, 2 * HW), BF),
     dqkv=((SEG, 3 * HW), BF),
@@ -156,7 +151,7 @@
     vfin=((8, 16, 256), F32),
 )
 SENDS = 24
-RECVS = 100
+RECVS = 66
 
 
 class Flight:
@@ -182,8 +177,8 @@
     vectors, refs = refs[:9], refs[9:]
     out_o, gtok_o, gq_o, gk_o, gv_o, go_o, gu_o, gd_o, gvec_o = refs[:9]
     scratch = refs[9:]
-    m = types.SimpleNamespace(**dict(zip(SCRATCH, scratch[:-3])))
-    ss, rs, sum_ss = scratch[-3:]
+    m = types.SimpleNamespace(**dict(zip(SCRATCH, scratch[:-4])))
+    ss, rs, far_ss, far_rs = scratch[-4:]
     batch = lax.axis_index("batch")
     place = lax.axis_index("seq")
     s = place // 4
@@ -235,8 +230,30 @@
         sent.append(flight)
         return flight
 
+    def far_copy(which, src, dst, seg):
+        return pltpu.make_async_remote_copy(
+            src_ref=src, dst_ref=dst, send_sem=far_ss.at[which], recv_sem=far_rs.at[which],
+            device_id=dev(seg, t, batch), device_id_type=MESH,
+        )
+
+    def slot_of(ref, seg):
+        return ref.at[pl.ds(pl.multiple_of(SLOT * seg, SLOT), SLOT)]
+
+    def far_wait(which, count, received):
+        for n in range(1, 16):
+            @pl.when(count == n)
+            def _(n=n):
+                part = m.kvs.at[0:SLOT * n]
+                if received:
+                    far_copy(which, part, part, s).wait_recv()
+                else:
+                    far_copy(which, part, part, s).wait_send()
+
     def block(c, k):
         return pl.ds(pl.multiple_of(CHUNK * c + HALF * k, HALF), HALF)
+
+    def within(rows, c):
+        return pl.ds(pl.multiple_of(rows.start - CHUNK * c, rows.size), rows.size)
 
     def loop(first, count, size, fn, unroll=4):
         def step(j, carry):
@@ -257,7 +274,7 @@
     for u in range(4):
         cols = slice(HW * u, HW * u + HW)
         m.pk1[u, 0:12, :] = jnp.concatenate(
-            [wq[:, cols], wk[:, cols], wv[:, cols], wo[:, cols]], axis=1
+            [wk[:, cols], wv[:, cols], wq[:, cols], wo[:, cols]], axis=1
         )
     m.vin[...] = jnp.zeros((16, 128), F32)
     for k, ref in enumerate(vectors[:8]):
@@ -314,26 +331,35 @@
     )
     squeeze = (iota((48, 64), 1) == row48 + 4 * owner48).astype(BF)
 
-    def spread_start(w, half):
-        a, b = pl.ds(0, half), pl.ds(half, half)
+    def spread_start(w, a, b):
         mine_a, mine_b = w.at[z, x, :, a], w.at[z, x, :, b]
         return (
             fly([(mine_a, mine_a, along_x(k)) for k in (1, 3, 2)], w.at[0, 0:3, :, a]),
             fly([(mine_b, mine_b, along_z(k)) for k in (1, 3, 2)], w.at[0, 0:3, :, b]),
         )
 
-    def spread_pass(w, half, moves):
-        a, b = pl.ds(0, half), pl.ds(half, half)
-        plane_a, plane_b = w.at[z, :, :, a], w.at[:, x, :, b]
+    def pass_a(w, a, moves):
+        plane_a = w.at[z, :, :, a]
         moves[0].wait_recv()
-        a2 = fly([(plane_a, plane_a, along_z(k)) for k in (1, 3, 2)], w.at[0:3, :, :, a])
+        return fly([(plane_a, plane_a, along_z(k)) for k in (1, 3, 2)], w.at[0:3, :, :, a])
+
+    def pass_b(w, b, moves):
+        plane_b = w.at[:, x, :, b]
         moves[1].wait_recv()
-        b2 = fly([(plane_b, plane_b, along_x(k)) for k in (1, 3, 2)], w.at[0:3, :, :, b])
-        return a2, b2
+        return fly([(plane_b, plane_b, along_x(k)) for k in (1, 3, 2)], w.at[0:3, :, :, b])
+
+    def spread_pass(w, a, b, moves):
+        return pass_a(w, a, moves), pass_b(w, b, moves)
+
+    kv_cols = pl.ds(0, 256), pl.ds(256, 128)
+    qo_cols = pl.ds(384, 128), pl.ds(512, 256)
+    up_down = pl.ds(0, D), pl.ds(D, D)
+    halves = pl.ds(0, D // 2), pl.ds(D // 2, D // 2)
 
     first1.wait_recv()
     m.w1[z, x] = dot(squeeze, m.p01[...].reshape(64, D)).astype(BF)
-    phase1 = spread_start(m.w1, D // 2)
+    phase1 = spread_start(m.w1, *kv_cols)
+    phase1b = spread_start(m.w1, *qo_cols)
     first2 = fly([(m.pk2.at[u], m.p02.at[t], here(u)) for u in group], m.p02.at[0:3])
     ag_tok = gather_start(m.toka)
 
@@ -383,13 +409,14 @@
     firstv.wait_recv()
     m.vs1[...] = add4(m.vb[...], m.vg).astype(BF)
     vx = fly([(m.vs1, m.vx.at[k - 1], along_x(k)) for k in (1, 2, 3)], m.vx)
-    ends1 = spread_pass(m.w1, D // 2, phase1)
+    ends1 = spread_pass(m.w1, *kv_cols, phase1)
+    ends1b = spread_pass(m.w1, *qo_cols, phase1b)
     vx.wait_recv()
     m.vs2[...] = add4(m.vs1[...], m.vx).astype(BF)
     vz = fly([(m.vs2, m.vz.at[k - 1], along_z(k)) for k in (1, 2, 3)], m.vz)
     first2.wait_recv()
     m.w2[z, x] = dot(squeeze, m.p02[...].reshape(64, 2 * D)).astype(BF)
-    phase2 = spread_start(m.w2, D)
+    phase2 = spread_start(m.w2, *up_down)
     gather_pass(ag_tok, m.toka)
     ag_do = gather_start(m.doa)
     vz.wait_recv()
@@ -425,27 +452,19 @@
     m.nrmt[...] = m.nrm[...].T
 
     finish(ends1)
-    w1 = m.w1[...].reshape(D, D)
-    qkv = dot(m.nrm[...], w1)
-    m.q[...] = ((qkv[:, 0:HW] + q_bias) * 0.125).astype(BF)
     kv_bias = jnp.concatenate([jnp.zeros((1, HW), F32), v_bias], axis=1)
-    m.kvl[...] = (qkv[:, HW:3 * HW] + kv_bias).astype(BF)
+    m.kvl[...] = (dot(m.nrm[...], m.w1[:, :, :, 0:2 * HW].reshape(D, 2 * HW)) + kv_bias).astype(BF)
 
     m.ssrc[...] = dot(pick, m.kvl[...]).astype(BF)
-    sum_at = take(16)
-
-    def sum_copy(k):
-        return pltpu.make_async_remote_copy(
-            src_ref=m.ssrc,
-            dst_ref=m.kvs.at[pl.ds(pl.multiple_of(SLOT * s, SLOT), SLOT)],
-            send_sem=sum_ss.at[k], recv_sem=rs.at[sum_at + k],
-            device_id=dev((s + k) % 16, t, batch), device_id_type=MESH,
-        )
-
     for k in range(1, 16):
         @pl.when(s + k < 16)
         def _(k=k):
-            sum_copy(k).start()
+            far_copy(0, m.ssrc, slot_of(m.kvs, s), (s + k) % 16).start()
+    ends2b = pass_b(m.w2, up_down[1], phase2)
+    finish(ends1b)
+    m.q[...] = (
+        (dot(m.nrm[...], m.w1[:, :, :, 2 * HW:3 * HW].reshape(D, HW)) + q_bias) * 0.125
+    ).astype(BF)
     w_o = m.w1[...].reshape(D, D)[:, 3 * HW:]
     m.wosl[t] = jnp.concatenate([w_o[0:D // 2, :], w_o[D // 2:, :]], axis=1)
     m.kv[0] = m.kvl[:, 0:HW]
@@ -468,11 +487,9 @@
         m.o1[...] = part if h == 0 else m.o1[...] + part
     gather_pass(ag_do, m.doa)
 
-    for k in range(1, 16):
-        @pl.when(s >= k)
-        def _(k=k):
-            sum_copy(k).wait_recv()
-    ends2 = spread_pass(m.w2, D, phase2)
+    far_wait(0, s, True)
+    ends2a = pass_a(m.w2, up_down[0], phase2)
+    ends2 = (ends2a, ends2b)
     m.ks[...] = m.kvs[:, 0:HW]
     m.vs[...] = m.kvs[:, HW:]
 
@@ -482,10 +499,10 @@
         rows_c = slice(CHUNK * c, CHUNK * c + CHUNK)
         part = None
         for h in range(HEADS):
-            m.ssum[h, rows_c, :] = dot_nt(of_head(m.q[rows_c, :], h), m.ks[...]) + sum_bias
+            m.ssum[h] = dot_nt(of_head(m.q[rows_c, :], h), m.ks[...]) + sum_bias
 
             def soften2(rows, h=h):
-                score = m.ssum[h, rows, :]
+                score = m.ssum[h, within(rows, c), :]
                 peak = jnp.max(score, axis=-1, keepdims=True)
                 power = jnp.exp(score - peak)
                 m.prob2[h, rows, :] = power.astype(BF)
@@ -601,25 +618,34 @@
     m.g2[:, :, :, 0:D] = dot(m.nmt[...], m.gp[...]).astype(BF).reshape(4, 4, 48, D)
     m.g2[:, :, :, D:] = dot(m.dot_[...], m.act[...]).astype(BF).reshape(4, 4, 48, D)
 
-    def reduce_start(g, tag, half):
+    def reduce_start(g, tag, a, b, at_a, at_b):
         rza, rxb = getattr(m, "rza" + tag), getattr(m, "rxb" + tag)
-        a, b = pl.ds(0, half), pl.ds(half, half)
         return (
-            fly([(g.at[(z + k) % 4, :, :, a], rza.at[k - 1], along_z(k)) for k in (1, 3, 2)], rza),
-            fly([(g.at[:, (x + k) % 4, :, b], rxb.at[k - 1], along_x(k)) for k in (1, 3, 2)], rxb),
-        )
-
-    def reduce_pass(g, tag, half, moves):
+            fly([(g.at[(z + k) % 4, :, :, a], rza.at[k - 1, :, :, at_a], along_z(k))
+                 for k in (1, 3, 2)], rza.at[:, :, :, at_a]),
+            fly([(g.at[:, (x + k) % 4, :, b], rxb.at[k - 1, :, :, at_b], along_x(k))
+                 for k in (1, 3, 2)], rxb.at[:, :, :, at_b]),
+        )
+
+    def reduce_pass(g, tag, pieces):
         rza, rxb = getattr(m, "rza" + tag), getattr(m, "rxb" + tag)
         rxa, rzb = getattr(m, "rxa" + tag), getattr(m, "rzb" + tag)
         ha, hb = getattr(m, "ha" + tag), getattr(m, "hb" + tag)
-        moves[0].wait_recv()
-        for k in range(4):
-            ha[k] = add4(g[z, k, :, 0:half], [rza[j, k] for j in range(3)]).astype(BF)
+        for (a, b, at_a, at_b), moves in pieces:
+            into = slice(at_a.start, at_a.start + at_a.size)
+            moves[0].wait_recv()
+            for k in range(4):
+                ha[k, :, into] = add4(
+                    g[z, k, :, a.start:a.start + a.size], [rza[j, k, :, into] for j in range(3)]
+                ).astype(BF)
         a2 = fly([(ha.at[(x + k) % 4], rxa.at[k - 1], along_x(k)) for k in (1, 3, 2)], rxa)
-        moves[1].wait_recv()
-        for k in range(4):
-            hb[k] = add4(g[k, x, :, half:], [rxb[j, k] for j in range(3)]).astype(BF)
+        for (a, b, at_a, at_b), moves in pieces:
+            into = slice(at_b.start, at_b.start + at_b.size)
+            moves[1].wait_recv()
+            for k in range(4):
+                hb[k, :, into] = add4(
+                    g[k, x, :, b.start:b.start + b.size], [rxb[j, k, :, into] for j in range(3)]
+                ).astype(BF)
         b2 = fly([(hb.at[(z + k) % 4], rzb.at[k - 1], along_z(k)) for k in (1, 3, 2)], rzb)
         return a2, b2
 
@@ -644,7 +670,8 @@
         fin[mine] = fx[t]
         return moves
 
-    rg2 = reduce_start(m.g2, "2", D)
+    cols2 = up_down + (pl.ds(0, D), pl.ds(0, D))
+    rg2 = reduce_start(m.g2, "2", *cols2)
 
     zero_row = jnp.zeros((1, D), F32)
     ones = jnp.ones((8, SEG), BF)
@@ -686,14 +713,14 @@
         m.sb[0, u] = cols[0:HALF, :]
         m.sb[1, u] = cols[HALF:, :]
     qt = m.q[...].T
-    m.dq[...] = jnp.zeros((SEG, HW), F32)
+    m.o1[...] = jnp.zeros((SEG, HW), F32)
 
     finish(aa)
     do_all = m.do[...].reshape(SEG, HW)
     do_wide = do_all.astype(F32)
     weighed = do_wide * m.att[...]
     for h in range(HEADS):
-        m.delta[:, h:h + 1] = jnp.sum(of_head(weighed, h), axis=-1, keepdims=True)
+        m.m1[:, h:h + 1] = jnp.sum(of_head(weighed, h), axis=-1, keepdims=True)
     dot1 = (do_wide * m.a1x[...]).astype(BF).T
     dot2 = (do_wide * m.a2x[...]).astype(BF).T
     ab = fly(
@@ -703,79 +730,70 @@
     m.gba[0, t] = m.sb[0, t]
     m.gba[1, t] = m.sb[1, t]
     ro = scatter_start("ro", (0, 1))
+    for c in range(2):
+        rows_c = slice(CHUNK * c, CHUNK * c + CHUNK)
+        for h in range(HEADS):
+            m.ssum[h] = dot_nt(of_head(do_all[rows_c, :], h), m.vs[...])
+
+            def back_sum(rows, h=h, c=c):
+                weight = m.prob2[h, rows, :].astype(F32)
+                slope = (m.ssum[h, within(rows, c), :] - m.m1[rows, h:h + 1]) * m.a2[rows, h:h + 1]
+                m.ds[h, rows, :] = (weight * slope).astype(BF)
+
+            loop(CHUNK * c, 2, ROWS, back_sum)
     for h in range(HEADS):
-        m.ssum[h] = dot_nt(of_head(do_all, h), m.vs[...])
-
-        def back_sum(rows, h=h):
-            weight = m.prob2[h, rows, :].astype(F32)
-            slope = (m.ssum[h, rows, :] - m.delta[rows, h:h + 1]) * m.a2[rows, h:h + 1]
-            m.ds[h, rows, :] = (weight * slope).astype(BF)
-
-        loop(0, 4, ROWS, back_sum)
         feat, feat_v = slice(64 * h, 64 * h + 64), slice(HW + 64 * h, HW + 64 * h + 64)
-        m.dkvst[feat, :] = dot(qt[feat, :], m.ds[h])
-        m.dkvst[feat_v, :] = dot(dot2[feat, :], m.prob2[h])
-    m.dkvs[...] = m.dkvst[...].T.astype(BF)
-    for k in range(1, 16):
-        @pl.when(s + k < 16)
-        def _(k=k):
-            sum_copy(k).wait_send()
-    grad_at = take(16)
-
-    def grad_copy(k):
-        slot = (s + 16 - k) % 16
-        return pltpu.make_async_remote_copy(
-            src_ref=m.dkvs.at[pl.ds(pl.multiple_of(SLOT * slot, SLOT), SLOT)],
-            dst_ref=m.sumg.at[k],
-            send_sem=sum_ss.at[k], recv_sem=rs.at[grad_at + k],
-            device_id=dev(slot, t, batch), device_id_type=MESH,
-        )
-
+        m.big[feat, 0:SUMS] = dot(qt[feat, :], m.ds[h])
+        m.big[feat_v, 0:SUMS] = dot(dot2[feat, :], m.prob2[h])
+    m.dkvs[...] = m.big[0:2 * HW, 0:SUMS].T.astype(BF)
     for k in range(1, 16):
         @pl.when(s >= k)
         def _(k=k):
-            grad_copy(k).start()
+            seg = (s + 16 - k) % 16
+            far_copy(1, slot_of(m.dkvs, seg), m.sumg.at[k], seg).start()
+    ends_g2 = reduce_pass(m.g2, "2", [(cols2, rg2)])
     scatter_pass("ro", (0, 1), ro)
 
     for h in range(HEADS):
-        m.dq[...] += dot(m.ds[h], of_head(m.ks[...], h))
+        m.o1[...] += dot(m.ds[h], of_head(m.ks[...], h))
     for h in range(HEADS):
         m.big[:, SEG * h:SEG * h + SEG] = dot_nt(of_head(do_all, h), m.kv[1])
     for h in range(HEADS):
         def back_own(rows, h=h):
             weight = m.prob1[h, rows, :].astype(F32)
-            slope = (m.big[rows, SEG * h:SEG * h + SEG] - m.delta[rows, h:h + 1]) * m.a1[rows, h:h + 1]
+            slope = (m.big[rows, SEG * h:SEG * h + SEG] - m.m1[rows, h:h + 1]) * m.a1[rows, h:h + 1]
             m.ds[h, rows, 0:SEG] = (weight * slope).astype(BF)
 
         loop(0, 4, ROWS, back_own)
         score_grads = m.ds[h, :, 0:SEG]
-        m.dq[...] += dot(score_grads, of_head(m.kv[0], h))
+        m.o1[...] += dot(score_grads, of_head(m.kv[0], h))
         feat, feat_v = slice(64 * h, 64 * h + 64), slice(HW + 64 * h, HW + 64 * h + 64)
-        m.dkvt[feat, :] = dot(qt[feat, :], score_grads)
-        m.dkvt[feat_v, :] = dot(dot1[feat, :], m.prob1[h])
+        m.bias[feat, :] = dot(qt[feat, :], score_grads)
+        m.bias[feat_v, :] = dot(dot1[feat, :], m.prob1[h])
     for u in range(4):
-        m.attt[HW * u:HW * u + HW, :] = m.atta[u].T
+        m.nmt[HW * u:HW * u + HW, :] = m.atta[u].T
     ab.wait_recv()
-    g_o = dot(m.attt[...], m.gba[...].reshape(SEG, HW))
-    ends_g2 = reduce_pass(m.g2, "2", D, rg2)
-
-    for k in range(1, 16):
-        @pl.when(s + k < 16)
-        def _(k=k):
-            grad_copy(k).wait_recv()
+    g_o = dot(m.nmt[...], m.gba[...].reshape(SEG, HW))
+    dq = m.o1[...].astype(BF) * jnp.asarray(0.125, BF)
+    m.g1[:, :, :, 2 * HW:] = (
+        jnp.concatenate([dot(m.nrmt[...], dq), g_o], axis=1).astype(BF).reshape(4, 4, 48, 2 * HW)
+    )
+    cols_qo = qo_cols + (pl.ds(256, 128), pl.ds(128, 256))
+    cols_kv = kv_cols + (pl.ds(0, 256), pl.ds(0, 128))
+    rg1_qo = reduce_start(m.g1, "1", *cols_qo)
+
+    far_wait(1, 15 - s, True)
 
     total = m.sumg[0].astype(F32)
     for k in range(1, SLOTS):
         total = total + m.sumg[k].astype(F32)
     high = total.astype(BF)
     rest = (total - high.astype(F32)).astype(BF)
-    dkv = (m.dkvt[...] + dot_tn(high, pick) + dot_tn(rest, pick)).T.astype(BF)
-    dq = m.dq[...].astype(BF) * jnp.asarray(0.125, BF)
-    m.dqkv[...] = jnp.concatenate([dq, dkv], axis=1)
-
-    g_qkv = dot(m.nrmt[...], m.dqkv[...])
-    m.g1[...] = jnp.concatenate([g_qkv, g_o], axis=1).astype(BF).reshape(4, 4, 48, D)
-    rg1 = reduce_start(m.g1, "1", D // 2)
+    dkv = (m.bias[0:2 * HW, :] + dot_tn(high, pick) + dot_tn(rest, pick)).T.astype(BF)
+    m.dqkv[...] = jnp.concatenate([dkv, dq], axis=1)
+
+    m.g1[:, :, :, 0:2 * HW] = dot(m.nrmt[...], dkv).astype(BF).reshape(4, 4, 48, 2 * HW)
+    rg1_kv = reduce_start(m.g1, "1", *cols_kv)
     m.rn_s[...] = dot_nt(m.dqkv[...], m.w1[...].reshape(D, D)[:, 0:3 * HW]).astype(BF)
     rn = [scatter_start("rn", (c,)) for c in range(2)]
 
@@ -789,7 +807,7 @@
         )
 
     zero8 = jnp.zeros((8, D), F32)
-    g_gain1, g_shift1 = lax.fori_loop(0, 8, gain_grads, (zero8, zero8))
+    g_gain1, g_shift1 = lax.fori_loop(0, 8, gain_grads, (zero8, zero8), unroll=4)
     scatter_pass("rn", (0,), rn[0])
     scatter_pass("rn", (1,), rn[1])
     g_qkvb = col_sums(m.dqkv[...])
@@ -801,8 +819,8 @@
     rows8 = (
         jnp.sum(g_gain1, axis=0, keepdims=True),
         jnp.sum(g_shift1, axis=0, keepdims=True),
-        in_place(g_qkvb[:, 0:HW]),
         in_place(g_qkvb[:, 2 * HW:]),
+        in_place(g_qkvb[:, HW:2 * HW]),
         col_sums(m.gbr[...]),
         g_gain2,
         g_shift2,
@@ -820,7 +838,7 @@
         out_o[HALF * c:HALF * c + HALF, :] = (
             scatter_end("ro", c, ro) + m.hid[block(c, t), :] + down_bias
         ).astype(BF)
-    ends_g1 = reduce_pass(m.g1, "1", D // 2, rg1)
+    ends_g1 = reduce_pass(m.g1, "1", [(cols_qo, rg1_qo), (cols_kv, rg1_kv)])
     vgx.wait_recv()
     m.vgs[...] = add4(m.vgr[...], m.vgx)
     vgz = fly([(m.vgs, m.vgz.at[k - 1], along_z(k)) for k in (1, 2, 3)], m.vgz)
@@ -859,16 +877,18 @@
     row16 = iota((16, 128), 0)
     gvec_o[...] = jnp.where(row16 < 8, moved_by(totals, own_12), moved_by(totals, own_48))
     fin_g1.wait_recv()
-    parts = [both(m.fin1, u, slice(0, D)) for u in range(4)]
-    for k, ref in enumerate((gq_o, gk_o, gv_o, go_o)):
-        ref[...] = jnp.concatenate([p[:, HW * k:HW * k + HW] for p in parts], axis=1)
+    for u in range(4):
+        part = both(m.fin1, u, slice(0, D))
+        ordered = jnp.concatenate(
+            [part[:, 0:256], part[:, 384:512], part[:, 256:384], part[:, 512:]], axis=1
+        )
+        for k, ref in enumerate((gk_o, gv_o, gq_o, go_o)):
+            ref[:, HW * u:HW * u + HW] = ordered[:, HW * k:HW * k + HW]
 
     for flight in sent:
         flight.wait_send()
-    for k in range(1, 16):
-        @pl.when(s >= k)
-        def _(k=k):
-            grad_copy(k).wait_send()
+    far_wait(0, 15 - s, False)
+    far_wait(1, s, False)
     assert used[0] <= RECVS, used[0]
 
 
@@ -904,7 +924,7 @@
         in_specs=[pl.BlockSpec(memory_space=pltpu.SMEM)] + [vmem] * 17,
         out_specs=[vmem] * 9,
         scratch_shapes=[pltpu.VMEM(dims, kind) for dims, kind in SCRATCH.values()]
-        + [pltpu.SemaphoreType.DMA((n,)) for n in (SENDS, RECVS, SLOTS)],
+        + [pltpu.SemaphoreType.DMA((n,)) for n in (SENDS, RECVS, 2, 2)],
         compiler_params=pltpu.CompilerParams(
             collective_id=0, has_side_effects=True, vmem_limit_bytes=62 * 2**20
         ),

time: 113 us -> 109 us (0.965)
  Pallas kernels: 112 us -> 108 us
    pallas_call x1, Pallas kernels: 110 us -> 106 us  [body(): pl.pallas_call(layer_kernel, out_shape=shapes + [shape((16, 128), F32)],...]
where the time goes in v4:
time: 109 us
  Pallas kernels  108 us (99%)
    pallas_call x1, Pallas kernels, body(): pl.pallas_call(layer_kernel, out_shape=shapes + [shape((16, 128), F32)],...  106 us
    pallas_call x1, Pallas kernels, body(): pl.pallas_call(hand_out, out_shape=shapes + [shape((1, 12), F32)] * 8 + [...  2.35 us

profile of v4, /device:TPU:1, one launch (start us, length us, event | category | flops | bytes accessed | tf_op | source)
XLA Modules:
  0.0 109.2 jit_solution(13383984698919329514)
XLA Ops:
  0.7 106.0 %layer.1 = (bf16[128,768]{1,0:T(8,128)(2,1)}, f32[128,768]{1,0:T(8,128)}, f32[12,768]{1,0:T(8,128)}, f32[12,768]{1,0:T(8,128)}, f32[12,768]{1,0:T(8,128)}, /*ind...) custom-call(s32[1,16]{1,0:T(1,128)} %seg_ref.1, bf16[128,768]{1,0:T(8,128)(2,1)} %bitcast.22, ...), custom_call_target="tpu_custom_call" | custom-call | tf_op jit(solution)/shard_map/layer/pallas_call | solution.py:921
  106.7 2.4 %hand_out.1 = (bf16[128,768]{1,0:T(8,128)(2,1)}, f32[128,768]{1,0:T(8,128)}, f32[12,768]{1,0:T(8,128)}, f32[12,768]{1,0:T(8,128)}, f32[12,768]{1,0:T(8,128)}, /*...) custom-call(bf16[128,768]{1,0:T(8,128)(2,1)} %get-tuple-element.43.r, ...), custom_call_target="tpu_custom_call" | custom-call | tf_op jit(solution)/shard_map/hand_out/pallas_call | solution.py:936

commit v5 on v4

--- a/solution.py
+++ b/solution.py
@@ -132,9 +132,13 @@
     rzb1=((3, 48, D // 2), BF),
     ha1=((4, 48, D // 2), BF),
     hb1=((4, 48, D // 2), BF),
-    rza2=((3, 4, 48, D), BF),
+    r1a=((2, 2, 48, D), BF),
+    s2a=((2, 2, 48, D), BF),
+    r2a=((2, 4, 48, D), BF),
+    r1b=((2, 2, 48, D), BF),
+    s2b=((2, 2, 48, D), BF),
+    r2b=((2, 4, 48, D), BF),
     rxa2=((3, 48, D), BF),
-    rxb2=((3, 4, 48, D), BF),
     rzb2=((3, 48, D), BF),
     ha2=((4, 48, D), BF),
     hb2=((4, 48, D), BF),
@@ -151,7 +155,7 @@
     vfin=((8, 16, 256), F32),
 )
 SENDS = 24
-RECVS = 66
+RECVS = 72
 
 
 class Flight:
@@ -670,8 +674,62 @@
         fin[mine] = fx[t]
         return moves
 
-    cols2 = up_down + (pl.ds(0, D), pl.ds(0, D))
-    rg2 = reduce_start(m.g2, "2", *cols2)
+
+    up_c, down_c = up_down
+    lo, hi = pl.ds(0, 2), pl.ds(2, 2)
+    z1, z2, z3 = (z + 1) % 4, (z + 2) % 4, (z + 3) % 4
+    x1, x2, x3 = (x + 1) % 4, (x + 2) % 4, (x + 3) % 4
+    relay_a = fly(
+        [(m.g2.at[z2, lo, :, up_c], m.r1a.at[0], along_z(1)),
+         (m.g2.at[z2, hi, :, up_c], m.r1a.at[1], along_z(3))], m.r1a
+    )
+    relay_b = fly(
+        [(m.g2.at[lo, x2, :, down_c], m.r1b.at[0], along_x(1)),
+         (m.g2.at[hi, x2, :, down_c], m.r1b.at[1], along_x(3))], m.r1b
+    )
+    plain_a = fly(
+        [(m.g2.at[z1, hi, :, up_c], m.r2a.at[0, hi], along_z(1)),
+         (m.g2.at[z3, lo, :, up_c], m.r2a.at[1, lo], along_z(3))], m.r1a
+    )
+    plain_b = fly(
+        [(m.g2.at[hi, x1, :, down_c], m.r2b.at[0, hi], along_x(1)),
+         (m.g2.at[lo, x3, :, down_c], m.r2b.at[1, lo], along_x(3))], m.r1b
+    )
+
+    def relay():
+        relay_a.wait_recv()
+        m.s2a[0] = (m.g2[z1, 0:2, :, 0:D].astype(F32) + m.r1a[0].astype(F32)).astype(BF)
+        m.s2a[1] = (m.g2[z3, 2:4, :, 0:D].astype(F32) + m.r1a[1].astype(F32)).astype(BF)
+        a = fly(
+            [(m.s2a.at[0], m.r2a.at[0, lo], along_z(1)),
+             (m.s2a.at[1], m.r2a.at[1, hi], along_z(3))], m.r1a
+        )
+        relay_b.wait_recv()
+        m.s2b[0] = (m.g2[0:2, x1, :, D:].astype(F32) + m.r1b[0].astype(F32)).astype(BF)
+        m.s2b[1] = (m.g2[2:4, x3, :, D:].astype(F32) + m.r1b[1].astype(F32)).astype(BF)
+        b = fly(
+            [(m.s2b.at[0], m.r2b.at[0, lo], along_x(1)),
+             (m.s2b.at[1], m.r2b.at[1, hi], along_x(3))], m.r1b
+        )
+        return a, b
+
+    def relayed(moves):
+        plain_a.wait_recv()
+        moves[0].wait_recv()
+        for k in range(4):
+            m.ha2[k] = (
+                m.g2[z, k, :, 0:D].astype(F32) + m.r2a[0, k].astype(F32) + m.r2a[1, k].astype(F32)
+            ).astype(BF)
+        a2 = fly([(m.ha2.at[(x + k) % 4], m.rxa2.at[k - 1], along_x(k)) for k in (1, 3, 2)], m.rxa2)
+        plain_b.wait_recv()
+        moves[1].wait_recv()
+        for k in range(4):
+            m.hb2[k] = (
+                m.g2[k, x, :, D:].astype(F32) + m.r2b[0, k].astype(F32) + m.r2b[1, k].astype(F32)
+            ).astype(BF)
+        b2 = fly([(m.hb2.at[(z + k) % 4], m.rzb2.at[k - 1], along_z(k)) for k in (1, 3, 2)], m.rzb2)
+        return a2, b2
+
 
     zero_row = jnp.zeros((1, D), F32)
     ones = jnp.ones((8, SEG), BF)
@@ -715,14 +773,6 @@
     qt = m.q[...].T
     m.o1[...] = jnp.zeros((SEG, HW), F32)
 
-    finish(aa)
-    do_all = m.do[...].reshape(SEG, HW)
-    do_wide = do_all.astype(F32)
-    weighed = do_wide * m.att[...]
-    for h in range(HEADS):
-        m.m1[:, h:h + 1] = jnp.sum(of_head(weighed, h), axis=-1, keepdims=True)
-    dot1 = (do_wide * m.a1x[...]).astype(BF).T
-    dot2 = (do_wide * m.a2x[...]).astype(BF).T
     ab = fly(
         [(m.sb.at[c, u], m.gba.at[c, t], here(u)) for u in group for c in (0, 1)],
         m.gba.at[:, 0:3],
@@ -732,15 +782,25 @@
     ro = scatter_start("ro", (0, 1))
     for c in range(2):
         rows_c = slice(CHUNK * c, CHUNK * c + CHUNK)
+        aa[c].wait_recv()
+        do_c = m.do[c].reshape(CHUNK, HW)
+        weighed = do_c.astype(F32) * m.att[rows_c, :]
         for h in range(HEADS):
-            m.ssum[h] = dot_nt(of_head(do_all[rows_c, :], h), m.vs[...])
+            m.m1[rows_c, h:h + 1] = jnp.sum(of_head(weighed, h), axis=-1, keepdims=True)
+        for h in range(HEADS):
+            m.ssum[h] = dot_nt(of_head(do_c, h), m.vs[...])
 
             def back_sum(rows, h=h, c=c):
-                weight = m.prob2[h, rows, :].astype(F32)
                 slope = (m.ssum[h, within(rows, c), :] - m.m1[rows, h:h + 1]) * m.a2[rows, h:h + 1]
-                m.ds[h, rows, :] = (weight * slope).astype(BF)
+                m.ds[h, rows, :] = (m.prob2[h, rows, :].astype(F32) * slope).astype(BF)
 
             loop(CHUNK * c, 2, ROWS, back_sum)
+        if c == 0:
+            rg2 = relay()
+    do_all = m.do[...].reshape(SEG, HW)
+    do_wide = do_all.astype(F32)
+    dot1 = (do_wide * m.a1x[...]).astype(BF).T
+    dot2 = (do_wide * m.a2x[...]).astype(BF).T
     for h in range(HEADS):
         feat, feat_v = slice(64 * h, 64 * h + 64), slice(HW + 64 * h, HW + 64 * h + 64)
         m.big[feat, 0:SUMS] = dot(qt[feat, :], m.ds[h])
@@ -751,7 +811,7 @@
         def _(k=k):
             seg = (s + 16 - k) % 16
             far_copy(1, slot_of(m.dkvs, seg), m.sumg.at[k], seg).start()
-    ends_g2 = reduce_pass(m.g2, "2", [(cols2, rg2)])
+    ends_g2 = relayed(rg2)
     scatter_pass("ro", (0, 1), ro)
 
     for h in range(HEADS):
@@ -782,6 +842,9 @@
     cols_kv = kv_cols + (pl.ds(0, 256), pl.ds(0, 128))
     rg1_qo = reduce_start(m.g1, "1", *cols_qo)
 
+    m.big[:, 0:2 * HW] = m.bias[0:2 * HW, :].T
+    pick_t = pick.T
+
     far_wait(1, 15 - s, True)
 
     total = m.sumg[0].astype(F32)
@@ -789,7 +852,7 @@
         total = total + m.sumg[k].astype(F32)
     high = total.astype(BF)
     rest = (total - high.astype(F32)).astype(BF)
-    dkv = (m.bias[0:2 * HW, :] + dot_tn(high, pick) + dot_tn(rest, pick)).T.astype(BF)
+    dkv = (m.big[:, 0:2 * HW] + dot(pick_t, high) + dot(pick_t, rest)).astype(BF)
     m.dqkv[...] = jnp.concatenate([dkv, dq], axis=1)
 
     m.g1[:, :, :, 0:2 * HW] = dot(m.nrmt[...], dkv).astype(BF).reshape(4, 4, 48, 2 * HW)

time: 109 us -> 107 us (0.982)
  Pallas kernels: 108 us -> 106 us
    pallas_call x1, Pallas kernels: 106 us -> 104 us  [body(): pl.pallas_call(layer_kernel, out_shape=shapes + [shape((16, 128), F32)],...]
where the time goes in v5:
time: 107 us
  Pallas kernels  106 us (99%)
    pallas_call x1, Pallas kernels, body(): pl.pallas_call(layer_kernel, out_shape=shapes + [shape((16, 128), F32)],...  104 us
    pallas_call x1, Pallas kernels, body(): pl.pallas_call(hand_out, out_shape=shapes + [shape((1, 12), F32)] * 8 + [...  2.35 us

profile of v5, /device:TPU:1, one launch (start us, length us, event | category | flops | bytes accessed | tf_op | source)
XLA Modules:
  0.0 106.8 jit_solution(15062597016322199963)
XLA Ops:
  0.7 103.6 %layer.1 = (bf16[128,768]{1,0:T(8,128)(2,1)}, f32[128,768]{1,0:T(8,128)}, f32[12,768]{1,0:T(8,128)}, f32[12,768]{1,0:T(8,128)}, f32[12,768]{1,0:T(8,128)}, /*ind...) custom-call(s32[1,16]{1,0:T(1,128)} %seg_ref.1, bf16[128,768]{1,0:T(8,128)(2,1)} %bitcast.22, ...), custom_call_target="tpu_custom_call" | custom-call | tf_op jit(solution)/shard_map/layer/pallas_call | solution.py:984
  104.3 2.4 %hand_out.1 = (bf16[128,768]{1,0:T(8,128)(2,1)}, f32[128,768]{1,0:T(8,128)}, f32[12,768]{1,0:T(8,128)}, f32[12,768]{1,0:T(8,128)}, f32[12,768]{1,0:T(8,128)}, /*...) custom-call(bf16[128,768]{1,0:T(8,128)(2,1)} %get-tuple-element.43.r, ...), custom_call_target="tpu_custom_call" | custom-call | tf_op jit(solution)/shard_map/hand_out/pallas_call | solution.py:999

commit v6 on v5

--- a/solution.py
+++ b/solution.py
@@ -811,7 +811,6 @@
         def _(k=k):
             seg = (s + 16 - k) % 16
             far_copy(1, slot_of(m.dkvs, seg), m.sumg.at[k], seg).start()
-    ends_g2 = relayed(rg2)
     scatter_pass("ro", (0, 1), ro)
 
     for h in range(HEADS):
@@ -832,6 +831,7 @@
         m.bias[feat_v, :] = dot(dot1[feat, :], m.prob1[h])
     for u in range(4):
         m.nmt[HW * u:HW * u + HW, :] = m.atta[u].T
+    ends_g2 = relayed(rg2)
     ab.wait_recv()
     g_o = dot(m.nmt[...], m.gba[...].reshape(SEG, HW))
     dq = m.o1[...].astype(BF) * jnp.asarray(0.125, BF)

time: 107 us -> 106 us (level)
  no operation moved by 1% of the time
where the time goes in v6:
time: 106 us
  Pallas kernels  105 us (99%)
    pallas_call x1, Pallas kernels, body(): pl.pallas_call(layer_kernel, out_shape=shapes + [shape((16, 128), F32)],...  103 us
    pallas_call x1, Pallas kernels, body(): pl.pallas_call(hand_out, out_shape=shapes + [shape((1, 12), F32)] * 8 + [...  2.35 us

profile of v6, /device:TPU:1, one launch (start us, length us, event | category | flops | bytes accessed | tf_op | source)
XLA Modules:
  0.0 106.1 jit_solution(9832778611435170180)
XLA Ops:
  0.7 102.9 %layer.1 = (bf16[128,768]{1,0:T(8,128)(2,1)}, f32[128,768]{1,0:T(8,128)}, f32[12,768]{1,0:T(8,128)}, f32[12,768]{1,0:T(8,128)}, f32[12,768]{1,0:T(8,128)}, /*ind...) custom-call(s32[1,16]{1,0:T(1,128)} %seg_ref.1, bf16[128,768]{1,0:T(8,128)(2,1)} %bitcast.22, ...), custom_call_target="tpu_custom_call" | custom-call | tf_op jit(solution)/shard_map/layer/pallas_call | solution.py:984
  103.6 2.4 %hand_out.1 = (bf16[128,768]{1,0:T(8,128)(2,1)}, f32[128,768]{1,0:T(8,128)}, f32[12,768]{1,0:T(8,128)}, f32[12,768]{1,0:T(8,128)}, f32[12,768]{1,0:T(8,128)}, /*...) custom-call(bf16[128,768]{1,0:T(8,128)(2,1)} %get-tuple-element.43.r, ...), custom_call_target="tpu_custom_call" | custom-call | tf_op jit(solution)/shard_map/hand_out/pallas_call | solution.py:999
